TPU v7x, 32 devices: a whole 2x2x4 slice. The times are simulated.
32 devices in a mesh: ctx: 16 (over z, y, core), fsdp: 2 (over x).
Axes of the slice: x: 2, y: 2, z: 4, core: 2. Of those that a mesh axis runs over, the one named last changes fastest.
Arguments:
- tokens: bfloat16 [2, 4096, 1280], P('fsdp', 'ctx'), may hold values from -6 to 6
- cotangent: bfloat16 [2, 4096, 1280], P('fsdp', 'ctx'), may hold values from -6 to 6
- lengths: int32 [2, 8], P('fsdp'), may hold values from 1 to 2048, as said below
- deal: int32 [32], replicated, may hold values from 0 to 31, as said below
- gain_attn: float32 [1280], P('fsdp'), may hold values from 0.5 to 1.5
- query_weight: float32 [1280, 1280], P('fsdp'), may hold values from -0.25 to 0.25
- query_bias: float32 [1280], P('fsdp'), may hold values from -3 to 3
- key_weight: float32 [1280, 1280], P('fsdp'), may hold values from -0.15625 to 0.15625
- value_weight: float32 [1280, 1280], P('fsdp'), may hold values from -0.15625 to 0.15625
- value_bias: float32 [1280], P('fsdp'), may hold values from -3 to 3
- query_scale: float32 [80], P('fsdp'), may hold values from -0.5 to 1.5
- proj_weight: float32 [1280, 1280], P('fsdp'), may hold values from -0.625 to 0.625
- gain_ffn: float32 [1280], P('fsdp'), may hold values from 0.5 to 1.5
- up_weight: float32 [1280, 1280], P('fsdp'), may hold values from -0.15625 to 0.15625
- down_weight: float32 [1280, 1280], P('fsdp'), may hold values from -0.15625 to 0.15625
Outputs:
- layer_out: bfloat16 [2, 4096, 1280], P('fsdp', 'ctx')
- grad_tokens: float32 [2, 4096, 1280], P('fsdp', 'ctx')
- grad_gain_attn: float32 [1280], P('fsdp')
- grad_query_weight: float32 [1280, 1280], P('fsdp')
- grad_query_bias: float32 [1280], P('fsdp')
- grad_key_weight: float32 [1280, 1280], P('fsdp')
- grad_value_weight: float32 [1280, 1280], P('fsdp')
- grad_value_bias: float32 [1280], P('fsdp')
- grad_query_scale: float32 [80], P('fsdp')
- grad_proj_weight: float32 [1280, 1280], P('fsdp')
- grad_gain_ffn: float32 [1280], P('fsdp')
- grad_up_weight: float32 [1280, 1280], P('fsdp')
- grad_down_weight: float32 [1280, 1280], P('fsdp')
Inputs may be any that keep to these rules, and one draw needn't show every extreme that they name: `lengths`: each row sums to 4096; its first or its last entry is 2048. `deal`: a permutation; the entries at positions 2 i and 2 i + 1 are j and 31 - j for some j below 16.
All inputs are finite; a program needn't handle non-finite values.
Results may differ from a plain program's by a relative error of at most 0.022.
Values may be sent and summed in bfloat16 or wider, within the bound.
A program may use at most 192 MiB of HBM per device.

v0:
```python
import math

import jax
import jax.numpy as jnp
from jax import lax
from jax.sharding import PartitionSpec as P

H = 16
HD = 80
BLK = 128


EPS = 1e-06
LOG2E = 1.442695041
NEG = -1e30


def from_behind(value, axis, steps):
    count = lax.axis_size(axis)
    pairs = [(source, (source + steps) % count) for source in range(count)]
    return lax.ppermute(value, axis, pairs)


def rms_scale(values):
    return lax.rsqrt(jnp.mean(values * values, axis=-1, keepdims=True) + EPS)


def softplus(values):
    return jnp.log(1.0 + jnp.exp(values))


def locate(deal, seq_ends, first_row, row_total):
    row_ids = first_row + jnp.arange(row_total, dtype=jnp.int32)
    block_of = row_ids // BLK
    blocks = jnp.arange(deal.shape[0], dtype=jnp.int32)
    natural = jnp.sum(jnp.where(block_of[:, None] == blocks[None, :], deal[None, :], 0), axis=1)
    position = natural * BLK + row_ids % BLK
    segment = jnp.sum((position[:, None] >= seq_ends[None, :]).astype(jnp.int32), axis=1)
    return (position, segment)


def allowed(query_pos, query_seg, key_pos, key_seg):
    return (query_seg[:, None] == key_seg[None, :]) & (key_pos[None, :] <= query_pos[:, None])


def attend(running, queries, query_pos, query_seg, key_blk, value_blk, key_pos, key_seg):
    run_max, run_sum, accum = running
    key_count = key_blk.shape[0]
    key_heads = key_blk.reshape(key_count, H, HD)
    value_heads = value_blk.reshape(key_count, H, HD)
    scores = jnp.einsum("qhd,khd->hqk", queries, key_heads, preferred_element_type=jnp.float32)
    visible = allowed(query_pos, query_seg, key_pos, key_seg)[None]
    scores = jnp.where(visible, scores, NEG)
    new_max = jnp.maximum(run_max, jnp.max(scores, axis=-1))
    shrink = jnp.exp(run_max - new_max)
    attn_probs = jnp.where(visible, jnp.exp(scores - new_max[:, :, None]), 0.0)
    run_sum = run_sum * shrink + jnp.sum(attn_probs, axis=-1)
    accum = accum * shrink.T[:, :, None] + jnp.einsum(
        "hqk,khd->qhd",
        attn_probs.astype(jnp.bfloat16),
        value_heads,
        preferred_element_type=jnp.float32,
    )
    return (new_max, run_sum, accum)


def attend_back(
    queries,
    out_grad,
    query_pos,
    query_seg,
    log_sum,
    row_delta,
    key_blk,
    value_blk,
    key_pos,
    key_seg,
):
    key_count = key_blk.shape[0]
    key_heads = key_blk.reshape(key_count, H, HD)
    value_heads = value_blk.reshape(key_count, H, HD)
    scores = jnp.einsum("qhd,khd->hqk", queries, key_heads, preferred_element_type=jnp.float32)
    visible = allowed(query_pos, query_seg, key_pos, key_seg)[None]
    attn_probs = jnp.where(visible, jnp.exp(scores - log_sum[:, :, None]), 0.0)
    value_part = jnp.einsum(
        "hqk,qhd->khd",
        attn_probs.astype(jnp.bfloat16),
        out_grad,
        preferred_element_type=jnp.float32,
    ).reshape(key_count, H * HD)
    prob_grad = jnp.einsum(
        "qhd,khd->hqk", out_grad, value_heads, preferred_element_type=jnp.float32
    )
    score_grad = (attn_probs * (prob_grad - row_delta[:, :, None])).astype(jnp.bfloat16)
    query_part = jnp.einsum(
        "hqk,khd->qhd", score_grad, key_heads, preferred_element_type=jnp.float32
    )
    key_part = jnp.einsum(
        "hqk,qhd->khd", score_grad, queries, preferred_element_type=jnp.float32
    ).reshape(key_count, H * HD)
    return (query_part, key_part, value_part)


def unpack(full_mats, full_vecs, full_scale):
    return (
        full_mats[0],
        full_mats[1],
        full_mats[2],
        full_mats[3],
        full_mats[4],
        full_mats[5],
        full_vecs[0].astype(jnp.float32),
        full_vecs[1].astype(jnp.float32),
        full_vecs[2].astype(jnp.float32),
        full_vecs[3].astype(jnp.float32),
        full_scale.astype(jnp.float32),
    )


def local(
    tokens,
    cotangent,
    lengths,
    deal,
    gain_attn,
    query_weight,
    query_bias,
    key_weight,
    value_weight,
    value_bias,
    query_scale,
    proj_weight,
    gain_ffn,
    up_weight,
    down_weight,
):
    row_count = tokens.shape[1]
    my_index = lax.axis_index("ctx")
    cycle_size = lax.axis_size("ctx")
    seq_ends = jnp.cumsum(lengths[0])
    query_pos, query_seg = locate(deal, seq_ends, my_index * row_count, row_count)
    matrices = jnp.stack(
        [query_weight, key_weight, value_weight, proj_weight, up_weight, down_weight]
    ).astype(jnp.bfloat16)
    vectors = jnp.stack([gain_attn, query_bias, value_bias, gain_ffn]).astype(jnp.bfloat16)
    scale_part = query_scale.astype(jnp.bfloat16)
    full_mats, full_vecs, full_scale = (
        lax.all_gather(matrices, "fsdp", axis=1, tiled=True),
        lax.all_gather(vectors, "fsdp", axis=1, tiled=True),
        lax.all_gather(scale_part, "fsdp", axis=0, tiled=True),
    )
    w_query, w_key, w_value, w_proj, w_up, w_down, gain_a, b_query, b_value, gain_f, q_param = (
        unpack(full_mats, full_vecs, full_scale)
    )
    inputs = tokens[0].astype(jnp.float32)
    inv_attn = rms_scale(inputs)
    unit_a = inputs * inv_attn
    normed = (unit_a * gain_a).astype(jnp.bfloat16)
    factor_head = softplus(q_param) * (LOG2E / math.sqrt(HD))
    factor = jnp.tile(factor_head, H)
    raw_query = jnp.dot(normed, w_query, preferred_element_type=jnp.float32) + b_query
    queries = (raw_query * factor).astype(jnp.bfloat16)
    key_rows = jnp.dot(normed, w_key, preferred_element_type=jnp.float32).astype(jnp.bfloat16)
    value_rows = (jnp.dot(normed, w_value, preferred_element_type=jnp.float32) + b_value).astype(
        jnp.bfloat16
    )
    query_heads = queries.reshape(row_count, H, HD)
    start_state = (
        jnp.full((H, row_count), NEG, jnp.float32),
        jnp.zeros((H, row_count), jnp.float32),
        jnp.zeros((row_count, H, HD), jnp.float32),
    )

    def visit(running, key_blk, value_blk, source):
        key_pos, key_seg = locate(deal, seq_ends, source * row_count, row_count)
        return attend(
            running, query_heads, query_pos, query_seg, key_blk, value_blk, key_pos, key_seg
        )

    own_state = visit(start_state, key_rows, value_rows, my_index)

    def pass_step(offset, packed):
        kv_blk, running = packed
        kv_blk = from_behind(kv_blk, "ctx", 1)
        source = (my_index - offset) % cycle_size
        return (kv_blk, visit(running, kv_blk[0], kv_blk[1], source))

    kv_final, softmax_state = lax.fori_loop(
        1, cycle_size, pass_step, (jnp.stack([key_rows, value_rows]), own_state)
    )
    run_max, run_sum, accum = softmax_state
    attn_f32 = accum / run_sum.T[:, :, None]
    log_sum = run_max + jnp.log(run_sum)
    mixed = attn_f32.reshape(row_count, H * HD).astype(jnp.bfloat16)
    hidden = inputs + jnp.dot(mixed, w_proj, preferred_element_type=jnp.float32)
    inv_ff = rms_scale(hidden)
    unit_ff = hidden * inv_ff
    normed_ff = (unit_ff * gain_f).astype(jnp.bfloat16)
    up_proj = jnp.dot(normed_ff, w_up, preferred_element_type=jnp.float32)
    gate_sig = jax.nn.sigmoid(up_proj)
    activated = (up_proj * gate_sig).astype(jnp.bfloat16)
    result = hidden + jnp.dot(activated, w_down, preferred_element_type=jnp.float32)
    layer_out = result.astype(jnp.bfloat16)[None]
    out_cot = cotangent[0]
    grad_down = jnp.einsum("tf,td->fd", activated, out_cot, preferred_element_type=jnp.float32)
    grad_act = jnp.einsum("td,fd->tf", out_cot, w_down, preferred_element_type=jnp.float32)
    up_grad = (grad_act * gate_sig * (1.0 + up_proj * (1.0 - gate_sig))).astype(jnp.bfloat16)
    grad_up = jnp.einsum("td,tf->df", normed_ff, up_grad, preferred_element_type=jnp.float32)
    normed_grad = jnp.einsum("tf,df->td", up_grad, w_up, preferred_element_type=jnp.float32)
    grad_gain_f = jnp.sum(normed_grad * unit_ff, axis=0)
    scaled_ff = normed_grad * gain_f
    hidden_grad = out_cot.astype(jnp.float32) + inv_ff * (
        scaled_ff - unit_ff * jnp.mean(scaled_ff * unit_ff, axis=-1, keepdims=True)
    )
    branch_grad = hidden_grad.astype(jnp.bfloat16)
    grad_proj = jnp.einsum("tc,td->cd", mixed, branch_grad, preferred_element_type=jnp.float32)
    out_grad = jnp.einsum(
        "td,cd->tc", branch_grad, w_proj, preferred_element_type=jnp.float32
    ).astype(jnp.bfloat16)
    out_heads = out_grad.reshape(row_count, H, HD)
    row_delta = jnp.einsum("qhd,qhd->hq", out_heads.astype(jnp.float32), attn_f32)

    def back_visit(key_blk, value_blk, source):
        key_pos, key_seg = locate(deal, seq_ends, source * row_count, row_count)
        return attend_back(
            query_heads,
            out_heads,
            query_pos,
            query_seg,
            log_sum,
            row_delta,
            key_blk,
            value_blk,
            key_pos,
            key_seg,
        )

    def back_step(offset, packed):
        kv_blk, kv_grad, query_acc = packed
        source = (my_index - offset) % cycle_size
        query_part, key_part, value_part = back_visit(kv_blk[0], kv_blk[1], source)
        kv_grad = kv_grad + jnp.stack([key_part, value_part])
        kv_blk = from_behind(kv_blk, "ctx", 1)
        kv_grad = from_behind(kv_grad.astype(jnp.bfloat16), "ctx", 1).astype(kv_grad.dtype)
        return (kv_blk, kv_grad, query_acc + query_part)

    back_init = (
        jnp.stack([key_rows, value_rows]),
        jnp.zeros((2, row_count, H * HD), jnp.float32),
        jnp.zeros((row_count, H, HD), jnp.float32),
    )
    kv_home, kv_grad_home, query_acc = lax.fori_loop(0, cycle_size, back_step, back_init)
    key_grad = kv_grad_home[0]
    value_grad = kv_grad_home[1]
    key_grad_b = key_grad.astype(jnp.bfloat16)
    value_grad_b = value_grad.astype(jnp.bfloat16)
    scaled_qgrad = query_acc.reshape(row_count, H * HD)
    grad_factor = jnp.sum((scaled_qgrad * raw_query).reshape(row_count, H, HD), axis=(0, 1))
    grad_scale = grad_factor * jax.nn.sigmoid(q_param) * (LOG2E / math.sqrt(HD))
    query_grad_b = (scaled_qgrad * factor).astype(jnp.bfloat16)
    grad_query = jnp.einsum("tc,td->cd", normed, query_grad_b, preferred_element_type=jnp.float32)
    grad_key = jnp.einsum("tc,td->cd", normed, key_grad_b, preferred_element_type=jnp.float32)
    grad_value = jnp.einsum("tc,td->cd", normed, value_grad_b, preferred_element_type=jnp.float32)
    grad_bq = jnp.sum(query_grad_b.astype(jnp.float32), axis=0)
    grad_bv = jnp.sum(value_grad_b.astype(jnp.float32), axis=0)
    normed_grad_a = (
        jnp.einsum("td,cd->tc", query_grad_b, w_query, preferred_element_type=jnp.float32)
        + jnp.einsum("td,cd->tc", key_grad_b, w_key, preferred_element_type=jnp.float32)
        + jnp.einsum("td,cd->tc", value_grad_b, w_value, preferred_element_type=jnp.float32)
    )
    grad_gain_a = jnp.sum(normed_grad_a * unit_a, axis=0)
    scaled_a = normed_grad_a * gain_a
    grad_inputs = hidden_grad + inv_attn * (
        scaled_a - unit_a * jnp.mean(scaled_a * unit_a, axis=-1, keepdims=True)
    )
    grad_mats = jnp.stack([grad_query, grad_key, grad_value, grad_proj, grad_up, grad_down])
    grad_vecs = jnp.stack([grad_gain_a, grad_bq, grad_bv, grad_gain_f])
    owned_mats, owned_vecs, owned_scale = (
        lax.psum_scatter(
            grad_mats.astype(jnp.bfloat16), "fsdp", scatter_dimension=1, tiled=True
        ).astype(jnp.float32),
        lax.psum_scatter(
            grad_vecs.astype(jnp.bfloat16), "fsdp", scatter_dimension=1, tiled=True
        ).astype(jnp.float32),
        lax.psum_scatter(
            grad_scale.astype(jnp.bfloat16), "fsdp", scatter_dimension=0, tiled=True
        ).astype(jnp.float32),
    )
    summed_mats, summed_vecs, summed_scale = (
        lax.psum(owned_mats.astype(jnp.bfloat16), "ctx").astype(jnp.float32),
        lax.psum(owned_vecs.astype(jnp.bfloat16), "ctx").astype(jnp.float32),
        lax.psum(owned_scale.astype(jnp.bfloat16), "ctx").astype(jnp.float32),
    )
    return (
        layer_out,
        grad_inputs[None],
        summed_vecs[0],
        summed_mats[0],
        summed_vecs[1],
        summed_mats[1],
        summed_mats[2],
        summed_vecs[2],
        summed_scale,
        summed_mats[3],
        summed_vecs[3],
        summed_mats[4],
        summed_mats[5],
    )


def solution(mesh):
    placed = (
        P("fsdp", "ctx", None),
        P("fsdp", "ctx", None),
        P("fsdp", None),
        P(),
        P("fsdp"),
        P("fsdp", None),
        P("fsdp"),
        P("fsdp", None),
        P("fsdp", None),
        P("fsdp"),
        P("fsdp"),
        P("fsdp", None),
        P("fsdp"),
        P("fsdp", None),
        P("fsdp", None),
    )
    return jax.shard_map(
        local,
        mesh=mesh,
        in_specs=placed,
        out_specs=(
            P("fsdp", "ctx", None),
            P("fsdp", "ctx", None),
            P("fsdp"),
            P("fsdp", None),
            P("fsdp"),
            P("fsdp", None),
            P("fsdp", None),
            P("fsdp"),
            P("fsdp"),
            P("fsdp", None),
            P("fsdp"),
            P("fsdp", None),
            P("fsdp", None),
        ),
        check_vma=False,
    )
```

profile of v0, /device:TPU:0, one launch (start us, length us, event | category | flops | bytes accessed | tf_op | source)
XLA Modules:
  0.0 1874.1 jit_solution(12044296254598671980)
XLA Ops:
  36.0 220.5 %all-gather.2.cloned.1.call-done = bf16[6,1280,1280]{2,1,0:T(8,128)(2,1)} async-done(((bf16[6,640,1280]{2,1,0:T(8,128)(2,1)}), bf16[6,1280,1280]{2,1,0:T(8,128)(2,1)}) %all-gather.2.cloned.1.call-update) | async-done | bytes 19660816 | tf_op jit(solution)/shard_map/all_gather | solution.py:148
  276.1 360.9 %while.43 = (s32[]{:T(128)}, bf16[2,256,1280]{1,2,0:T(8,128)(2,1)}, f32[16,256]{1,0:T(8,128)S(1)}, f32[16,256]{1,0:T(8,128)S(1)}, f32[256,16,80]{0,2,1:T(8,128)S...) while((s32[]{:T(128)}, bf16[2,256,1280]{1,2,0:T(8,128)(2,1)}, ...), condition=%wide.region_11.12_spmd, body=%wide.region_6.11_spmd.sunk | while | flops 346932224 | bytes 28192232 | solution.py:188
  276.5 19.6 %collective-permute-done = bf16[2,256,1280]{1,2,0:T(8,128)(2,1)S(1)} collective-permute-done((bf16[2,256,1280]{1,2,0:T(8,128)(2,1)}, bf16[2,256,1280]{1,2,0:T(8,128)(2,1)S(1)}, u32[]{:S(2)}, u32[]{:S(2)}) %collective-permute-start) | collective-permute-done | bytes 1310752 | tf_op jit(solution)/shard_map/while/body/eval_jaxpr/ppermute | solution.py:21
  300.5 19.6 %collective-permute-done = bf16[2,256,1280]{1,2,0:T(8,128)(2,1)S(1)} collective-permute-done((bf16[2,256,1280]{1,2,0:T(8,128)(2,1)}, bf16[2,256,1280]{1,2,0:T(8,128)(2,1)S(1)}, u32[]{:S(2)}, u32[]{:S(2)}) %collective-permute-start) | collective-permute-done | bytes 1310752 | tf_op jit(solution)/shard_map/while/body/eval_jaxpr/ppermute | solution.py:21
  324.6 19.6 %collective-permute-done = bf16[2,256,1280]{1,2,0:T(8,128)(2,1)S(1)} collective-permute-done((bf16[2,256,1280]{1,2,0:T(8,128)(2,1)}, bf16[2,256,1280]{1,2,0:T(8,128)(2,1)S(1)}, u32[]{:S(2)}, u32[]{:S(2)}) %collective-permute-start) | collective-permute-done | bytes 1310752 | tf_op jit(solution)/shard_map/while/body/eval_jaxpr/ppermute | solution.py:21
  348.6 19.6 %collective-permute-done = bf16[2,256,1280]{1,2,0:T(8,128)(2,1)S(1)} collective-permute-done((bf16[2,256,1280]{1,2,0:T(8,128)(2,1)}, bf16[2,256,1280]{1,2,0:T(8,128)(2,1)S(1)}, u32[]{:S(2)}, u32[]{:S(2)}) %collective-permute-start) | collective-permute-done | bytes 1310752 | tf_op jit(solution)/shard_map/while/body/eval_jaxpr/ppermute | solution.py:21
  372.7 19.6 %collective-permute-done = bf16[2,256,1280]{1,2,0:T(8,128)(2,1)S(1)} collective-permute-done((bf16[2,256,1280]{1,2,0:T(8,128)(2,1)}, bf16[2,256,1280]{1,2,0:T(8,128)(2,1)S(1)}, u32[]{:S(2)}, u32[]{:S(2)}) %collective-permute-start) | collective-permute-done | bytes 1310752 | tf_op jit(solution)/shard_map/while/body/eval_jaxpr/ppermute | solution.py:21
  396.7 19.6 %collective-permute-done = bf16[2,256,1280]{1,2,0:T(8,128)(2,1)S(1)} collective-permute-done((bf16[2,256,1280]{1,2,0:T(8,128)(2,1)}, bf16[2,256,1280]{1,2,0:T(8,128)(2,1)S(1)}, u32[]{:S(2)}, u32[]{:S(2)}) %collective-permute-start) | collective-permute-done | bytes 1310752 | tf_op jit(solution)/shard_map/while/body/eval_jaxpr/ppermute | solution.py:21
  420.8 19.6 %collective-permute-done = bf16[2,256,1280]{1,2,0:T(8,128)(2,1)S(1)} collective-permute-done((bf16[2,256,1280]{1,2,0:T(8,128)(2,1)}, bf16[2,256,1280]{1,2,0:T(8,128)(2,1)S(1)}, u32[]{:S(2)}, u32[]{:S(2)}) %collective-permute-start) | collective-permute-done | bytes 1310752 | tf_op jit(solution)/shard_map/while/body/eval_jaxpr/ppermute | solution.py:21
  444.8 19.6 %collective-permute-done = bf16[2,256,1280]{1,2,0:T(8,128)(2,1)S(1)} collective-permute-done((bf16[2,256,1280]{1,2,0:T(8,128)(2,1)}, bf16[2,256,1280]{1,2,0:T(8,128)(2,1)S(1)}, u32[]{:S(2)}, u32[]{:S(2)}) %collective-permute-start) | collective-permute-done | bytes 1310752 | tf_op jit(solution)/shard_map/while/body/eval_jaxpr/ppermute | solution.py:21
  468.9 19.6 %collective-permute-done = bf16[2,256,1280]{1,2,0:T(8,128)(2,1)S(1)} collective-permute-done((bf16[2,256,1280]{1,2,0:T(8,128)(2,1)}, bf16[2,256,1280]{1,2,0:T(8,128)(2,1)S(1)}, u32[]{:S(2)}, u32[]{:S(2)}) %collective-permute-start) | collective-permute-done | bytes 1310752 | tf_op jit(solution)/shard_map/while/body/eval_jaxpr/ppermute | solution.py:21
  492.9 19.6 %collective-permute-done = bf16[2,256,1280]{1,2,0:T(8,128)(2,1)S(1)} collective-permute-done((bf16[2,256,1280]{1,2,0:T(8,128)(2,1)}, bf16[2,256,1280]{1,2,0:T(8,128)(2,1)S(1)}, u32[]{:S(2)}, u32[]{:S(2)}) %collective-permute-start) | collective-permute-done | bytes 1310752 | tf_op jit(solution)/shard_map/while/body/eval_jaxpr/ppermute | solution.py:21
  516.9 19.6 %collective-permute-done = bf16[2,256,1280]{1,2,0:T(8,128)(2,1)S(1)} collective-permute-done((bf16[2,256,1280]{1,2,0:T(8,128)(2,1)}, bf16[2,256,1280]{1,2,0:T(8,128)(2,1)S(1)}, u32[]{:S(2)}, u32[]{:S(2)}) %collective-permute-start) | collective-permute-done | bytes 1310752 | tf_op jit(solution)/shard_map/while/body/eval_jaxpr/ppermute | solution.py:21
  541.0 19.6 %collective-permute-done = bf16[2,256,1280]{1,2,0:T(8,128)(2,1)S(1)} collective-permute-done((bf16[2,256,1280]{1,2,0:T(8,128)(2,1)}, bf16[2,256,1280]{1,2,0:T(8,128)(2,1)S(1)}, u32[]{:S(2)}, u32[]{:S(2)}) %collective-permute-start) | collective-permute-done | bytes 1310752 | tf_op jit(solution)/shard_map/while/body/eval_jaxpr/ppermute | solution.py:21
  565.0 19.6 %collective-permute-done = bf16[2,256,1280]{1,2,0:T(8,128)(2,1)S(1)} collective-permute-done((bf16[2,256,1280]{1,2,0:T(8,128)(2,1)}, bf16[2,256,1280]{1,2,0:T(8,128)(2,1)S(1)}, u32[]{:S(2)}, u32[]{:S(2)}) %collective-permute-start) | collective-permute-done | bytes 1310752 | tf_op jit(solution)/shard_map/while/body/eval_jaxpr/ppermute | solution.py:21
  589.1 19.6 %collective-permute-done = bf16[2,256,1280]{1,2,0:T(8,128)(2,1)S(1)} collective-permute-done((bf16[2,256,1280]{1,2,0:T(8,128)(2,1)}, bf16[2,256,1280]{1,2,0:T(8,128)(2,1)S(1)}, u32[]{:S(2)}, u32[]{:S(2)}) %collective-permute-start) | collective-permute-done | bytes 1310752 | tf_op jit(solution)/shard_map/while/body/eval_jaxpr/ppermute | solution.py:21
  613.1 19.6 %collective-permute-done = bf16[2,256,1280]{1,2,0:T(8,128)(2,1)S(1)} collective-permute-done((bf16[2,256,1280]{1,2,0:T(8,128)(2,1)}, bf16[2,256,1280]{1,2,0:T(8,128)(2,1)S(1)}, u32[]{:S(2)}, u32[]{:S(2)}) %collective-permute-start) | collective-permute-done | bytes 1310752 | tf_op jit(solution)/shard_map/while/body/eval_jaxpr/ppermute | solution.py:21
  656.6 737.3 %while.44 = (s32[]{:T(128)}, bf16[2,256,1280]{1,2,0:T(8,128)(2,1)}, f32[2,256,1280]{1,2,0:T(8,128)}, f32[256,16,80]{0,2,1:T(8,128)}, s32[256]{0:T(256)S(1)}, /*i...) while((s32[]{:T(128)}, bf16[2,256,1280]{1,2,0:T(8,128)(2,1)}, ...), condition=%wide.region_17.18_spmd.clone, body=%wide.region_14.17_spmd.clone.sunk | while | flops 851416064 | bytes 70905472 | solution.py:252
  670.4 18.2 collective-permute-done.2
  691.6 11.0 collective-permute-done.1
  717.8 16.9 collective-permute-done.2
  737.7 11.0 collective-permute-done.1
  763.9 16.9 collective-permute-done.2
  783.8 11.0 collective-permute-done.1
  809.9 16.9 collective-permute-done.2
  829.9 11.0 collective-permute-done.1
  856.0 16.9 collective-permute-done.2
  875.9 11.0 collective-permute-done.1
  902.1 16.9 collective-permute-done.2
  922.0 11.0 collective-permute-done.1
  948.1 16.9 collective-permute-done.2
  968.1 11.0 collective-permute-done.1
  994.2 16.9 collective-permute-done.2
  1014.1 11.0 collective-permute-done.1
  1040.3 16.9 collective-permute-done.2
  1060.2 11.0 collective-permute-done.1
  1086.4 16.9 collective-permute-done.2
  1132.4 16.9 collective-permute-done.2
  1178.5 16.9 collective-permute-done.2
  1224.6 16.9 collective-permute-done.2
  1270.7 16.9 collective-permute-done.2
  1316.7 16.9 collective-permute-done.2
  1362.8 16.9 collective-permute-done.2
  1426.6 204.2 %reduce-scatter.5.cloned.1.call-done = bf16[6,640,1280]{2,1,0:T(8,128)(2,1)} async-done(((bf16[6,1280,1280]{2,1,0:T(8,128)(2,1)}), bf16[6,640,1280]{2,1,0:T(8,128)(2,1)}) %reduce-scatter.5.cloned.1.call-update) | async-done | bytes 9830416 | tf_op jit(solution)/shard_map/reduce_scatter | solution.py:279
  1647.1 35.5 %all-reduce.2 = (bf16[4,640]{1,0:T(4,128)(2,1)S(1)}, bf16[40]{0:T(256)(128)(2,1)S(1)}) all-reduce(bf16[4,640]{1,0:T(4,128)(2,1)S(1)} %copy.82, bf16[40]{0:T(256)(128)(2,1)S(1)} %dynamic-slice.2), channel_id=1, replica_groups=mesh['ctx'=16,'fsdp'=2] {'ctx'}, use_global_device_ids=true, to_apply=%region_24.25 | all-reduce | flops 2600 | bytes 10400 | tf_op jit(solution)/shard_map/psum | solution.py:291
  1683.7 157.1 %all-reduce.5.cloned.1.call-done = bf16[6,640,1280]{2,1,0:T(8,128)(2,1)} async-done(((bf16[6,640,1280]{2,1,0:T(8,128)(2,1)}), bf16[6,640,1280]{2,1,0:T(8,128)(2,1)}) %all-reduce.5.cloned.1.call-update) | async-done | bytes 9830416 | tf_op jit(solution)/shard_map/psum | solution.py:290
  1840.9 12.3 convert_element_type.241
  1853.1 13.9 slice_bitcast_fusion
  (746 shorter events, 547.3 us)
Async XLA Ops:
  7.2 249.4 %all-gather.2.cloned.1.call-start = ((), (), s32[]{:S(2)}) async-start(), calls=%async_computation.2 | async-start | bytes 29491200 | tf_op jit(solution)/shard_map/all_gather | solution.py:148
  22.2 1608.6 %reduce-scatter.5.cloned.1.call-start = ((), (), s32[]{:S(2)}) async-start(), calls=%async_computation.3 | async-start | bytes 29491200 | tf_op jit(solution)/shard_map/reduce_scatter | solution.py:279
  276.1 20.0 %collective-permute-start = (bf16[2,256,1280]{1,2,0:T(8,128)(2,1)}, bf16[2,256,1280]{1,2,0:T(8,128)(2,1)S(1)}, u32[]{:S(2)}, u32[]{:S(2)}) collective-permute-start(bf16[2,256,1280]{1,2,0:T(8,128)(2,1)} %get-tuple-element.1084), channel_id=1, source_target_pairs={{0,2},{2,4},{4,6},{6,8},{8,10},{10,12},{12,14},{14,16},{16,18},{18... | collective-permute-start | bytes 3932168 | tf_op jit(solution)/shard_map/while/body/eval_jaxpr/ppermute | solution.py:21
  300.2 19.9 %collective-permute-start = (bf16[2,256,1280]{1,2,0:T(8,128)(2,1)}, bf16[2,256,1280]{1,2,0:T(8,128)(2,1)S(1)}, u32[]{:S(2)}, u32[]{:S(2)}) collective-permute-start(bf16[2,256,1280]{1,2,0:T(8,128)(2,1)} %get-tuple-element.1084), channel_id=1, source_target_pairs={{0,2},{2,4},{4,6},{6,8},{8,10},{10,12},{12,14},{14,16},{16,18},{18... | collective-permute-start | bytes 3932168 | tf_op jit(solution)/shard_map/while/body/eval_jaxpr/ppermute | solution.py:21
  324.2 19.9 %collective-permute-start = (bf16[2,256,1280]{1,2,0:T(8,128)(2,1)}, bf16[2,256,1280]{1,2,0:T(8,128)(2,1)S(1)}, u32[]{:S(2)}, u32[]{:S(2)}) collective-permute-start(bf16[2,256,1280]{1,2,0:T(8,128)(2,1)} %get-tuple-element.1084), channel_id=1, source_target_pairs={{0,2},{2,4},{4,6},{6,8},{8,10},{10,12},{12,14},{14,16},{16,18},{18... | collective-permute-start | bytes 3932168 | tf_op jit(solution)/shard_map/while/body/eval_jaxpr/ppermute | solution.py:21
  348.3 19.9 %collective-permute-start = (bf16[2,256,1280]{1,2,0:T(8,128)(2,1)}, bf16[2,256,1280]{1,2,0:T(8,128)(2,1)S(1)}, u32[]{:S(2)}, u32[]{:S(2)}) collective-permute-start(bf16[2,256,1280]{1,2,0:T(8,128)(2,1)} %get-tuple-element.1084), channel_id=1, source_target_pairs={{0,2},{2,4},{4,6},{6,8},{8,10},{10,12},{12,14},{14,16},{16,18},{18... | collective-permute-start | bytes 3932168 | tf_op jit(solution)/shard_map/while/body/eval_jaxpr/ppermute | solution.py:21
  372.3 19.9 %collective-permute-start = (bf16[2,256,1280]{1,2,0:T(8,128)(2,1)}, bf16[2,256,1280]{1,2,0:T(8,128)(2,1)S(1)}, u32[]{:S(2)}, u32[]{:S(2)}) collective-permute-start(bf16[2,256,1280]{1,2,0:T(8,128)(2,1)} %get-tuple-element.1084), channel_id=1, source_target_pairs={{0,2},{2,4},{4,6},{6,8},{8,10},{10,12},{12,14},{14,16},{16,18},{18... | collective-permute-start | bytes 3932168 | tf_op jit(solution)/shard_map/while/body/eval_jaxpr/ppermute | solution.py:21
  396.4 19.9 %collective-permute-start = (bf16[2,256,1280]{1,2,0:T(8,128)(2,1)}, bf16[2,256,1280]{1,2,0:T(8,128)(2,1)S(1)}, u32[]{:S(2)}, u32[]{:S(2)}) collective-permute-start(bf16[2,256,1280]{1,2,0:T(8,128)(2,1)} %get-tuple-element.1084), channel_id=1, source_target_pairs={{0,2},{2,4},{4,6},{6,8},{8,10},{10,12},{12,14},{14,16},{16,18},{18... | collective-permute-start | bytes 3932168 | tf_op jit(solution)/shard_map/while/body/eval_jaxpr/ppermute | solution.py:21
  420.4 19.9 %collective-permute-start = (bf16[2,256,1280]{1,2,0:T(8,128)(2,1)}, bf16[2,256,1280]{1,2,0:T(8,128)(2,1)S(1)}, u32[]{:S(2)}, u32[]{:S(2)}) collective-permute-start(bf16[2,256,1280]{1,2,0:T(8,128)(2,1)} %get-tuple-element.1084), channel_id=1, source_target_pairs={{0,2},{2,4},{4,6},{6,8},{8,10},{10,12},{12,14},{14,16},{16,18},{18... | collective-permute-start | bytes 3932168 | tf_op jit(solution)/shard_map/while/body/eval_jaxpr/ppermute | solution.py:21
  444.4 19.9 %collective-permute-start = (bf16[2,256,1280]{1,2,0:T(8,128)(2,1)}, bf16[2,256,1280]{1,2,0:T(8,128)(2,1)S(1)}, u32[]{:S(2)}, u32[]{:S(2)}) collective-permute-start(bf16[2,256,1280]{1,2,0:T(8,128)(2,1)} %get-tuple-element.1084), channel_id=1, source_target_pairs={{0,2},{2,4},{4,6},{6,8},{8,10},{10,12},{12,14},{14,16},{16,18},{18... | collective-permute-start | bytes 3932168 | tf_op jit(solution)/shard_map/while/body/eval_jaxpr/ppermute | solution.py:21
  468.5 19.9 %collective-permute-start = (bf16[2,256,1280]{1,2,0:T(8,128)(2,1)}, bf16[2,256,1280]{1,2,0:T(8,128)(2,1)S(1)}, u32[]{:S(2)}, u32[]{:S(2)}) collective-permute-start(bf16[2,256,1280]{1,2,0:T(8,128)(2,1)} %get-tuple-element.1084), channel_id=1, source_target_pairs={{0,2},{2,4},{4,6},{6,8},{8,10},{10,12},{12,14},{14,16},{16,18},{18... | collective-permute-start | bytes 3932168 | tf_op jit(solution)/shard_map/while/body/eval_jaxpr/ppermute | solution.py:21
  492.5 19.9 %collective-permute-start = (bf16[2,256,1280]{1,2,0:T(8,128)(2,1)}, bf16[2,256,1280]{1,2,0:T(8,128)(2,1)S(1)}, u32[]{:S(2)}, u32[]{:S(2)}) collective-permute-start(bf16[2,256,1280]{1,2,0:T(8,128)(2,1)} %get-tuple-element.1084), channel_id=1, source_target_pairs={{0,2},{2,4},{4,6},{6,8},{8,10},{10,12},{12,14},{14,16},{16,18},{18... | collective-permute-start | bytes 3932168 | tf_op jit(solution)/shard_map/while/body/eval_jaxpr/ppermute | solution.py:21
  516.6 19.9 %collective-permute-start = (bf16[2,256,1280]{1,2,0:T(8,128)(2,1)}, bf16[2,256,1280]{1,2,0:T(8,128)(2,1)S(1)}, u32[]{:S(2)}, u32[]{:S(2)}) collective-permute-start(bf16[2,256,1280]{1,2,0:T(8,128)(2,1)} %get-tuple-element.1084), channel_id=1, source_target_pairs={{0,2},{2,4},{4,6},{6,8},{8,10},{10,12},{12,14},{14,16},{16,18},{18... | collective-permute-start | bytes 3932168 | tf_op jit(solution)/shard_map/while/body/eval_jaxpr/ppermute | solution.py:21
  540.6 19.9 %collective-permute-start = (bf16[2,256,1280]{1,2,0:T(8,128)(2,1)}, bf16[2,256,1280]{1,2,0:T(8,128)(2,1)S(1)}, u32[]{:S(2)}, u32[]{:S(2)}) collective-permute-start(bf16[2,256,1280]{1,2,0:T(8,128)(2,1)} %get-tuple-element.1084), channel_id=1, source_target_pairs={{0,2},{2,4},{4,6},{6,8},{8,10},{10,12},{12,14},{14,16},{16,18},{18... | collective-permute-start | bytes 3932168 | tf_op jit(solution)/shard_map/while/body/eval_jaxpr/ppermute | solution.py:21
  668.6 20.0 %collective-permute-start.2 = (bf16[2,256,1280]{1,2,0:T(8,128)(2,1)}, bf16[2,256,1280]{1,2,0:T(8,128)(2,1)}, u32[]{:S(2)}, u32[]{:S(2)}) collective-permute-start(bf16[2,256,1280]{1,2,0:T(8,128)(2,1)} %fusion.203), channel_id=1, source_target_pairs={{0,2},{2,4},{4,6},{6,8},{8,10},{10,12},{12,14},{14,16},{16,18},{18... | collective-permute-start | bytes 3932168 | tf_op jit(solution)/shard_map/while/body/eval_jaxpr/ppermute | solution.py:21
  668.6 34.1 %collective-permute-start.1 = (bf16[2,256,1280]{1,2,0:T(8,128)(2,1)}, bf16[2,256,1280]{1,2,0:T(8,128)(2,1)}, u32[]{:S(2)}, u32[]{:S(2)}) collective-permute-start(bf16[2,256,1280]{1,2,0:T(8,128)(2,1)} %copy.110), channel_id=1, source_target_pairs={{0,2},{2,4},{4,6},{6,8},{8,10},{10,12},{12,14},{14,16},{16,18},{18... | collective-permute-start | bytes 3932168 | tf_op jit(solution)/shard_map/while/body/eval_jaxpr/ppermute | solution.py:21
  714.7 20.0 %collective-permute-start.2 = (bf16[2,256,1280]{1,2,0:T(8,128)(2,1)}, bf16[2,256,1280]{1,2,0:T(8,128)(2,1)}, u32[]{:S(2)}, u32[]{:S(2)}) collective-permute-start(bf16[2,256,1280]{1,2,0:T(8,128)(2,1)} %fusion.203), channel_id=1, source_target_pairs={{0,2},{2,4},{4,6},{6,8},{8,10},{10,12},{12,14},{14,16},{16,18},{18... | collective-permute-start | bytes 3932168 | tf_op jit(solution)/shard_map/while/body/eval_jaxpr/ppermute | solution.py:21
  714.7 34.1 %collective-permute-start.1 = (bf16[2,256,1280]{1,2,0:T(8,128)(2,1)}, bf16[2,256,1280]{1,2,0:T(8,128)(2,1)}, u32[]{:S(2)}, u32[]{:S(2)}) collective-permute-start(bf16[2,256,1280]{1,2,0:T(8,128)(2,1)} %copy.110), channel_id=1, source_target_pairs={{0,2},{2,4},{4,6},{6,8},{8,10},{10,12},{12,14},{14,16},{16,18},{18... | collective-permute-start | bytes 3932168 | tf_op jit(solution)/shard_map/while/body/eval_jaxpr/ppermute | solution.py:21
  760.7 20.0 %collective-permute-start.2 = (bf16[2,256,1280]{1,2,0:T(8,128)(2,1)}, bf16[2,256,1280]{1,2,0:T(8,128)(2,1)}, u32[]{:S(2)}, u32[]{:S(2)}) collective-permute-start(bf16[2,256,1280]{1,2,0:T(8,128)(2,1)} %fusion.203), channel_id=1, source_target_pairs={{0,2},{2,4},{4,6},{6,8},{8,10},{10,12},{12,14},{14,16},{16,18},{18... | collective-permute-start | bytes 3932168 | tf_op jit(solution)/shard_map/while/body/eval_jaxpr/ppermute | solution.py:21
  760.7 34.1 %collective-permute-start.1 = (bf16[2,256,1280]{1,2,0:T(8,128)(2,1)}, bf16[2,256,1280]{1,2,0:T(8,128)(2,1)}, u32[]{:S(2)}, u32[]{:S(2)}) collective-permute-start(bf16[2,256,1280]{1,2,0:T(8,128)(2,1)} %copy.110), channel_id=1, source_target_pairs={{0,2},{2,4},{4,6},{6,8},{8,10},{10,12},{12,14},{14,16},{16,18},{18... | collective-permute-start | bytes 3932168 | tf_op jit(solution)/shard_map/while/body/eval_jaxpr/ppermute | solution.py:21
  806.8 20.0 %collective-permute-start.2 = (bf16[2,256,1280]{1,2,0:T(8,128)(2,1)}, bf16[2,256,1280]{1,2,0:T(8,128)(2,1)}, u32[]{:S(2)}, u32[]{:S(2)}) collective-permute-start(bf16[2,256,1280]{1,2,0:T(8,128)(2,1)} %fusion.203), channel_id=1, source_target_pairs={{0,2},{2,4},{4,6},{6,8},{8,10},{10,12},{12,14},{14,16},{16,18},{18... | collective-permute-start | bytes 3932168 | tf_op jit(solution)/shard_map/while/body/eval_jaxpr/ppermute | solution.py:21
  806.8 34.1 %collective-permute-start.1 = (bf16[2,256,1280]{1,2,0:T(8,128)(2,1)}, bf16[2,256,1280]{1,2,0:T(8,128)(2,1)}, u32[]{:S(2)}, u32[]{:S(2)}) collective-permute-start(bf16[2,256,1280]{1,2,0:T(8,128)(2,1)} %copy.110), channel_id=1, source_target_pairs={{0,2},{2,4},{4,6},{6,8},{8,10},{10,12},{12,14},{14,16},{16,18},{18... | collective-permute-start | bytes 3932168 | tf_op jit(solution)/shard_map/while/body/eval_jaxpr/ppermute | solution.py:21
  852.9 20.0 %collective-permute-start.2 = (bf16[2,256,1280]{1,2,0:T(8,128)(2,1)}, bf16[2,256,1280]{1,2,0:T(8,128)(2,1)}, u32[]{:S(2)}, u32[]{:S(2)}) collective-permute-start(bf16[2,256,1280]{1,2,0:T(8,128)(2,1)} %fusion.203), channel_id=1, source_target_pairs={{0,2},{2,4},{4,6},{6,8},{8,10},{10,12},{12,14},{14,16},{16,18},{18... | collective-permute-start | bytes 3932168 | tf_op jit(solution)/shard_map/while/body/eval_jaxpr/ppermute | solution.py:21
  852.9 34.1 %collective-permute-start.1 = (bf16[2,256,1280]{1,2,0:T(8,128)(2,1)}, bf16[2,256,1280]{1,2,0:T(8,128)(2,1)}, u32[]{:S(2)}, u32[]{:S(2)}) collective-permute-start(bf16[2,256,1280]{1,2,0:T(8,128)(2,1)} %copy.110), channel_id=1, source_target_pairs={{0,2},{2,4},{4,6},{6,8},{8,10},{10,12},{12,14},{14,16},{16,18},{18... | collective-permute-start | bytes 3932168 | tf_op jit(solution)/shard_map/while/body/eval_jaxpr/ppermute | solution.py:21
  898.9 20.0 %collective-permute-start.2 = (bf16[2,256,1280]{1,2,0:T(8,128)(2,1)}, bf16[2,256,1280]{1,2,0:T(8,128)(2,1)}, u32[]{:S(2)}, u32[]{:S(2)}) collective-permute-start(bf16[2,256,1280]{1,2,0:T(8,128)(2,1)} %fusion.203), channel_id=1, source_target_pairs={{0,2},{2,4},{4,6},{6,8},{8,10},{10,12},{12,14},{14,16},{16,18},{18... | collective-permute-start | bytes 3932168 | tf_op jit(solution)/shard_map/while/body/eval_jaxpr/ppermute | solution.py:21
  898.9 34.1 %collective-permute-start.1 = (bf16[2,256,1280]{1,2,0:T(8,128)(2,1)}, bf16[2,256,1280]{1,2,0:T(8,128)(2,1)}, u32[]{:S(2)}, u32[]{:S(2)}) collective-permute-start(bf16[2,256,1280]{1,2,0:T(8,128)(2,1)} %copy.110), channel_id=1, source_target_pairs={{0,2},{2,4},{4,6},{6,8},{8,10},{10,12},{12,14},{14,16},{16,18},{18... | collective-permute-start | bytes 3932168 | tf_op jit(solution)/shard_map/while/body/eval_jaxpr/ppermute | solution.py:21
  945.0 20.0 %collective-permute-start.2 = (bf16[2,256,1280]{1,2,0:T(8,128)(2,1)}, bf16[2,256,1280]{1,2,0:T(8,128)(2,1)}, u32[]{:S(2)}, u32[]{:S(2)}) collective-permute-start(bf16[2,256,1280]{1,2,0:T(8,128)(2,1)} %fusion.203), channel_id=1, source_target_pairs={{0,2},{2,4},{4,6},{6,8},{8,10},{10,12},{12,14},{14,16},{16,18},{18... | collective-permute-start | bytes 3932168 | tf_op jit(solution)/shard_map/while/body/eval_jaxpr/ppermute | solution.py:21
  945.0 34.1 %collective-permute-start.1 = (bf16[2,256,1280]{1,2,0:T(8,128)(2,1)}, bf16[2,256,1280]{1,2,0:T(8,128)(2,1)}, u32[]{:S(2)}, u32[]{:S(2)}) collective-permute-start(bf16[2,256,1280]{1,2,0:T(8,128)(2,1)} %copy.110), channel_id=1, source_target_pairs={{0,2},{2,4},{4,6},{6,8},{8,10},{10,12},{12,14},{14,16},{16,18},{18... | collective-permute-start | bytes 3932168 | tf_op jit(solution)/shard_map/while/body/eval_jaxpr/ppermute | solution.py:21
  991.1 20.0 %collective-permute-start.2 = (bf16[2,256,1280]{1,2,0:T(8,128)(2,1)}, bf16[2,256,1280]{1,2,0:T(8,128)(2,1)}, u32[]{:S(2)}, u32[]{:S(2)}) collective-permute-start(bf16[2,256,1280]{1,2,0:T(8,128)(2,1)} %fusion.203), channel_id=1, source_target_pairs={{0,2},{2,4},{4,6},{6,8},{8,10},{10,12},{12,14},{14,16},{16,18},{18... | collective-permute-start | bytes 3932168 | tf_op jit(solution)/shard_map/while/body/eval_jaxpr/ppermute | solution.py:21
  991.1 34.1 %collective-permute-start.1 = (bf16[2,256,1280]{1,2,0:T(8,128)(2,1)}, bf16[2,256,1280]{1,2,0:T(8,128)(2,1)}, u32[]{:S(2)}, u32[]{:S(2)}) collective-permute-start(bf16[2,256,1280]{1,2,0:T(8,128)(2,1)} %copy.110), channel_id=1, source_target_pairs={{0,2},{2,4},{4,6},{6,8},{8,10},{10,12},{12,14},{14,16},{16,18},{18... | collective-permute-start | bytes 3932168 | tf_op jit(solution)/shard_map/while/body/eval_jaxpr/ppermute | solution.py:21
  1037.2 20.0 %collective-permute-start.2 = (bf16[2,256,1280]{1,2,0:T(8,128)(2,1)}, bf16[2,256,1280]{1,2,0:T(8,128)(2,1)}, u32[]{:S(2)}, u32[]{:S(2)}) collective-permute-start(bf16[2,256,1280]{1,2,0:T(8,128)(2,1)} %fusion.203), channel_id=1, source_target_pairs={{0,2},{2,4},{4,6},{6,8},{8,10},{10,12},{12,14},{14,16},{16,18},{18... | collective-permute-start | bytes 3932168 | tf_op jit(solution)/shard_map/while/body/eval_jaxpr/ppermute | solution.py:21
  1037.2 34.1 %collective-permute-start.1 = (bf16[2,256,1280]{1,2,0:T(8,128)(2,1)}, bf16[2,256,1280]{1,2,0:T(8,128)(2,1)}, u32[]{:S(2)}, u32[]{:S(2)}) collective-permute-start(bf16[2,256,1280]{1,2,0:T(8,128)(2,1)} %copy.110), channel_id=1, source_target_pairs={{0,2},{2,4},{4,6},{6,8},{8,10},{10,12},{12,14},{14,16},{16,18},{18... | collective-permute-start | bytes 3932168 | tf_op jit(solution)/shard_map/while/body/eval_jaxpr/ppermute | solution.py:21
  1083.2 20.0 %collective-permute-start.2 = (bf16[2,256,1280]{1,2,0:T(8,128)(2,1)}, bf16[2,256,1280]{1,2,0:T(8,128)(2,1)}, u32[]{:S(2)}, u32[]{:S(2)}) collective-permute-start(bf16[2,256,1280]{1,2,0:T(8,128)(2,1)} %fusion.203), channel_id=1, source_target_pairs={{0,2},{2,4},{4,6},{6,8},{8,10},{10,12},{12,14},{14,16},{16,18},{18... | collective-permute-start | bytes 3932168 | tf_op jit(solution)/shard_map/while/body/eval_jaxpr/ppermute | solution.py:21
  1083.2 34.1 %collective-permute-start.1 = (bf16[2,256,1280]{1,2,0:T(8,128)(2,1)}, bf16[2,256,1280]{1,2,0:T(8,128)(2,1)}, u32[]{:S(2)}, u32[]{:S(2)}) collective-permute-start(bf16[2,256,1280]{1,2,0:T(8,128)(2,1)} %copy.110), channel_id=1, source_target_pairs={{0,2},{2,4},{4,6},{6,8},{8,10},{10,12},{12,14},{14,16},{16,18},{18... | collective-permute-start | bytes 3932168 | tf_op jit(solution)/shard_map/while/body/eval_jaxpr/ppermute | solution.py:21
  1129.3 20.0 %collective-permute-start.2 = (bf16[2,256,1280]{1,2,0:T(8,128)(2,1)}, bf16[2,256,1280]{1,2,0:T(8,128)(2,1)}, u32[]{:S(2)}, u32[]{:S(2)}) collective-permute-start(bf16[2,256,1280]{1,2,0:T(8,128)(2,1)} %fusion.203), channel_id=1, source_target_pairs={{0,2},{2,4},{4,6},{6,8},{8,10},{10,12},{12,14},{14,16},{16,18},{18... | collective-permute-start | bytes 3932168 | tf_op jit(solution)/shard_map/while/body/eval_jaxpr/ppermute | solution.py:21
  1129.3 34.1 %collective-permute-start.1 = (bf16[2,256,1280]{1,2,0:T(8,128)(2,1)}, bf16[2,256,1280]{1,2,0:T(8,128)(2,1)}, u32[]{:S(2)}, u32[]{:S(2)}) collective-permute-start(bf16[2,256,1280]{1,2,0:T(8,128)(2,1)} %copy.110), channel_id=1, source_target_pairs={{0,2},{2,4},{4,6},{6,8},{8,10},{10,12},{12,14},{14,16},{16,18},{18... | collective-permute-start | bytes 3932168 | tf_op jit(solution)/shard_map/while/body/eval_jaxpr/ppermute | solution.py:21
  1175.4 20.0 %collective-permute-start.2 = (bf16[2,256,1280]{1,2,0:T(8,128)(2,1)}, bf16[2,256,1280]{1,2,0:T(8,128)(2,1)}, u32[]{:S(2)}, u32[]{:S(2)}) collective-permute-start(bf16[2,256,1280]{1,2,0:T(8,128)(2,1)} %fusion.203), channel_id=1, source_target_pairs={{0,2},{2,4},{4,6},{6,8},{8,10},{10,12},{12,14},{14,16},{16,18},{18... | collective-permute-start | bytes 3932168 | tf_op jit(solution)/shard_map/while/body/eval_jaxpr/ppermute | solution.py:21
  1175.4 34.1 %collective-permute-start.1 = (bf16[2,256,1280]{1,2,0:T(8,128)(2,1)}, bf16[2,256,1280]{1,2,0:T(8,128)(2,1)}, u32[]{:S(2)}, u32[]{:S(2)}) collective-permute-start(bf16[2,256,1280]{1,2,0:T(8,128)(2,1)} %copy.110), channel_id=1, source_target_pairs={{0,2},{2,4},{4,6},{6,8},{8,10},{10,12},{12,14},{14,16},{16,18},{18... | collective-permute-start | bytes 3932168 | tf_op jit(solution)/shard_map/while/body/eval_jaxpr/ppermute | solution.py:21
  1221.4 20.0 %collective-permute-start.2 = (bf16[2,256,1280]{1,2,0:T(8,128)(2,1)}, bf16[2,256,1280]{1,2,0:T(8,128)(2,1)}, u32[]{:S(2)}, u32[]{:S(2)}) collective-permute-start(bf16[2,256,1280]{1,2,0:T(8,128)(2,1)} %fusion.203), channel_id=1, source_target_pairs={{0,2},{2,4},{4,6},{6,8},{8,10},{10,12},{12,14},{14,16},{16,18},{18... | collective-permute-start | bytes 3932168 | tf_op jit(solution)/shard_map/while/body/eval_jaxpr/ppermute | solution.py:21
  1221.4 34.1 %collective-permute-start.1 = (bf16[2,256,1280]{1,2,0:T(8,128)(2,1)}, bf16[2,256,1280]{1,2,0:T(8,128)(2,1)}, u32[]{:S(2)}, u32[]{:S(2)}) collective-permute-start(bf16[2,256,1280]{1,2,0:T(8,128)(2,1)} %copy.110), channel_id=1, source_target_pairs={{0,2},{2,4},{4,6},{6,8},{8,10},{10,12},{12,14},{14,16},{16,18},{18... | collective-permute-start | bytes 3932168 | tf_op jit(solution)/shard_map/while/body/eval_jaxpr/ppermute | solution.py:21
  1267.5 20.0 %collective-permute-start.2 = (bf16[2,256,1280]{1,2,0:T(8,128)(2,1)}, bf16[2,256,1280]{1,2,0:T(8,128)(2,1)}, u32[]{:S(2)}, u32[]{:S(2)}) collective-permute-start(bf16[2,256,1280]{1,2,0:T(8,128)(2,1)} %fusion.203), channel_id=1, source_target_pairs={{0,2},{2,4},{4,6},{6,8},{8,10},{10,12},{12,14},{14,16},{16,18},{18... | collective-permute-start | bytes 3932168 | tf_op jit(solution)/shard_map/while/body/eval_jaxpr/ppermute | solution.py:21
  1267.5 34.1 %collective-permute-start.1 = (bf16[2,256,1280]{1,2,0:T(8,128)(2,1)}, bf16[2,256,1280]{1,2,0:T(8,128)(2,1)}, u32[]{:S(2)}, u32[]{:S(2)}) collective-permute-start(bf16[2,256,1280]{1,2,0:T(8,128)(2,1)} %copy.110), channel_id=1, source_target_pairs={{0,2},{2,4},{4,6},{6,8},{8,10},{10,12},{12,14},{14,16},{16,18},{18... | collective-permute-start | bytes 3932168 | tf_op jit(solution)/shard_map/while/body/eval_jaxpr/ppermute | solution.py:21
  1313.6 20.0 %collective-permute-start.2 = (bf16[2,256,1280]{1,2,0:T(8,128)(2,1)}, bf16[2,256,1280]{1,2,0:T(8,128)(2,1)}, u32[]{:S(2)}, u32[]{:S(2)}) collective-permute-start(bf16[2,256,1280]{1,2,0:T(8,128)(2,1)} %fusion.203), channel_id=1, source_target_pairs={{0,2},{2,4},{4,6},{6,8},{8,10},{10,12},{12,14},{14,16},{16,18},{18... | collective-permute-start | bytes 3932168 | tf_op jit(solution)/shard_map/while/body/eval_jaxpr/ppermute | solution.py:21
  1313.6 34.1 %collective-permute-start.1 = (bf16[2,256,1280]{1,2,0:T(8,128)(2,1)}, bf16[2,256,1280]{1,2,0:T(8,128)(2,1)}, u32[]{:S(2)}, u32[]{:S(2)}) collective-permute-start(bf16[2,256,1280]{1,2,0:T(8,128)(2,1)} %copy.110), channel_id=1, source_target_pairs={{0,2},{2,4},{4,6},{6,8},{8,10},{10,12},{12,14},{14,16},{16,18},{18... | collective-permute-start | bytes 3932168 | tf_op jit(solution)/shard_map/while/body/eval_jaxpr/ppermute | solution.py:21
  1359.7 20.0 %collective-permute-start.2 = (bf16[2,256,1280]{1,2,0:T(8,128)(2,1)}, bf16[2,256,1280]{1,2,0:T(8,128)(2,1)}, u32[]{:S(2)}, u32[]{:S(2)}) collective-permute-start(bf16[2,256,1280]{1,2,0:T(8,128)(2,1)} %fusion.203), channel_id=1, source_target_pairs={{0,2},{2,4},{4,6},{6,8},{8,10},{10,12},{12,14},{14,16},{16,18},{18... | collective-permute-start | bytes 3932168 | tf_op jit(solution)/shard_map/while/body/eval_jaxpr/ppermute | solution.py:21
  1359.7 34.1 %collective-permute-start.1 = (bf16[2,256,1280]{1,2,0:T(8,128)(2,1)}, bf16[2,256,1280]{1,2,0:T(8,128)(2,1)}, u32[]{:S(2)}, u32[]{:S(2)}) collective-permute-start(bf16[2,256,1280]{1,2,0:T(8,128)(2,1)} %copy.110), channel_id=1, source_target_pairs={{0,2},{2,4},{4,6},{6,8},{8,10},{10,12},{12,14},{14,16},{16,18},{18... | collective-permute-start | bytes 3932168 | tf_op jit(solution)/shard_map/while/body/eval_jaxpr/ppermute | solution.py:21
  1414.4 231.7 %reduce-scatter.7.cloned.1.call-start = ((), (), s32[]{:S(2)}) async-start(), calls=%async_computation.5 | async-start | bytes 491520
  1426.5 414.4 %all-reduce.5.cloned.1.call-start = ((), (), s32[]{:S(2)}) async-start(), calls=%async_computation.4 | async-start | bytes 19660800 | tf_op jit(solution)/shard_map/psum | solution.py:290
  (89 other events, 794.7 us)
Sparse Core Ops, SparseCore 0:
  22.3 234.2 all-gather.1
  1414.5 216.1 reduce-scatter.4
  1633.7 12.3 reduce-scatter.6
  1649.7 191.1 all-reduce.4
where the time goes:
time: 1890 us; the launch traced here: 1870 us
  waiting for transfers between devices  1320 us (70%)
  matrix products  220 us (12%)
  local copies, waits for them, and re-layouts  134 us (7%)
  other arithmetic  126 us (7%)
  blocking collectives  50.8 us (3%)
    ppermute x47, waiting for transfers between devices, from_behind(): return lax.ppermute(value, axis, pairs)  742 us
    all_gather x1, waiting for transfers between devices, local(): lax.all_gather(matrices, 'fsdp', axis=1, tiled=True)  221 us
    reduce_scatter x1, waiting for transfers between devices, local(): lax.psum_scatter(grad_mats.astype(jnp.bfloat16), 'fsdp', scatter_dimensio...  204 us
    psum x1, waiting for transfers between devices, local(): lax.psum(owned_mats.astype(jnp.bfloat16), 'ctx').astype(jnp.float32)  157 us
    while x142, local copies, waits for them, and re-layouts  77.3 us
    dot_general x16, matrix products, attend_back(): jnp.einsum('hqk,khd->qhd', score_grad, key_heads, preferred_element_type=...  48.8 us
    convert_element_type x16, other arithmetic, back_step(): from_behind(kv_grad.astype(jnp.bfloat16), 'ctx', 1).astype(kv_grad.dtype)  48.2 us
    dot_general x16, matrix products, attend_back(): jnp.einsum('qhd,khd->hqk', out_grad, value_heads, preferred_element_type=...  44.6 us
  transfers between devices with their start and end apart: 51, of which 51 were waited for; matrix products, arithmetic and copies ran while one was open for 7% of the time, Pallas kernels for 0%

commit v1 on v0

v1 whole, which is shorter than its diff:
```python
import functools
import math

import jax
import jax.numpy as jnp
from jax import lax
from jax.experimental import pallas as pl
from jax.experimental.pallas import tpu as pltpu
from jax.sharding import PartitionSpec as P

H = 16
HD = 80
BLK = 128
D = 1280
EPS = 1e-06
LOG2E = 1.442695041
NEG = -1e30
MESH = pl.DeviceIdType.MESH
F32 = jnp.float32
BF16 = jnp.bfloat16
VMEM = pltpu.VMEM
MIB = 1 << 20

NN = (((1,), (0,)), ((), ()))
NT = (((1,), (1,)), ((), ()))
TN = (((0,), (0,)), ((), ()))


def dot(left, right, dims=NN):
    return lax.dot_general(left, right, dims, preferred_element_type=F32)


def al(value, multiple):
    return pl.multiple_of(value, multiple)


def in_vmem():
    return pl.BlockSpec(memory_space=pltpu.VMEM)


def in_smem():
    return pl.BlockSpec(memory_space=pltpu.SMEM)


def in_any():
    return pl.BlockSpec(memory_space=pl.ANY)


def gather_kernel(
    n, nf, x_ref, wh_ref, vec_ref, wo_ref, w1_ref, w2_ref,
    a_out, qkv_out, mats_out, vecs_out,
    abuf, whbuf, wht, vecbuf, stage, wcast,
    ag_send, ag_recv, wh_send, wh_recv, vec_send, vec_recv,
    ld_sem, own_sem, mx_send, mx_recv, ms_send, ms_recv, a_sem,
):
    c = lax.axis_index("ctx")
    f = lax.axis_index("fsdp")
    rows = wh_ref.shape[0]
    part = rows // 2
    zlen = n // 4
    z, y, core = c // 4, (c // 2) % 2, c % 2

    def idx(zz, yy, cc):
        return (zz * 2 + yy) * 2 + cc

    up, down = idx(z + 1, y, core), idx(z - 1, y, core)
    ypeer, twin = idx(z, 1 - y, core), idx(z, y, 1 - core)
    has_up, has_down = z < zlen - 1, z > 0
    targets = (up, down, ypeer, twin)
    guards = (has_up, has_down, None, None)
    fpeers = [(f + s) % nf for s in range(1, nf)]

    barrier = pltpu.get_barrier_semaphore()
    for target, guard in zip(targets, guards):
        def greet(target=target):
            pl.semaphore_signal(barrier, inc=1, device_id=(target, f), device_id_type=MESH)
        if guard is None:
            greet()
        else:
            pl.when(guard)(greet)
    for peer in fpeers:
        pl.semaphore_signal(barrier, inc=1, device_id=(c, peer), device_id_type=MESH)
    pl.semaphore_wait(barrier, 1 + nf + jnp.minimum(z, 1) + jnp.minimum(zlen - 1 - z, 1))

    def ag_copy(way, origin, i):
        return pltpu.make_async_remote_copy(
            src_ref=abuf.at[origin, i], dst_ref=abuf.at[origin, i],
            send_sem=ag_send.at[way, origin, i], recv_sem=ag_recv.at[origin, i],
            device_id=(targets[way], f), device_id_type=MESH,
        )

    def send(way, origin, i, guard=None):
        guards_here = [g for g in (guards[way], guard) if g is not None]
        def go():
            ag_copy(way, origin, i).start()
        if guards_here:
            pl.when(functools.reduce(jnp.logical_and, guards_here))(go)
        else:
            go()

    def arrive(origin, i):
        ag_copy(3, origin, i).wait_recv()

    for i in range(2):
        x = x_ref[pl.ds(i * BLK, BLK), :].astype(F32)
        scale = lax.rsqrt(jnp.mean(x * x, axis=-1, keepdims=True) + EPS)
        abuf[c, i] = (x * scale).astype(BF16)
        for way in range(4):
            send(way, c, i)

    def wh_copy(s, peer):
        return pltpu.make_async_remote_copy(
            src_ref=wh_ref, dst_ref=whbuf.at[pl.ds(al(f * rows, 16), rows)],
            send_sem=wh_send.at[s], recv_sem=wh_recv.at[s],
            device_id=(c, peer), device_id_type=MESH,
        )

    def vec_copy(s, peer):
        return pltpu.make_async_remote_copy(
            src_ref=vec_ref, dst_ref=vecbuf.at[f],
            send_sem=vec_send.at[s], recv_sem=vec_recv.at[s],
            device_id=(c, peer), device_id_type=MESH,
        )

    for s, peer in enumerate(fpeers):
        wh_copy(s, peer).start()
        vec_copy(s, peer).start()
    whbuf[pl.ds(al(f * rows, 16), rows), :] = wh_ref[...]
    vecbuf[f] = vec_ref[...]

    shards = (wo_ref, w1_ref, w2_ref)
    steps = [(m, h) for h in range(2) for m in range(3)]

    def half_of(h):
        return (core + h) % 2

    def load(step):
        m, h = steps[step]
        return pltpu.make_async_copy(
            shards[m].at[pl.ds(al(half_of(h) * part, 16), part)],
            stage.at[step % 2], ld_sem.at[step % 2],
        )

    def mx_copy(m, s, peer, source):
        return pltpu.make_async_remote_copy(
            src_ref=wcast.at[m, pl.ds(al(core * part, 16), part)],
            dst_ref=mats_out.at[m, pl.ds(al(source * rows + core * part, 16), part)],
            send_sem=mx_send.at[m, s], recv_sem=mx_recv.at[m, s],
            device_id=(c, peer), device_id_type=MESH,
        )

    def own_copy(m):
        return pltpu.make_async_copy(
            wcast.at[m], mats_out.at[m, pl.ds(al(f * rows, 16), rows)], own_sem.at[m]
        )

    load(0).start()
    for step, (m, h) in enumerate(steps):
        if step + 1 < len(steps):
            load(step + 1).start()
        load(step).wait()
        chunk = part // 4 if part % 64 == 0 else part
        @pl.loop(0, part // chunk)
        def _(t, m=m, h=h, step=step):
            wcast[m, pl.ds(al(half_of(h) * part + t * chunk, 16), chunk), :] = stage[
                step % 2, pl.ds(al(t * chunk, 16), chunk), :
            ].astype(BF16)
        if h == 0:
            for s, peer in enumerate(fpeers):
                mx_copy(m, s, peer, f).start()
        else:
            own_copy(m).start()

    for s, peer in enumerate(fpeers):
        wh_copy(s, peer).wait_recv()
        vec_copy(s, peer).wait_recv()
    wht[...] = whbuf[...].astype(F32).T.astype(BF16)
    vecs_out[...] = vecbuf[...]

    def a_copy(origin):
        return pltpu.make_async_copy(abuf.at[origin], a_out.at[origin], a_sem.at[origin])

    def project(origin):
        block = abuf[origin].reshape(2 * BLK, D)
        qkv_out[origin] = dot(wht[: 3 * HD, :], block, NT)
        a_copy(origin).start()

    def level(k):
        if k == 0:
            return [(z, None)]
        return [(z + k, z + k < zlen), (z - k, z - k >= 0)]

    def when(guard, body):
        if guard is None:
            body()
        else:
            pl.when(guard)(body)

    def pair_arrivals(k, i):
        for zz, guard in level(k):
            def body(zz=zz):
                origin = idx(zz, 1 - y, core)
                arrive(origin, i)
                send(3, origin, i)
            when(guard, body)

    def compute(k):
        for zz, guard in level(k):
            def body(zz=zz):
                for yy in (y, 1 - y):
                    for i in range(2):
                        arrive(idx(zz, yy, 1 - core), i)
                @pl.loop(0, 4)
                def _(t):
                    project(zz * 4 + t)
            when(guard, body)

    def ms_copy(m, s, source):
        where = pl.ds(al(source * rows + core * part, 16), part)
        return pltpu.make_async_remote_copy(
            src_ref=mats_out.at[m, where], dst_ref=mats_out.at[m, where],
            send_sem=ms_send.at[m, s], recv_sem=ms_recv.at[m, s],
            device_id=(twin, f), device_id_type=MESH,
        )

    def pass_matrix(m):
        for s, peer in enumerate(fpeers):
            source = (f + nf - 1 - s) % nf
            mx_copy(m, s, peer, source).wait_recv()
            ms_copy(m, s, source).start()

    for k in range(1, zlen):
        for i in range(2):
            for sign, (zz, guard) in zip((1, -1), level(k)):
                def body(zz=zz, sign=sign):
                    origin = idx(zz, y, core)
                    arrive(origin, i)
                    send(1 if sign == 1 else 0, origin, i)
                    send(2, origin, i)
                    send(3, origin, i)
                when(guard, body)
            pair_arrivals(k - 1, i)
        compute(k - 1)
        if k == 2:
            pass_matrix(0)
    for i in range(2):
        pair_arrivals(zlen - 1, i)
    pass_matrix(1)
    compute(zlen - 1)
    pass_matrix(2)

    for m in range(3):
        own_copy(m).wait()
        for s, peer in enumerate(fpeers):
            source = (f + nf - 1 - s) % nf
            mx_copy(m, s, peer, f).wait_send()
            ms_copy(m, s, source).wait_send()
            other = pl.ds(al(source * rows + (1 - core) * part, 16), part)
            pltpu.make_async_remote_copy(
                src_ref=mats_out.at[m, other], dst_ref=mats_out.at[m, other],
                send_sem=ms_send.at[m, s], recv_sem=ms_recv.at[m, s],
                device_id=(twin, f), device_id_type=MESH,
            ).wait_recv()
    for s, peer in enumerate(fpeers):
        wh_copy(s, peer).wait_send()
        vec_copy(s, peer).wait_send()
    for i in range(2):
        for way in range(4):
            when(guards[way], lambda way=way, i=i: ag_copy(way, c, i).wait_send())
        for k in range(zlen):
            for sign, (zz, guard) in zip((1, -1), level(k)):
                def body(zz=zz, sign=sign, k=k, i=i):
                    if k:
                        origin = idx(zz, y, core)
                        back = 1 if sign == 1 else 0
                        when(guards[back], lambda: ag_copy(back, origin, i).wait_send())
                        ag_copy(2, origin, i).wait_send()
                        ag_copy(3, origin, i).wait_send()
                    ag_copy(3, idx(zz, 1 - y, core), i).wait_send()
                when(guard, body)
    @pl.loop(0, n)
    def _(o):
        a_copy(o).wait()


def gather(n, nf, x, wh, vec, wo, w1, w2):
    rows = wh.shape[0]
    dma = pltpu.SemaphoreType.DMA
    peers = max(nf - 1, 1)
    return pl.pallas_call(
        functools.partial(gather_kernel, n, nf),
        out_shape=(
            jax.ShapeDtypeStruct((n, 2, BLK, D), BF16),
            jax.ShapeDtypeStruct((n, 3 * HD, 2 * BLK), F32),
            jax.ShapeDtypeStruct((3, nf * rows, D), BF16),
            jax.ShapeDtypeStruct((nf,) + vec.shape, F32),
        ),
        in_specs=[in_vmem(), in_vmem(), in_vmem(), in_any(), in_any(), in_any()],
        out_specs=(in_any(), in_vmem(), in_any(), in_vmem()),
        scratch_shapes=[
            VMEM((n, 2, BLK, D), BF16),
            VMEM((nf * rows, 256), BF16),
            VMEM((256, nf * rows), BF16),
            VMEM((nf,) + vec.shape, F32),
            VMEM((2, rows // 2, D), F32),
            VMEM((3, rows, D), BF16),
            dma((4, n, 2)), dma((n, 2)), dma((peers,)), dma((peers,)), dma((peers,)), dma((peers,)),
            dma((2,)), dma((3,)), dma((3, peers)), dma((3, peers)), dma((3, peers)), dma((3, peers)),
            dma((n,)),
        ],
        compiler_params=pltpu.CompilerParams(
            collective_id=0, has_side_effects=True, vmem_limit_bytes=56 * MIB
        ),
        name="gather_tokens",
    )(x, wh, vec, wo, w1, w2)


def swap_kernel(n, src, dst, send_sem, recv_sem, own_sem):
    c = lax.axis_index("ctx")
    f = lax.axis_index("fsdp")
    barrier = pltpu.get_barrier_semaphore()
    for s in range(1, n):
        pl.semaphore_signal(barrier, inc=1, device_id=((c + s) % n, f), device_id_type=MESH)
    pl.semaphore_wait(barrier, n - 1)

    def copy(s, block):
        return pltpu.make_async_remote_copy(
            src_ref=src.at[(c + s) % n], dst_ref=dst.at[block],
            send_sem=send_sem.at[s], recv_sem=recv_sem.at[s],
            device_id=((c + s) % n, f), device_id_type=MESH,
        )

    for s in range(1, n):
        copy(s, c).start()
    own = pltpu.make_async_copy(src.at[c], dst.at[c], own_sem)
    own.start()
    own.wait()
    for s in range(1, n):
        copy(s, (c + n - s) % n).wait_recv()
    for s in range(1, n):
        copy(s, c).wait_send()


def swap(n, blocks, collective):
    dma = pltpu.SemaphoreType.DMA
    return pl.pallas_call(
        functools.partial(swap_kernel, n),
        out_shape=jax.ShapeDtypeStruct(blocks.shape, blocks.dtype),
        in_specs=[in_vmem()],
        out_specs=in_vmem(),
        scratch_shapes=[dma((n,)), dma((n,)), dma],
        compiler_params=pltpu.CompilerParams(
            collective_id=collective, has_side_effects=True, vmem_limit_bytes=32 * MIB
        ),
        name=f"swap_{collective}",
    )(blocks)


def seq_start(ends, base, token):
    start = jnp.zeros_like(token)
    for e in ends:
        start = jnp.where(e - base <= token, jnp.maximum(start, e - base), start)
    return start


def read_ends(lengths_ref):
    ends, total = [], jnp.int32(0)
    for i in range(lengths_ref.shape[1]):
        total = total + lengths_ref[0, i]
        ends.append(total)
    return ends


def pad_rows(block):
    return jnp.concatenate([block, jnp.zeros((BLK - HD, block.shape[1]), block.dtype)], axis=0)


class Layout:
    def __init__(self, n, total_blocks):
        self.n = n
        self.hpd = 2 * H // n
        self.half_blocks = total_blocks // 2
        self.size = self.half_blocks * BLK
        self.rows = self.hpd * self.size
        self.tile = 512

    def half(self, i):
        return i if self.hpd == 2 else lax.axis_index("ctx") % 2

    def nat(self, deal_ref, d, i):
        half = self.half(i)
        block = deal_ref[2 * d + half]
        if self.hpd == 1:
            block = block - half * self.half_blocks
        return al(block * BLK, BLK)

    def base(self, unit):
        return self.half(unit) * self.size if self.hpd == 1 else unit * self.size


def fwd_kernel(
    lay, deal_ref, len_ref, qkv_ref, bias_ref, c_ref,
    ot_out, qraw, qst, kt, vt, kn, ot, lse,
    m_ref, l_ref, acc_ref,
):
    tile = lay.tile

    @pl.loop(0, lay.n)
    def _(d):
        for i in range(lay.hpd):
            nat = lay.nat(deal_ref, d, i)
            cols = pl.ds(nat, BLK)
            half = lay.half(i)
            src = pl.ds(half * BLK if lay.hpd == 2 else al(half * BLK, BLK), BLK)
            block = qkv_ref[d, :, src] + bias_ref[...]
            qr, kr, vr = block[:HD], block[HD : 2 * HD], block[2 * HD :]
            qraw[:, cols] = qr
            qst[:, cols] = pad_rows(qr * c_ref[...]).astype(BF16)
            kt[:, cols] = kr.astype(BF16)
            vt[:, cols] = vr.astype(BF16)
            kn[cols, :] = pad_rows(kr).T.astype(BF16)

    ends = read_ends(len_ref)
    for unit in range(lay.hpd):
        base = lay.base(unit)
        row0 = unit * lay.size

        @pl.loop(0, lay.size // tile)
        def _(qi):
            cols = pl.ds(al(row0 + qi * tile, tile), tile)
            t_row = qi * tile + lax.broadcasted_iota(jnp.int32, (1, tile), 1)
            start = seq_start(ends, base, t_row)
            low = seq_start(ends, base, qi * tile) // tile
            m_ref[...] = jnp.full_like(m_ref, NEG)
            l_ref[...] = jnp.zeros_like(l_ref)
            acc_ref[...] = jnp.zeros_like(acc_ref)

            def visit(j, diagonal):
                keys = pl.ds(al(row0 + j * tile, tile), tile)
                s = dot(kn[keys, :], qst[:, cols])
                u = j * tile + lax.broadcasted_iota(jnp.int32, (tile, 1), 0)
                seen = u >= start
                if diagonal:
                    seen = seen & (u <= t_row)
                s = jnp.where(seen, s, NEG)
                m_old = m_ref[...]
                m_new = jnp.maximum(m_old, jnp.max(s, axis=0, keepdims=True))
                p = jnp.exp(s - m_new)
                shrink = jnp.exp(m_old - m_new)
                m_ref[...] = m_new
                l_ref[...] = l_ref[...] * shrink + jnp.sum(p, axis=0, keepdims=True)
                acc_ref[...] = acc_ref[...] * shrink + dot(vt[:, keys], p.astype(BF16))

            @pl.loop(low, qi)
            def _(j):
                visit(j, False)

            visit(qi, True)
            ot[:, cols] = acc_ref[...] / l_ref[...]
            lse[:, cols] = m_ref[...] + jnp.log(l_ref[...])

    @pl.loop(0, lay.n)
    def _(d):
        for i in range(lay.hpd):
            ot_out[d, i] = ot[:, pl.ds(lay.nat(deal_ref, d, i), BLK)].astype(BF16)


def attend(lay, deal, lengths, qkv, bias, factor):
    rows = lay.rows
    return pl.pallas_call(
        functools.partial(fwd_kernel, lay),
        out_shape=(
            jax.ShapeDtypeStruct((lay.n, lay.hpd, HD, BLK), BF16),
            jax.ShapeDtypeStruct((HD, rows), F32),
            jax.ShapeDtypeStruct((BLK, rows), BF16),
            jax.ShapeDtypeStruct((HD, rows), BF16),
            jax.ShapeDtypeStruct((HD, rows), BF16),
            jax.ShapeDtypeStruct((rows, BLK), BF16),
            jax.ShapeDtypeStruct((HD, rows), F32),
            jax.ShapeDtypeStruct((1, rows), F32),
        ),
        in_specs=[in_smem(), in_smem()] + [in_vmem()] * 3,
        out_specs=tuple([in_vmem()] * 8),
        scratch_shapes=[
            VMEM((1, lay.tile), F32), VMEM((1, lay.tile), F32), VMEM((HD, lay.tile), F32),
        ],
        compiler_params=pltpu.CompilerParams(vmem_limit_bytes=56 * MIB),
        name="attend",
    )(deal, lengths, qkv, bias, factor)


def bwd_kernel(
    lay, deal_ref, len_ref, dot_ref, qraw, qst, kt, vt, kn, ot, lse, c_ref, a_ref,
    msg_out, small_out, dw_out,
    qn, vn, don, dost, delta, dk, dv, dqt,
):
    tile = lay.tile

    @pl.loop(0, lay.n)
    def _(d):
        for i in range(lay.hpd):
            cols = pl.ds(lay.nat(deal_ref, d, i), BLK)
            block = dot_ref[d, i].astype(F32)
            delta[:, cols] = jnp.sum(block * ot[:, cols], axis=0, keepdims=True)
            block = pad_rows(block)
            dost[:, cols] = block.astype(BF16)
            don[cols, :] = block.T.astype(BF16)

    @pl.loop(0, lay.rows // BLK)
    def _(t):
        cols = pl.ds(al(t * BLK, BLK), BLK)
        qn[cols, :] = qst[:, cols].astype(F32).T.astype(BF16)
        vn[cols, :] = pad_rows(vt[:, cols].astype(F32)).T.astype(BF16)
        dk[cols, :] = jnp.zeros((BLK, BLK), F32)
        dv[cols, :] = jnp.zeros((BLK, BLK), F32)

    ends = read_ends(len_ref)
    for unit in range(lay.hpd):
        base = lay.base(unit)
        row0 = unit * lay.size

        @pl.loop(0, lay.size // tile)
        def _(qi):
            cols = pl.ds(al(row0 + qi * tile, tile), tile)
            t_row = qi * tile + lax.broadcasted_iota(jnp.int32, (1, tile), 1)
            start = seq_start(ends, base, t_row)
            low = seq_start(ends, base, qi * tile) // tile
            dqt[:, cols] = jnp.zeros((HD, tile), F32)

            def visit(j, diagonal):
                keys = pl.ds(al(row0 + j * tile, tile), tile)
                s = dot(kn[keys, :], qst[:, cols])
                u = j * tile + lax.broadcasted_iota(jnp.int32, (tile, 1), 0)
                seen = u >= start
                if diagonal:
                    seen = seen & (u <= t_row)
                p = jnp.exp(jnp.where(seen, s - lse[:, cols], NEG))
                dp = dot(vn[keys, :], dost[:, cols])
                ds = (p * (dp - delta[:, cols])).astype(BF16)
                dv[keys, :] += dot(p.astype(BF16), don[cols, :])
                dk[keys, :] += dot(ds, qn[cols, :])
                dqt[:, cols] += dot(kt[:, keys], ds)

            @pl.loop(low, qi)
            def _(j):
                visit(j, False)

            visit(qi, True)

    small_out[...] = jnp.zeros_like(small_out)

    @pl.loop(0, lay.n)
    def _(d):
        for i in range(lay.hpd):
            cols = pl.ds(lay.nat(deal_ref, d, i), BLK)
            dqs = dqt[:, cols]
            dq = (dqs * c_ref[...]).astype(BF16)
            dkt = dk[cols, :].T[:HD].astype(BF16)
            dvt = dv[cols, :].T[:HD].astype(BF16)
            msg_out[d, 0, i] = dq
            msg_out[d, 1, i] = dkt
            msg_out[d, 2, i] = dvt
            small_out[0] += dqs * qraw[:, cols]
            small_out[1] += dq.astype(F32)
            small_out[2] += dvt.astype(F32)

    dw_out[...] = jnp.zeros_like(dw_out)

    @pl.loop(0, lay.n)
    def _(d):
        if lay.hpd == 2:
            left = jnp.concatenate(
                [msg_out[d, :, 0].reshape(3 * HD, BLK), msg_out[d, :, 1].reshape(3 * HD, BLK)], axis=1
            )
            right = a_ref[d].reshape(2 * BLK, D)
        else:
            left = msg_out[d, :, 0].reshape(3 * HD, BLK)
            right = a_ref[d, lay.half(0)]
        dw_out[...] += dot(left, right)


def attend_back(lay, deal, lengths, grad_t, kept, factor, tokens):
    rows = lay.rows
    return pl.pallas_call(
        functools.partial(bwd_kernel, lay),
        out_shape=(
            jax.ShapeDtypeStruct((lay.n, 3, lay.hpd, HD, BLK), BF16),
            jax.ShapeDtypeStruct((3, HD, BLK), F32),
            jax.ShapeDtypeStruct((3 * HD, D), F32),
        ),
        in_specs=[in_smem(), in_smem()] + [in_vmem()] * 10,
        out_specs=tuple([in_vmem()] * 3),
        scratch_shapes=[
            VMEM((rows, BLK), BF16), VMEM((rows, BLK), BF16), VMEM((rows, BLK), BF16),
            VMEM((BLK, rows), BF16), VMEM((1, rows), F32),
            VMEM((rows, BLK), F32), VMEM((rows, BLK), F32), VMEM((HD, rows), F32),
        ],
        compiler_params=pltpu.CompilerParams(vmem_limit_bytes=58 * MIB),
        name="attend_back",
    )(deal, lengths, grad_t, *kept, factor, tokens)


WIDE = 256


def over_columns(body):
    @pl.loop(0, D // WIDE)
    def _(j):
        body(pl.ds(al(j * WIDE, WIDE), WIDE))


def ffn_kernel(
    x_ref, cot_ref, ot_ref, g2_ref, mats_ref,
    out_ref, dh_ref, gt_ref, dwo_ref, dw1_ref, dw2_ref, dg2_ref,
    ot, o_rows, hidden, nh, b, up, z, du, db, gb, wide,
):
    tok = x_ref.shape[0]
    wo, w1, w2 = mats_ref.at[0], mats_ref.at[1], mats_ref.at[2]
    for i in range(2):
        for h in range(H):
            ot[pl.ds(h * HD, HD), pl.ds(i * BLK, BLK)] = ot_ref[h, i]
    @pl.loop(0, D // WIDE)
    def _(j):
        sl = pl.ds(al(j * WIDE, WIDE), WIDE)
        o_rows[:, sl] = ot[sl, :].astype(F32).T.astype(BF16)

    def body(sl):
        hidden[:, sl] = x_ref[:, sl].astype(F32) + dot(o_rows[...], wo[:, sl])
    over_columns(body)
    hid = hidden[...]
    r2 = lax.rsqrt(jnp.mean(hid * hid, axis=-1, keepdims=True) + EPS)
    nh[...] = hid * r2
    b[...] = (nh[...] * g2_ref[...]).astype(BF16)

    def body(sl):
        u = dot(b[...], w1[:, sl])
        up[:, sl] = u
        z[:, sl] = (u * jax.nn.sigmoid(u)).astype(BF16)
    over_columns(body)

    def body(sl):
        out_ref[:, sl] = (hidden[:, sl] + dot(z[...], w2[:, sl])).astype(BF16)
        dz = dot(cot_ref[...], w2[sl, :], NT)
        u = up[:, sl]
        sig = jax.nn.sigmoid(u)
        du[:, sl] = (dz * sig * (1.0 + u * (1.0 - sig))).astype(BF16)
    over_columns(body)

    def body(sl):
        g = dot(du[...], w1[sl, :], NT)
        db[:, sl] = g * g2_ref[:, sl]
        dg2_ref[:, sl] = jnp.sum(g * nh[:, sl], axis=0, keepdims=True)
    over_columns(body)
    scaled = db[...]
    mean = jnp.mean(scaled * nh[...], axis=-1, keepdims=True)
    dh = cot_ref[...].astype(F32) + r2 * (scaled - nh[...] * mean)
    dh_ref[...] = dh
    gb[...] = dh.astype(BF16)

    @pl.loop(0, D // WIDE)
    def _(j):
        sl = pl.ds(al(j * WIDE, WIDE), WIDE)
        wide[sl, :] = dot(wo[sl, :], gb[...], NT).astype(BF16)
    for i in range(2):
        for h in range(H):
            gt_ref[h, i] = wide[pl.ds(h * HD, HD), pl.ds(i * BLK, BLK)]

    def body(sl):
        dwo_ref[sl, :] = dot(ot[sl, :], gb[...]).astype(BF16)
        dw1_ref[sl, :] = dot(b[:, sl], du[...], TN).astype(BF16)
        dw2_ref[sl, :] = dot(z[:, sl], cot_ref[...], TN).astype(BF16)
    over_columns(body)


def ffn(x, cot, ot, g2, mats):
    tok = x.shape[0]
    grad = jax.ShapeDtypeStruct((D, D), BF16)
    return pl.pallas_call(
        ffn_kernel,
        out_shape=(
            jax.ShapeDtypeStruct((tok, D), BF16),
            jax.ShapeDtypeStruct((tok, D), F32),
            jax.ShapeDtypeStruct((H, 2, HD, BLK), BF16),
            grad, grad, grad,
            jax.ShapeDtypeStruct((1, D), F32),
        ),
        in_specs=[in_vmem()] * 5,
        out_specs=tuple([in_vmem()] * 7),
        scratch_shapes=[
            VMEM((D, tok), BF16), VMEM((tok, D), BF16), VMEM((tok, D), F32), VMEM((tok, D), F32),
            VMEM((tok, D), BF16), VMEM((tok, D), F32), VMEM((tok, D), BF16), VMEM((tok, D), BF16),
            VMEM((tok, D), F32), VMEM((tok, D), BF16), VMEM((D, tok), BF16),
        ],
        compiler_params=pltpu.CompilerParams(vmem_limit_bytes=56 * MIB),
        name="feed_forward",
    )(x, cot, ot, g2, mats)


def input_grad_kernel(x_ref, dh_ref, msg_ref, g1_ref, wq, wk, wv, out_ref, dg1_ref, wide, dat):
    mats = (wq, wk, wv)
    for p in range(3):
        for i in range(2):
            for h in range(H):
                wide[p, pl.ds(h * HD, HD), pl.ds(i * BLK, BLK)] = msg_ref[h, p, i]

    @pl.loop(0, D // WIDE)
    def _(j):
        sl = pl.ds(al(j * WIDE, WIDE), WIDE)
        total = dot(wq[sl, :], wide[0]) + dot(wk[sl, :], wide[1]) + dot(wv[sl, :], wide[2])
        dat[:, sl] = total.T
    x = x_ref[...].astype(F32)
    r1 = lax.rsqrt(jnp.mean(x * x, axis=-1, keepdims=True) + EPS)
    na = x * r1
    da = dat[...]
    dg1_ref[...] = jnp.sum(da * na, axis=0, keepdims=True)
    scaled = da * g1_ref[...]
    mean = jnp.mean(scaled * na, axis=-1, keepdims=True)
    out_ref[...] = dh_ref[...] + r1 * (scaled - na * mean)


def input_grad(x, dh, msg, g1, wq, wk, wv):
    tok = x.shape[0]
    return pl.pallas_call(
        input_grad_kernel,
        out_shape=(
            jax.ShapeDtypeStruct((tok, D), F32),
            jax.ShapeDtypeStruct((1, D), F32),
        ),
        in_specs=[in_vmem()] * 7,
        out_specs=(in_vmem(), in_vmem()),
        scratch_shapes=[VMEM((3, D, tok), BF16), VMEM((tok, D), F32)],
        compiler_params=pltpu.CompilerParams(vmem_limit_bytes=48 * MIB),
        name="input_grad",
    )(x, dh, msg, g1, wq, wk, wv)


def local(
    n, nf, tokens, cotangent, lengths, deal, gain_attn, query_weight, query_bias, key_weight,
    value_weight, value_bias, query_scale, proj_weight, gain_ffn, up_weight, down_weight,
):
    c = lax.axis_index("ctx")
    f = lax.axis_index("fsdp")
    lay = Layout(n, deal.shape[0])
    head = c * lay.hpd // 2
    rows = query_weight.shape[0]
    x, cot = tokens[0], cotangent[0]

    def low(v):
        return v.astype(BF16).astype(F32)

    g1_own = low(gain_attn)
    slices = [
        lax.dynamic_slice(w, (0, head * HD), (rows, HD)) for w in (query_weight, key_weight, value_weight)
    ]
    wh = jnp.concatenate(slices, axis=1).astype(BF16).astype(F32) * g1_own[:, None]
    wh = jnp.pad(wh, ((0, 0), (0, 256 - 3 * HD))).astype(BF16)
    vec = jnp.stack([g1_own, low(query_bias), low(value_bias), low(gain_ffn)])
    vec = jnp.concatenate([vec, jnp.pad(low(query_scale), (0, rows - query_scale.shape[0]))[None]])
    vec = jnp.pad(vec, ((0, 3), (0, -rows % 128)))

    a_all, qkv, mats, vecs = gather(n, nf, x, wh, vec, proj_weight, up_weight, down_weight)
    whole = jnp.swapaxes(vecs[:, :5, :rows], 0, 1).reshape(5, nf * rows)
    g1, bq, bv, g2 = whole[0], whole[1], whole[2], whole[3]
    q_param = vecs[:, 4, : query_scale.shape[0]].reshape(HD)
    factor = jnp.log(1.0 + jnp.exp(q_param)) * (LOG2E / math.sqrt(HD))
    bias = jnp.concatenate([
        lax.dynamic_slice(bq, (head * HD,), (HD,)), jnp.zeros((HD,), F32),
        lax.dynamic_slice(bv, (head * HD,), (HD,)),
    ])
    bias = jnp.broadcast_to(bias[:, None], (3 * HD, BLK))
    factor_col = jnp.broadcast_to(factor[:, None], (HD, BLK))

    core = c % 2
    part = rows // 2
    pairs = [(i, i ^ 1) for i in range(n)]
    stacked = jnp.stack([query_weight, key_weight, value_weight])
    mine = lax.dynamic_slice(stacked, (0, core * part, 0), (3, part, D)).astype(BF16)
    mine = lax.all_gather(mine, "fsdp", axis=1)
    other = lax.ppermute(mine, "ctx", pairs)
    first = jnp.where(core == 0, mine, other)
    second = jnp.where(core == 0, other, mine)
    proj = jnp.concatenate([first, second], axis=2).reshape(3, nf * rows, D)

    ot, *kept = attend(lay, deal, lengths, qkv, bias, factor_col)
    ot = swap(n, ot, 1).reshape(H, 2, HD, BLK)
    layer_out, dh, gt, dwo, dw1, dw2, dg2 = ffn(x, cot, ot, g2[None], mats)

    grads = lax.psum_scatter(jnp.stack([dwo, dw1, dw2]), "fsdp", scatter_dimension=1, tiled=True)
    grads = lax.psum(grads, "ctx").astype(F32)

    gt = swap(n, gt.reshape(n, lay.hpd, HD, BLK), 2)
    msg, small, dw = attend_back(lay, deal, lengths, gt, kept, factor_col, a_all)
    back = swap(n, msg, 3)
    if lay.hpd == 1:
        back = back.reshape(H, 2, 3, HD, BLK).transpose(0, 2, 1, 3, 4)
    grad_x, dg1 = input_grad(x, dh, back, g1[None], proj[0], proj[1], proj[2])

    dw = lax.psum_scatter(dw.astype(BF16), "fsdp", scatter_dimension=1, tiled=True)
    dw = lax.all_gather(dw, "ctx").astype(F32)
    dw = dw.reshape(H, 2 // lay.hpd, 3, HD, rows).sum(axis=1)
    dw = dw.transpose(1, 0, 2, 3).reshape(3, D, rows)
    dw = dw.transpose(0, 2, 1) * g1_own[None, :, None]

    small = jnp.sum(small, axis=-1)
    bias_part = jnp.zeros((2, H, HD), F32)
    bias_part = lax.dynamic_update_slice(bias_part, small[1:][:, None], (0, head, 0)).reshape(2, D)
    vectors = jnp.concatenate([dg1.reshape(D), dg2.reshape(D), bias_part.reshape(2 * D), small[0]])
    vectors = lax.psum(vectors, ("ctx", "fsdp"))

    def own(v):
        size = v.shape[0] // nf
        return lax.dynamic_slice(v, (f * size,), (size,))

    grad_scale = vectors[4 * D :] * jax.nn.sigmoid(q_param) * (LOG2E / math.sqrt(HD))
    return (
        layer_out[None],
        grad_x[None],
        own(vectors[:D]),
        dw[0],
        own(vectors[2 * D : 3 * D]),
        dw[1],
        dw[2],
        own(vectors[3 * D : 4 * D]),
        own(grad_scale),
        grads[0],
        own(vectors[D : 2 * D]),
        grads[1],
        grads[2],
    )


def solution(mesh):
    whole, vector, matrix = P("fsdp", "ctx", None), P("fsdp"), P("fsdp", None)
    return jax.shard_map(
        functools.partial(local, mesh.shape["ctx"], mesh.shape["fsdp"]),
        mesh=mesh,
        in_specs=(
            whole, whole, matrix, P(), vector, matrix, vector, matrix, matrix, vector, vector,
            matrix, vector, matrix, matrix,
        ),
        out_specs=(
            whole, whole, vector, matrix, vector, matrix, matrix, vector, vector, matrix, vector,
            matrix, matrix,
        ),
        check_vma=False,
    )
```

time: 1890 us -> 613 us (0.32)
  waiting for transfers between devices: 1320 us -> 224 us
  Pallas kernels: 0 us -> 231 us
  matrix products: 220 us -> 0 us
  local copies, waits for them, and re-layouts: 134 us -> 44.5 us
  other arithmetic: 126 us -> 46.9 us
    ppermute x47 -> x1, waiting for transfers between devices: 742 us -> 0.01 us  [local(): other = lax.ppermute(mine, 'ctx', pairs)]
    pallas_call x0 -> x8, Pallas kernels: none -> 231 us  [the longest x1 72.9 us: gather(): pl.pallas_call(functools.partial(gather_kernel, n, nf), out_shape=(jax.Sh...]
    dot_general x130 -> x0, matrix products: 220 us -> none  [the longest x16 48.8 us: attend_back(): jnp.einsum('hqk,khd->qhd', score_grad, key_heads, preferred_element_type=...]
    reduce_scatter x1, waiting for transfers between devices: 204 us -> 0.92 us  [local(): lax.psum_scatter(jnp.stack([dwo, dw1, dw2]), 'fsdp', scatter_dimension=1,...]
    all_gather x1 -> x2, waiting for transfers between devices: 221 us -> 122 us  [the longest x1 65.2 us: local(): mine = lax.all_gather(mine, 'fsdp', axis=1)]
    while x143 -> x0, local copies, waits for them, and re-layouts: 78.8 us -> none
    convert_element_type x38 -> x5, other arithmetic: 84.9 us -> 10.7 us  [the longest x1 3.81 us: local(): lax.dynamic_slice(stacked, (0, core * part, 0), (3, part, D)).astype(BF16)]
    psum x1, waiting for transfers between devices: 157 us -> 93.8 us  [local(): grads = lax.psum(grads, 'ctx').astype(F32)]
  transfers between devices with their start and end apart: 51 -> 6, of which waited for: 51 -> 5; matrix products, arithmetic and copies ran while one was open for 7% -> 10% of each run, Pallas kernels for 0% -> 8%
where the time goes in v1:
time: 613 us; the launch traced here: 611 us
  Pallas kernels  231 us (38%)
  waiting for transfers between devices  224 us (37%)
  blocking collectives  49.8 us (8%)
  other arithmetic  46.9 us (8%)
  local copies, waits for them, and re-layouts  44.5 us (7%)
  between operations  14 us (2%)
    psum x1, waiting for transfers between devices, local(): grads = lax.psum(grads, 'ctx').astype(F32)  93.8 us
    pallas_call x1, Pallas kernels, gather(): pl.pallas_call(functools.partial(gather_kernel, n, nf), out_shape=(jax.Sh...  72.9 us
    pallas_call x3, Pallas kernels, swap(): pl.pallas_call(functools.partial(swap_kernel, n), out_shape=jax.ShapeDtyp...  70.9 us
    all_gather x1, waiting for transfers between devices, local(): mine = lax.all_gather(mine, 'fsdp', axis=1)  65.2 us
    all_gather x1, waiting for transfers between devices, local(): dw = lax.all_gather(dw, 'ctx').astype(F32)  56.5 us
    psum x1, blocking collectives, local(): vectors = lax.psum(vectors, ('ctx', 'fsdp'))  49.8 us
    pallas_call x1, Pallas kernels, attend_back(): pl.pallas_call(functools.partial(bwd_kernel, lay), out_shape=(jax.ShapeDt...  35.1 us
    pallas_call x1, Pallas kernels, ffn(): pl.pallas_call(ffn_kernel, out_shape=(jax.ShapeDtypeStruct((tok, D), BF16...  23.4 us
  transfers between devices with their start and end apart: 6, of which 5 were waited for; matrix products, arithmetic and copies ran while one was open for 10% of the time, Pallas kernels for 8%

profile of v1, /device:TPU:0, one launch (start us, length us, event | category | flops | bytes accessed | tf_op | source)
XLA Modules:
  0.0 610.7 jit_solution(6674778866844038114)
XLA Ops:
  7.2 0.7 convert_convert_fusion.3
  8.6 0.7 convert_convert_fusion.2
  9.3 0.7 convert_convert_fusion.1
  10.0 0.7 convert_convert_fusion
  10.7 1.2 dynamic-slice_convert_fusion.2
  11.9 1.5 dynamic-slice_convert_fusion
  13.7 0.8 pad.14.wh_ref
  15.1 72.9 %gather_tokens.1 = (bf16[16,2,128,1280]{3,2,1,0:T(8,128)(2,1)}, f32[16,240,256]{2,1,0:T(8,128)}, bf16[3,1280,1280]{2,1,0:T(8,128)(2,1)}, f32[2,8,640]{2,1,0:T(8,128)}) custom-call(bf16[256,1280]{1,0:T(8,128)(2,1)} %bitcast.44, bf16[640,256]{1,0:T(8,128)(2,1)} %pad.14.wh_ref, f32[8,640]{1,0:T(8,128)} %pad.16.vec_ref, f32[640,1280]{1,0:T(8,128)} %wo_ref.1, ...), custom_call_target="tpu_custom_call" | custom-call | tf_op jit(solution)/shard_map/gather_tokens/pallas_call | solution.py:290
  88.0 0.8 slice_bitcast_fusion.6
  88.7 0.7 divide_reduce_fusion
  90.4 0.8 broadcast_in_dim.38.bias_ref
  91.2 0.7 broadcast_in_dim.39.c_ref
  91.9 19.2 %attend.1 = (bf16[16,2,80,128]{3,2,1,0:T(8,128)(2,1)}, f32[80,4096]{1,0:T(8,128)}, bf16[128,4096]{1,0:T(8,128)(2,1)}, bf16[80,4096]{1,0:T(8,128)(2,1)}, bf16[80,...) custom-call(s32[32]{0:T(128)} %deal_ref.3, s32[1,8]{1,0:T(1,128)} %len_ref.3, ...), custom_call_target="tpu_custom_call" | custom-call | tf_op jit(solution)/shard_map/attend/pallas_call | solution.py:470
  111.1 1.1 copy-done.5
  112.2 15.3 %swap_1.1.ot_ref = bf16[16,2,80,128]{3,2,1,0:T(8,128)(2,1)S(1)} custom-call(bf16[16,2,80,128]{3,2,1,0:T(8,128)(2,1)S(1)} %copy-done.5), custom_call_target="tpu_custom_call" | custom-call | tf_op jit(solution)/shard_map/swap_1/pallas_call | solution.py:346
  127.6 0.8 copy-done.2
  128.4 23.4 %feed_forward.1 = (bf16[256,1280]{1,0:T(8,128)(2,1)}, f32[256,1280]{1,0:T(8,128)}, bf16[16,2,80,128]{3,2,1,0:T(8,128)(2,1)}, bf16[1280,1280]{1,0:T(8,128)(2,1)},...) custom-call(bf16[256,1280]{1,0:T(8,128)(2,1)} %bitcast.45, bf16[256,1280]{1,0:T(8,128)(2,1)} %bitcast.62, ...), custom_call_target="tpu_custom_call" | custom-call | tf_op jit(solution)/shard_map/feed_forward/pallas_call | solution.py:678
  151.8 1.1 copy-done.6
  152.9 18.8 %swap_2.1.dot_ref = bf16[16,2,80,128]{3,2,1,0:T(8,128)(2,1)S(1)} custom-call(bf16[16,2,80,128]{3,2,1,0:T(8,128)(2,1)S(1)} %copy-done.6), custom_call_target="tpu_custom_call" | custom-call | tf_op jit(solution)/shard_map/swap_2/pallas_call | solution.py:346
  171.6 0.8 copy-done.1
  172.5 35.1 %attend_back.1 = (bf16[16,3,2,80,128]{4,3,2,1,0:T(8,128)(2,1)}, f32[3,80,128]{2,1,0:T(8,128)}, f32[240,1280]{1,0:T(8,128)}) custom-call(s32[32]{0:T(128)} %deal_ref.3, s32[1,8]{1,0:T(1,128)} %len_ref.3, bf16[16,2,80,128]{3,2,1,0:T(8,128)(2,1)} %copy-done.1, f32[80,4096]{1,0:T(8,128)} %get-tuple-element.44.qraw, bf16[128,4096]{1,0:T(8,128)(2,1)} %get-tuple-element.45.qst, ...), custom_call_target="tpu_custom_call" | custom-call | tf_op jit(solution)/shard_map/attend_back/pallas_call | solution.py:584
  207.6 2.3 convert_element_type.51
  209.9 2.1 copy.43
  212.2 3.8 fusion.2
  216.0 9.5 %pad_maximum_fusion = bf16[3,1280,1280]{2,1,0:T(8,128)(2,1)} fusion(bf16[1,1280,1280]{2,1,0:T(8,128)(2,1)} %bitcast.60, bf16[1,1280,1280]{2,1,0:T(8,128)(2,1)} %bitcast.59, bf16[1,1280,1280]{2,1,0:T(8,128)(2,1)} %bitcast.58), kind=kLoop, calls=%fused_computation.7 | loop fusion | flops 9830400 | bytes 19660800 | tf_op jit(solution)/shard_map/stack | solution.py:788
  225.6 7.4 %reduce-scatter.7.cloned.1.call-done = bf16[640,240]{1,0:T(8,128)(2,1)} async-done(((bf16[1280,240]{1,0:T(8,128)(2,1)}), bf16[640,240]{1,0:T(8,128)(2,1)}) %reduce-scatter.7.cloned.1.call-update) | async-done | bytes 307216
  233.0 1.9 copy.44
  234.9 65.2 %all-gather.5.cloned.1.call-done = bf16[3,640,1280]{2,1,0:T(8,128)(2,1)} async-done(((bf16[3,320,1280]{2,1,0:T(8,128)(2,1)}), bf16[3,640,1280]{2,1,0:T(8,128)(2,1)}) %all-gather.5.cloned.1.call-update) | async-done | bytes 4915216 | tf_op jit(solution)/shard_map/all_gather | solution.py:778
  300.1 1.5 copy-done.3
  301.7 36.8 %swap_3.1.msg_ref = bf16[16,3,2,80,128]{4,3,2,1,0:T(8,128)(2,1)S(1)} custom-call(bf16[16,3,2,80,128]{4,3,2,1,0:T(8,128)(2,1)S(1)} %copy-done.3), custom_call_target="tpu_custom_call" | custom-call | tf_op jit(solution)/shard_map/swap_3/pallas_call | solution.py:346
  339.1 8.4 %broadcast_select_fusion = (bf16[3,2,320,1280]{3,2,1,0:T(8,128)(2,1)}, bf16[3,2,320,1280]{3,2,1,0:T(8,128)(2,1)}) fusion(bf16[3,2,320,1280]{3,2,1,0:T(8,128)(2,1)} %collective-permute-done, bf16[3,2,320,1280]{3,2,1,0:T(8,128)(2,1)} %bitcast.54, pred[]{:T(512)S(6)} %eq.6), kind=kLoop, calls=%fused_computation.13 | loop fusion | flops 4915200 | bytes 19660800 | tf_op jit(solution)/shard_map/jit(_where)/select_n | solution.py:781
  347.5 7.4 %pad_maximum_fusion.1 = (bf16[1,2,640,1280]{3,2,1,0:T(8,128)(2,1)}, bf16[1,2,640,1280]{3,2,1,0:T(8,128)(2,1)}, bf16[1,2,640,1280]{3,2,1,0:T(8,128)(2,1)}) fusion(bf16[3,2,320,1280]{3,2,1,0:T(8,128)(2,1)} %get-tuple-element.113, bf16[3,2,320,1280]{3,2,1,0:T(8,128)(2,1)} %get-tuple-element.114), kind=kLoop, calls=%fused_computation.23 | loop fusion | flops 19660800 | bytes 19660800 | tf_op jit(solution)/shard_map/concatenate | solution.py:782
  354.9 9.9 %input_grad.1 = (f32[256,1280]{1,0:T(8,128)}, f32[1,1280]{1,0:T(1,128)S(1)}) custom-call(bf16[256,1280]{1,0:T(8,128)(2,1)S(1)} %bitcast.46, f32[256,1280]{1,0:T(8,128)S(1)} %copy-done.4, bf16[16,3,2,80,128]{4,3,2,1,0:T(8,128)(2,1)S(1)} %swap_3.1.msg_ref, f32[1,1280]{1,0:T(1,128)S(1)} %bitcast.47, bf16[1280,1280]{1,0:T(8,128)(2,1)} %bitcast.50, ...), custom_call_target="tpu_custom_call" | custom-call | tf_op jit(solution)/shard_map/input_grad/pallas_call | solution.py:723
  364.8 49.8 %psum.14 = f32[5200]{0:T(1024)S(1)} all-reduce(f32[5200]{0:T(1024)S(1)} %pad_maximum_fusion.2), channel_id=1, replica_groups=mesh['ctx'=16,'fsdp'=2] {'ctx','fsdp'}, use_global_device_ids=true, to_apply=%region_1.2 | all-reduce | flops 5200 | bytes 41600 | tf_op jit(solution)/shard_map/psum | solution.py:808
  414.6 0.7 dynamic_slice.40
  416.6 0.7 dynamic_slice.39
  417.9 0.9 reduce-scatter.5.cloned.1.call-done
  418.8 56.5 %all-gather.7.cloned.1.call-done = bf16[3840,640]{1,0:T(8,128)(2,1)} async-done(((bf16[240,640]{1,0:T(8,128)(2,1)}), bf16[3840,640]{1,0:T(8,128)(2,1)}) %all-gather.7.cloned.1.call-update) | async-done | bytes 4915216 | tf_op jit(solution)/shard_map/all_gather | solution.py:799
  475.3 3.1 convert_bitcast_fusion
  478.4 4.5 copy.39
  482.9 4.5 bitcast_multiply_fusion
  487.4 3.4 slice_bitcast_fusion.3
  490.9 4.6 copy.40
  495.5 4.6 copy.41
  500.1 2.9 copy.42
  503.0 93.8 %all-reduce.5.cloned.1.call-done = bf16[3,640,1280]{2,1,0:T(8,128)(2,1)} async-done(((bf16[3,640,1280]{2,1,0:T(8,128)(2,1)}), bf16[3,640,1280]{2,1,0:T(8,128)(2,1)}) %all-reduce.5.cloned.1.call-update) | async-done | bytes 4915216 | tf_op jit(solution)/shard_map/psum | solution.py:789
  596.8 3.2 convert_element_type.52
  600.1 4.1 slice_bitcast_fusion
  (60 shorter events, 5.5 us)
Async XLA Ops:
  7.2 225.8 %reduce-scatter.7.cloned.1.call-start = ((), (), s32[]{:S(2)}) async-start(), calls=%async_computation.6 | async-start | bytes 983040
  111.1 1.1 copy-start.5
  127.5 0.8 copy-start.2
  151.8 1.1 copy-start.6
  171.6 0.8 copy-start.1
  207.6 4.6 copy-start.7
  212.1 88.0 %all-gather.5.cloned.1.call-start = ((), (), s32[]{:S(2)}) async-start(), calls=%async_computation.4 | async-start | bytes 7372800 | tf_op jit(solution)/shard_map/all_gather | solution.py:778
  216.0 202.8 %reduce-scatter.5.cloned.1.call-start = ((), (), s32[]{:S(2)}) async-start(), calls=%async_computation.2 | async-start | bytes 14745600 | tf_op jit(solution)/shard_map/reduce_scatter | solution.py:788
  225.5 113.0 %copy-start.8 = (f32[3,80,128]{2,1,0:T(8,128)S(1)}, f32[3,80,128]{2,1,0:T(8,128)}, u32[]{:S(2)}) copy-start(f32[3,80,128]{2,1,0:T(8,128)} %get-tuple-element.56) | copy-start | bytes 368644
  225.5 113.6 %copy-start.9 = (f32[1,1280]{1,0:T(1,128)S(1)}, f32[1,1280]{1,0:T(1,128)}, u32[]{:S(2)}) copy-start(f32[1,1280]{1,0:T(1,128)} %get-tuple-element.55) | copy-start | bytes 15364
  225.6 249.8 %all-gather.7.cloned.1.call-start = ((), (), s32[]{:S(2)}) async-start(), calls=%async_computation.5 | async-start | bytes 5222400 | tf_op jit(solution)/shard_map/all_gather | solution.py:799
  234.9 362.0 %all-reduce.5.cloned.1.call-start = ((), (), s32[]{:S(2)}) async-start(), calls=%async_computation.3 | async-start | bytes 9830400 | tf_op jit(solution)/shard_map/psum | solution.py:789
  300.1 39.0 %collective-permute-start = (bf16[3,2,320,1280]{3,2,1,0:T(8,128)(2,1)}, bf16[3,2,320,1280]{3,2,1,0:T(8,128)(2,1)}, u32[]{:S(2)}, u32[]{:S(2)}) collective-permute-start(bf16[3,2,320,1280]{3,2,1,0:T(8,128)(2,1)} %bitcast.53), channel_id=1, source_target_pairs={{0,2},{2,0},{4,6},{6,4},{8,10},{10,8},{12,14},{14,12},{16,18},{18,... | collective-permute-start | bytes 14745608 | tf_op jit(solution)/shard_map/ppermute | solution.py:779
  300.1 1.5 copy-start.3
  347.5 7.4 %copy-start = (bf16[1,256,1280]{2,1,0:T(8,128)(2,1)S(1)}, bf16[1,256,1280]{2,1,0:T(8,128)(2,1)}, u32[]{:S(2)}) copy-start(bf16[1,256,1280]{2,1,0:T(8,128)(2,1)} %param.15) | copy-start | bytes 1966084
  347.5 7.4 %copy-start.4 = (f32[256,1280]{1,0:T(8,128)S(1)}, f32[256,1280]{1,0:T(8,128)}, u32[]{:S(2)}) copy-start(f32[256,1280]{1,0:T(8,128)} %get-tuple-element.42.dh_ref) | copy-start | bytes 3932164
Sparse Core Ops, SparseCore 0:
  212.2 20.7 reduce-scatter.6
  235.2 64.8 all-gather.4
  302.5 116.1 reduce-scatter.4
  420.8 54.4 all-gather.6
  478.8 117.9 all-reduce.4

commit v2 on v1

v2 whole, which is shorter than its diff:
```python
import functools
import math

import jax
import jax.numpy as jnp
from jax import lax
from jax.experimental import pallas as pl
from jax.experimental.pallas import tpu as pltpu
from jax.sharding import PartitionSpec as P

H = 16
HD = 80
BLK = 128
D = 1280
EPS = 1e-06
LOG2E = 1.442695041
NEG = -1e30
MESH = pl.DeviceIdType.MESH
F32 = jnp.float32
BF16 = jnp.bfloat16
VMEM = pltpu.VMEM
MIB = 1 << 20

NN = (((1,), (0,)), ((), ()))
NT = (((1,), (1,)), ((), ()))
TN = (((0,), (0,)), ((), ()))


def dot(left, right, dims=NN):
    return lax.dot_general(left, right, dims, preferred_element_type=F32)


def al(value, multiple):
    return pl.multiple_of(value, multiple)


def in_vmem():
    return pl.BlockSpec(memory_space=pltpu.VMEM)


def in_smem():
    return pl.BlockSpec(memory_space=pltpu.SMEM)


def in_any():
    return pl.BlockSpec(memory_space=pl.ANY)


def cost(microseconds):
    return pl.CostEstimate(flops=0, bytes_accessed=int(microseconds * 3.0e6), transcendentals=0)


class Place:
    def __init__(self, n, nf):
        self.n, self.nf = n, nf
        self.c = lax.axis_index("ctx")
        self.f = lax.axis_index("fsdp")
        self.zlen = n // 4
        self.z, self.y, self.core = self.c // 4, (self.c // 2) % 2, self.c % 2
        self.twin = self.idx(self.z, self.y, 1 - self.core)
        self.ypeer = self.idx(self.z, 1 - self.y, self.core)
        self.targets = (
            self.idx(self.z + 1, self.y, self.core), self.idx(self.z - 1, self.y, self.core),
            self.ypeer, self.twin,
        )
        self.guards = (self.z < self.zlen - 1, self.z > 0, None, None)
        self.fpeers = [(self.f + s) % nf for s in range(1, nf)]
        self.fsources = [(self.f + nf - s) % nf for s in range(1, nf)]

    def idx(self, z, y, core):
        return (z * 2 + y) * 2 + core

    def level(self, k):
        if k == 0:
            return [(self.z, None, 0)]
        return [
            (self.z + k, self.z + k < self.zlen, 1),
            (self.z - k, self.z - k >= 0, -1),
        ]

    def greet_neighbours(self):
        barrier = pltpu.get_barrier_semaphore()
        for target, guard in zip(self.targets, self.guards):
            when(guard, lambda target=target: pl.semaphore_signal(
                barrier, inc=1, device_id=(target, self.f), device_id_type=MESH))
        for peer in self.fpeers:
            pl.semaphore_signal(barrier, inc=1, device_id=(self.c, peer), device_id_type=MESH)
        ends = jnp.minimum(self.z, 1) + jnp.minimum(self.zlen - 1 - self.z, 1)
        pl.semaphore_wait(barrier, 1 + self.nf + ends)

    def greet_all(self, with_fsdp):
        barrier = pltpu.get_barrier_semaphore()
        for s in range(1, self.n):
            pl.semaphore_signal(
                barrier, inc=1, device_id=((self.c + s) % self.n, self.f), device_id_type=MESH)
        if with_fsdp:
            for peer in self.fpeers:
                pl.semaphore_signal(barrier, inc=1, device_id=(self.c, peer), device_id_type=MESH)
        pl.semaphore_wait(barrier, self.n - 1 + (self.nf - 1 if with_fsdp else 0))


def when(guard, body):
    if guard is None:
        body()
    else:
        pl.when(guard)(body)


class Spread:
    def __init__(self, place, buf, send_sem, recv_sem, pieces):
        self.p, self.buf, self.send_sem, self.recv_sem, self.pieces = place, buf, send_sem, recv_sem, pieces

    def copy(self, way, origin, i):
        where = self.buf.at[origin, i] if self.pieces > 1 else self.buf.at[origin]
        return pltpu.make_async_remote_copy(
            src_ref=where, dst_ref=where,
            send_sem=self.send_sem.at[way, origin, i], recv_sem=self.recv_sem.at[origin, i],
            device_id=(self.p.targets[way], self.p.f), device_id_type=MESH,
        )

    def send(self, way, origin, i):
        when(self.p.guards[way], lambda: self.copy(way, origin, i).start())

    def arrive(self, origin, i):
        self.copy(3, origin, i).wait_recv()

    def start(self, i):
        for way in range(4):
            self.send(way, self.p.c, i)

    def chain(self, k, i):
        p = self.p
        for zz, guard, sign in p.level(k):
            def body(zz=zz, sign=sign):
                origin = p.idx(zz, p.y, p.core)
                self.arrive(origin, i)
                self.send(1 if sign == 1 else 0, origin, i)
                self.send(2, origin, i)
                self.send(3, origin, i)
            when(guard, body)

    def pair(self, k, i):
        p = self.p
        for zz, guard, _ in p.level(k):
            def body(zz=zz):
                origin = p.idx(zz, 1 - p.y, p.core)
                self.arrive(origin, i)
                self.send(3, origin, i)
            when(guard, body)

    def from_twin(self, zz):
        p = self.p
        for yy in (p.y, 1 - p.y):
            for i in range(self.pieces):
                self.arrive(p.idx(zz, yy, 1 - p.core), i)

    def drain(self):
        p = self.p
        for i in range(self.pieces):
            for way in range(4):
                when(p.guards[way], lambda way=way, i=i: self.copy(way, p.c, i).wait_send())
            for k in range(p.zlen):
                for zz, guard, sign in p.level(k):
                    def body(zz=zz, sign=sign, k=k, i=i):
                        if k:
                            origin = p.idx(zz, p.y, p.core)
                            on = 1 if sign == 1 else 0
                            when(p.guards[on], lambda: self.copy(on, origin, i).wait_send())
                            self.copy(2, origin, i).wait_send()
                            self.copy(3, origin, i).wait_send()
                        self.copy(3, p.idx(zz, 1 - p.y, p.core), i).wait_send()
                    when(guard, body)


class Reduce:
    def __init__(self, place, mine, result, acc, xrecv, yrecv, urecv, drecv, sems):
        self.p, self.mine, self.result, self.acc = place, mine, result, acc
        self.xrecv, self.yrecv, self.urecv, self.drecv = xrecv, yrecv, urecv, drecv
        (self.xs, self.xr, self.ys, self.yr, self.us, self.ur, self.ds, self.dr) = sems
        self.height = acc.shape[0] // place.zlen
        self.width = D // 2
        zlen = place.zlen
        ends = []
        for k in range(zlen // 2):
            ends += [zlen - 1 - k, k]
        self.order = ends

    @staticmethod
    def scratch(nf, zlen, height):
        dma = pltpu.SemaphoreType.DMA
        peers = max(nf - 1, 1)
        piece = VMEM((zlen, height // zlen, D // 2), BF16)
        return [
            VMEM((height // zlen, D // 2), BF16), VMEM((height, D), BF16), VMEM((peers, height, D), BF16),
            piece, piece, piece,
            dma((peers, zlen, 2)), dma((peers, zlen, 2)), dma((zlen,)), dma((zlen,)),
            dma((zlen,)), dma((zlen,)), dma((zlen,)), dma((zlen,)),
        ]

    def at(self, piece, side):
        return (
            pl.ds(al(piece * self.height, 16), self.height),
            pl.ds(al(side * self.width, 128), self.width),
        )

    def remote(self, src, dst, send, recv, c, f):
        return pltpu.make_async_remote_copy(
            src_ref=src, dst_ref=dst, send_sem=send, recv_sem=recv,
            device_id=(c, f), device_id_type=MESH,
        )

    def x_copy(self, s, peer, piece, turn):
        side = (self.p.y + 1 + turn) % 2
        where = self.at(piece, side)
        return self.remote(
            self.mine.at[peer].at[where], self.xrecv.at[s].at[where],
            self.xs.at[s, piece, turn], self.xr.at[s, piece, turn], self.p.c, peer,
        )

    def start_x(self):
        for piece in self.order:
            for turn in range(2):
                for s, peer in enumerate(self.p.fpeers):
                    self.x_copy(s, peer, piece, turn).start()

    def add(self, dst, terms):
        step = 48 if self.height % 48 == 0 else 16
        @pl.loop(0, self.height // step)
        def _(t):
            at = pl.ds(al(t * step, 16), step)
            total = terms[0][at, :].astype(F32)
            for term in terms[1:]:
                total = total + term[at, :].astype(F32)
            dst[at, :] = total.astype(BF16)

    def sum_x(self, piece, turn):
        side = (self.p.y + 1 + turn) % 2
        where = self.at(piece, side)
        terms = [self.mine.at[self.p.f].at[where]]
        for s, peer in enumerate(self.p.fpeers):
            self.x_copy(s, peer, piece, turn).wait_recv()
            terms.append(self.xrecv.at[s].at[where])
        self.add(self.acc.at[where], terms)

    def y_copy(self, piece):
        src = self.acc.at[self.at(piece, 1 - self.p.y)]
        return self.remote(
            src, self.yrecv.at[piece], self.ys.at[piece], self.yr.at[piece], self.p.ypeer, self.p.f)

    def u_copy(self, piece):
        src = self.acc.at[self.at(piece, self.p.y)]
        return self.remote(
            src, self.urecv.at[piece], self.us.at[piece], self.ur.at[piece], self.p.targets[0], self.p.f)

    def d_copy(self, piece):
        src = self.acc.at[self.at(piece, self.p.y)]
        return self.remote(
            src, self.drecv.at[piece], self.ds.at[piece], self.dr.at[piece], self.p.targets[1], self.p.f)

    def mine_of(self, piece):
        return self.acc.at[self.at(piece, self.p.y)]

    def xy(self, t):
        piece = self.order[t]
        self.sum_x(piece, 0)
        self.y_copy(piece).start()
        self.sum_x(piece, 1)

    def after_y(self, t):
        piece = self.order[t]
        self.y_copy(piece).wait_recv()
        self.add(self.mine_of(piece), [self.mine_of(piece), self.yrecv.at[piece]])

    def chain(self, t, hop):
        p, piece = self.p, self.order[t]
        if hop < piece:
            @pl.when(p.z == hop)
            def _():
                if hop:
                    self.u_copy(piece).wait_recv()
                    self.add(self.mine_of(piece), [self.mine_of(piece), self.urecv.at[piece]])
                self.u_copy(piece).start()
        if p.zlen - 1 - hop > piece:
            @pl.when(p.z == p.zlen - 1 - hop)
            def _():
                if hop:
                    self.d_copy(piece).wait_recv()
                    self.add(self.mine_of(piece), [self.mine_of(piece), self.drecv.at[piece]])
                self.d_copy(piece).start()

    def last(self):
        p = self.p
        @pl.when(p.z > 0)
        def _():
            self.u_copy(p.z).wait_recv()
            self.add(self.mine_of(p.z), [self.mine_of(p.z), self.urecv.at[p.z]])
        @pl.when(p.z < p.zlen - 1)
        def _():
            self.d_copy(p.z).wait_recv()
            self.add(self.mine_of(p.z), [self.mine_of(p.z), self.drecv.at[p.z]])
        self.add(self.result, [self.mine_of(p.z)])

    def drain(self):
        p = self.p
        for piece in self.order:
            for turn in range(2):
                for s, peer in enumerate(p.fpeers):
                    self.x_copy(s, peer, piece, turn).wait_send()
            self.y_copy(piece).wait_send()
            pl.when(p.z < piece)(lambda piece=piece: self.u_copy(piece).wait_send())
            pl.when(p.z > piece)(lambda piece=piece: self.d_copy(piece).wait_send())


def gather_kernel(
    n, nf, x_ref, wh_ref, vec_ref, wo_ref, w1_ref, w2_ref, wq_ref, wk_ref, wv_ref,
    a_out, qkv_out, mats_out, vecs_out, mine_out, other_out,
    abuf, norm, whbuf, wht, vecbuf, g1_ref, stage, wcast,
    ag_send, ag_recv, wh_send, wh_recv, vec_send, vec_recv,
    ld_sem, own_sem, mx_send, mx_recv, ms_send, ms_recv, a_sem, keep_sem,
):
    p = Place(n, nf)
    c, f, core, zlen = p.c, p.f, p.core, p.zlen
    rows = wh_ref.shape[0]
    part = rows // 2
    p.greet_neighbours()
    spread = Spread(p, abuf, ag_send, ag_recv, 2)

    for i in range(2):
        abuf[c, i] = x_ref[pl.ds(i * BLK, BLK), :]
        spread.start(i)

    def wh_copy(s, peer):
        return pltpu.make_async_remote_copy(
            src_ref=wh_ref, dst_ref=whbuf.at[pl.ds(al(f * rows, 16), rows)],
            send_sem=wh_send.at[s], recv_sem=wh_recv.at[s],
            device_id=(c, peer), device_id_type=MESH,
        )

    def vec_copy(s, peer):
        return pltpu.make_async_remote_copy(
            src_ref=vec_ref, dst_ref=vecbuf.at[f],
            send_sem=vec_send.at[s], recv_sem=vec_recv.at[s],
            device_id=(c, peer), device_id_type=MESH,
        )

    for s, peer in enumerate(p.fpeers):
        vec_copy(s, peer).start()
        wh_copy(s, peer).start()
    whbuf[pl.ds(al(f * rows, 16), rows), :] = wh_ref[...]
    vecbuf[f] = vec_ref[...]

    shards = (wo_ref, w1_ref, w2_ref, wq_ref, wk_ref, wv_ref)
    steps = [(m, h) for h in range(2) for m in range(3)] + [(m, h) for h in range(2) for m in range(3, 6)]

    def half_of(h):
        return (core + h) % 2

    def load(step):
        m, h = steps[step]
        return pltpu.make_async_copy(
            shards[m].at[pl.ds(al(half_of(h) * part, 16), part)],
            stage.at[step % 2], ld_sem.at[step % 2],
        )

    def mx_copy(m, s, peer, source):
        return pltpu.make_async_remote_copy(
            src_ref=wcast.at[m, core],
            dst_ref=mats_out.at[m, pl.ds(al(source * rows + core * part, 16), part)],
            send_sem=mx_send.at[m, s], recv_sem=mx_recv.at[m, s],
            device_id=(c, peer), device_id_type=MESH,
        )

    def keep_copies(m):
        if m < 3:
            return [
                pltpu.make_async_copy(
                    wcast.at[m, h], mats_out.at[m, pl.ds(al(f * rows + h * part, 16), part)],
                    keep_sem.at[m, h],
                ) for h in range(2)
            ]
        return [
            pltpu.make_async_copy(wcast.at[m, half_of(h)], out.at[m - 3], keep_sem.at[m, h])
            for h, out in enumerate((mine_out, other_out))
        ]

    def cast(step):
        m, h = steps[step]
        if step + 1 < len(steps):
            load(step + 1).start()
        load(step).wait()
        chunk = part // 4 if part % 64 == 0 else part
        @pl.loop(0, part // chunk)
        def _(t):
            wcast[m, half_of(h), pl.ds(al(t * chunk, 16), chunk), :] = stage[
                step % 2, pl.ds(al(t * chunk, 16), chunk), :
            ].astype(BF16)
        if h == 0 and m < 3:
            for s, peer in enumerate(p.fpeers):
                mx_copy(m, s, peer, f).start()
        if h == 1:
            for copy in keep_copies(m):
                copy.start()

    load(0).start()
    for step in range(len(steps)):
        cast(step)

    for s, peer in enumerate(p.fpeers):
        wh_copy(s, peer).wait_recv()
        vec_copy(s, peer).wait_recv()
    wht[...] = whbuf[...].astype(F32).T.astype(BF16)
    vecs_out[...] = vecbuf[...]
    for source in range(nf):
        g1_ref[:, pl.ds(source * rows, rows)] = vecbuf[source, 0:1, 0:rows]

    def a_copy(slot, origin):
        return pltpu.make_async_copy(norm.at[slot], a_out.at[origin], a_sem.at[slot])

    def project(slot, origin):
        for i in range(2):
            x = abuf[origin, i].astype(F32)
            scale = lax.rsqrt(jnp.mean(x * x, axis=-1, keepdims=True) + EPS)
            norm[slot, i] = (x * scale * g1_ref[...]).astype(BF16)
        a_copy(slot, origin).start()
        block = norm[slot].reshape(2 * BLK, D)
        qkv_out[origin] = dot(wht[: 3 * HD, :], block, NT)

    def compute(k):
        for zz, guard, _ in p.level(k):
            def body(zz=zz):
                spread.from_twin(zz)
                @pl.loop(0, 4)
                def _(t):
                    if k:
                        a_copy(t, zz * 4 + t).wait()
                    project(t, zz * 4 + t)
            when(guard, body)

    def ms_copy(m, s, source, half):
        where = mats_out.at[m, pl.ds(al(source * rows + half * part, 16), part)]
        return pltpu.make_async_remote_copy(
            src_ref=where, dst_ref=where,
            send_sem=ms_send.at[m, s], recv_sem=ms_recv.at[m, s],
            device_id=(p.twin, f), device_id_type=MESH,
        )

    def pass_matrix(m):
        for s, (peer, source) in enumerate(zip(p.fpeers, p.fsources)):
            mx_copy(m, s, peer, source).wait_recv()
            ms_copy(m, s, source, core).start()

    for k in range(1, zlen):
        for i in range(2):
            spread.chain(k, i)
            spread.pair(k - 1, i)
        compute(k - 1)
        if k == 2:
            pass_matrix(0)
    for i in range(2):
        spread.pair(zlen - 1, i)
    pass_matrix(1)
    compute(zlen - 1)
    pass_matrix(2)

    for m in range(6):
        for copy in keep_copies(m):
            copy.wait()
    for m in range(3):
        for s, (peer, source) in enumerate(zip(p.fpeers, p.fsources)):
            mx_copy(m, s, peer, f).wait_send()
            ms_copy(m, s, source, core).wait_send()
            ms_copy(m, s, source, 1 - core).wait_recv()
    for s, peer in enumerate(p.fpeers):
        wh_copy(s, peer).wait_send()
        vec_copy(s, peer).wait_send()
    spread.drain()
    for slot in range(4):
        a_copy(slot, slot).wait()


def gather(n, nf, x, wh, vec, mats):
    rows = wh.shape[0]
    dma = pltpu.SemaphoreType.DMA
    peers = max(nf - 1, 1)
    half = jax.ShapeDtypeStruct((3, rows // 2, D), BF16)
    return pl.pallas_call(
        functools.partial(gather_kernel, n, nf),
        out_shape=(
            jax.ShapeDtypeStruct((n, 2, BLK, D), BF16),
            jax.ShapeDtypeStruct((n, 3 * HD, 2 * BLK), F32),
            jax.ShapeDtypeStruct((3, nf * rows, D), BF16),
            jax.ShapeDtypeStruct((nf,) + vec.shape, F32),
            half, half,
        ),
        in_specs=[in_vmem(), in_vmem(), in_vmem()] + [in_any()] * 6,
        out_specs=(in_any(), in_vmem(), in_any(), in_vmem(), in_any(), in_any()),
        scratch_shapes=[
            VMEM((n, 2, BLK, D), BF16),
            VMEM((4, 2, BLK, D), BF16),
            VMEM((nf * rows, 256), BF16),
            VMEM((256, nf * rows), BF16),
            VMEM((nf,) + vec.shape, F32),
            VMEM((1, nf * rows), F32),
            VMEM((2, rows // 2, D), F32),
            VMEM((6, 2, rows // 2, D), BF16),
            dma((4, n, 2)), dma((n, 2)), dma((peers,)), dma((peers,)), dma((peers,)), dma((peers,)),
            dma((2,)), dma((3,)), dma((3, peers)), dma((3, peers)), dma((3, peers)), dma((3, peers)),
            dma((4,)), dma((6, 2)),
        ],
        compiler_params=pltpu.CompilerParams(
            collective_id=0, has_side_effects=True, vmem_limit_bytes=56 * MIB
        ),
        cost_estimate=cost(60),
        name="gather_tokens",
    )(x, wh, vec, *mats)


class Swap:
    def __init__(self, place, src, dst, send_sem, recv_sem, own_sem):
        self.p, self.src, self.dst = place, src, dst
        self.send_sem, self.recv_sem, self.own_sem = send_sem, recv_sem, own_sem

    def copy(self, s, block):
        p = self.p
        return pltpu.make_async_remote_copy(
            src_ref=self.src.at[(p.c + s) % p.n], dst_ref=self.dst.at[block],
            send_sem=self.send_sem.at[s], recv_sem=self.recv_sem.at[s],
            device_id=((p.c + s) % p.n, p.f), device_id_type=MESH,
        )

    def own(self):
        return pltpu.make_async_copy(self.src.at[self.p.c], self.dst.at[self.p.c], self.own_sem)

    def start(self):
        for s in range(1, self.p.n):
            self.copy(s, self.p.c).start()
        self.own().start()

    def wait(self):
        self.own().wait()
        for s in range(1, self.p.n):
            self.copy(s, (self.p.c + self.p.n - s) % self.p.n).wait_recv()

    def drain(self):
        for s in range(1, self.p.n):
            self.copy(s, self.p.c).wait_send()


def swap_kernel(n, nf, src, dst, send_sem, recv_sem, own_sem):
    p = Place(n, nf)
    p.greet_all(False)
    swap = Swap(p, src, dst, send_sem, recv_sem, own_sem)
    swap.start()
    swap.wait()
    swap.drain()


def swap_out(n, nf, blocks):
    dma = pltpu.SemaphoreType.DMA
    return pl.pallas_call(
        functools.partial(swap_kernel, n, nf),
        out_shape=jax.ShapeDtypeStruct(blocks.shape, blocks.dtype),
        in_specs=[in_vmem()],
        out_specs=in_vmem(),
        scratch_shapes=[dma((n,)), dma((n,)), dma],
        compiler_params=pltpu.CompilerParams(
            collective_id=1, has_side_effects=True, vmem_limit_bytes=32 * MIB
        ),
        cost_estimate=cost(15),
        name="swap_out",
    )(blocks)


def swap_grad_kernel(
    n, nf, src, ot, bt, zt, gb, du, cot,
    dst, sum_out,
    mine, theirs, got, send_sem, recv_sem, own_sem, tw_send, tw_recv, out_sem,
):
    p = Place(n, nf)
    p.greet_all(False)
    swap = Swap(p, src, dst, send_sem, recv_sem, own_sem)
    swap.start()
    part = mine.shape[2]
    rows = 2 * part
    pairs = ((ot, gb), (bt, du), (zt, cot))

    def twin_copy(m):
        return pltpu.make_async_remote_copy(
            src_ref=theirs.at[:, m], dst_ref=got.at[:, m],
            send_sem=tw_send.at[m], recv_sem=tw_recv.at[m],
            device_id=(p.twin, p.f), device_id_type=MESH,
        )

    def out_copy(m):
        return pltpu.make_async_copy(mine.at[:, m], sum_out.at[:, m], out_sem.at[m])

    for half, keep in ((1 - p.core, theirs), (p.core, mine)):
        for m, (left, right) in enumerate(pairs):
            @pl.loop(0, D // WIDE)
            def _(j):
                sl = pl.ds(al(j * WIDE, WIDE), WIDE)
                for source in range(nf):
                    where = pl.ds(al(source * rows + half * part, 16), part)
                    keep[source, m, :, sl] = dot(left[where, :], right[:, sl]).astype(BF16)
            if keep is theirs:
                twin_copy(m).start()
    for m in range(3):
        twin_copy(m).wait_recv()
        for source in range(nf):
            chunk = part // 4 if part % 64 == 0 else part
            @pl.loop(0, part // chunk)
            def _(t):
                where = pl.ds(al(t * chunk, 16), chunk)
                mine[source, m, where, :] = (
                    mine[source, m, where, :].astype(F32) + got[source, m, where, :].astype(F32)
                ).astype(BF16)
        out_copy(m).start()
    swap.wait()
    swap.drain()
    for m in range(3):
        twin_copy(m).wait_send()
        out_copy(m).wait()


def swap_grad(n, nf, blocks, ot, bt, zt, gb, du, cot):
    dma = pltpu.SemaphoreType.DMA
    part = D // nf // 2
    shape = (nf, 3, part, D)
    return pl.pallas_call(
        functools.partial(swap_grad_kernel, n, nf),
        out_shape=(
            jax.ShapeDtypeStruct(blocks.shape, blocks.dtype),
            jax.ShapeDtypeStruct(shape, BF16),
        ),
        in_specs=[in_vmem()] * 7,
        out_specs=(in_vmem(), in_any()),
        scratch_shapes=[
            VMEM(shape, BF16), VMEM(shape, BF16), VMEM(shape, BF16),
            dma((n,)), dma((n,)), dma, dma((3,)), dma((3,)), dma((3,)),
        ],
        compiler_params=pltpu.CompilerParams(
            collective_id=2, has_side_effects=True, vmem_limit_bytes=48 * MIB
        ),
        cost_estimate=cost(18),
        name="swap_grad",
    )(blocks, ot, bt, zt, gb, du, cot)


def seq_start(ends, base, token):
    start = jnp.zeros_like(token)
    for e in ends:
        start = jnp.where(e - base <= token, jnp.maximum(start, e - base), start)
    return start


def read_ends(lengths_ref):
    ends, total = [], jnp.int32(0)
    for i in range(lengths_ref.shape[1]):
        total = total + lengths_ref[0, i]
        ends.append(total)
    return ends


def pad_rows(block):
    return jnp.concatenate([block, jnp.zeros((BLK - HD, block.shape[1]), block.dtype)], axis=0)


class Layout:
    def __init__(self, n, total_blocks):
        self.n = n
        self.hpd = 2 * H // n
        self.half_blocks = total_blocks // 2
        self.size = self.half_blocks * BLK
        self.rows = self.hpd * self.size
        self.tile = 512

    def half(self, i):
        return i if self.hpd == 2 else lax.axis_index("ctx") % 2

    def nat(self, deal_ref, d, i):
        half = self.half(i)
        block = deal_ref[2 * d + half]
        if self.hpd == 1:
            block = block - half * self.half_blocks
        return al(block * BLK, BLK)

    def base(self, unit):
        return self.half(unit) * self.size if self.hpd == 1 else unit * self.size


def fwd_kernel(
    lay, deal_ref, len_ref, qkv_ref, bias_ref, c_ref,
    ot_out, qraw, qst, kt, vt, kn, ot, lse,
    m_ref, l_ref, acc_ref,
):
    tile = lay.tile

    @pl.loop(0, lay.n)
    def _(d):
        for i in range(lay.hpd):
            nat = lay.nat(deal_ref, d, i)
            cols = pl.ds(nat, BLK)
            half = lay.half(i)
            src = pl.ds(half * BLK if lay.hpd == 2 else al(half * BLK, BLK), BLK)
            block = qkv_ref[d, :, src] + bias_ref[...]
            qr, kr, vr = block[:HD], block[HD : 2 * HD], block[2 * HD :]
            qraw[:, cols] = qr
            qst[:, cols] = pad_rows(qr * c_ref[...]).astype(BF16)
            kt[:, cols] = kr.astype(BF16)
            vt[:, cols] = vr.astype(BF16)
            kn[cols, :] = pad_rows(kr).T.astype(BF16)

    ends = read_ends(len_ref)
    for unit in range(lay.hpd):
        base = lay.base(unit)
        row0 = unit * lay.size

        @pl.loop(0, lay.size // tile)
        def _(qi):
            cols = pl.ds(al(row0 + qi * tile, tile), tile)
            t_row = qi * tile + lax.broadcasted_iota(jnp.int32, (1, tile), 1)
            start = seq_start(ends, base, t_row)
            low = seq_start(ends, base, qi * tile) // tile
            m_ref[...] = jnp.full_like(m_ref, NEG)
            l_ref[...] = jnp.zeros_like(l_ref)
            acc_ref[...] = jnp.zeros_like(acc_ref)

            def visit(j, diagonal):
                keys = pl.ds(al(row0 + j * tile, tile), tile)
                s = dot(kn[keys, :], qst[:, cols])
                u = j * tile + lax.broadcasted_iota(jnp.int32, (tile, 1), 0)
                seen = u >= start
                if diagonal:
                    seen = seen & (u <= t_row)
                s = jnp.where(seen, s, NEG)
                m_old = m_ref[...]
                m_new = jnp.maximum(m_old, jnp.max(s, axis=0, keepdims=True))
                p = jnp.exp(s - m_new)
                shrink = jnp.exp(m_old - m_new)
                m_ref[...] = m_new
                l_ref[...] = l_ref[...] * shrink + jnp.sum(p, axis=0, keepdims=True)
                acc_ref[...] = acc_ref[...] * shrink + dot(vt[:, keys], p.astype(BF16))

            @pl.loop(low, qi)
            def _(j):
                visit(j, False)

            visit(qi, True)
            ot[:, cols] = acc_ref[...] / l_ref[...]
            lse[:, cols] = m_ref[...] + jnp.log(l_ref[...])

    @pl.loop(0, lay.n)
    def _(d):
        for i in range(lay.hpd):
            ot_out[d, i] = ot[:, pl.ds(lay.nat(deal_ref, d, i), BLK)].astype(BF16)


def attend(lay, deal, lengths, qkv, bias, factor):
    rows = lay.rows
    return pl.pallas_call(
        functools.partial(fwd_kernel, lay),
        out_shape=(
            jax.ShapeDtypeStruct((lay.n, lay.hpd, HD, BLK), BF16),
            jax.ShapeDtypeStruct((HD, rows), F32),
            jax.ShapeDtypeStruct((BLK, rows), BF16),
            jax.ShapeDtypeStruct((HD, rows), BF16),
            jax.ShapeDtypeStruct((HD, rows), BF16),
            jax.ShapeDtypeStruct((rows, BLK), BF16),
            jax.ShapeDtypeStruct((HD, rows), F32),
            jax.ShapeDtypeStruct((1, rows), F32),
        ),
        in_specs=[in_smem(), in_smem()] + [in_vmem()] * 3,
        out_specs=tuple([in_vmem()] * 8),
        scratch_shapes=[
            VMEM((1, lay.tile), F32), VMEM((1, lay.tile), F32), VMEM((HD, lay.tile), F32),
        ],
        compiler_params=pltpu.CompilerParams(vmem_limit_bytes=56 * MIB),
        cost_estimate=cost(19),
        name="attend",
    )(deal, lengths, qkv, bias, factor)


def bwd_kernel(
    lay, deal_ref, len_ref, dot_ref, qraw, qst, kt, vt, kn, ot, lse, c_ref,
    msg_out, small_out,
    qn, vn, don, dost, delta, dk, dv, dqt, sums,
):
    tile = lay.tile

    @pl.loop(0, lay.n)
    def _(d):
        for i in range(lay.hpd):
            cols = pl.ds(lay.nat(deal_ref, d, i), BLK)
            block = dot_ref[d, i].astype(F32)
            delta[:, cols] = jnp.sum(block * ot[:, cols], axis=0, keepdims=True)
            block = pad_rows(block)
            dost[:, cols] = block.astype(BF16)
            don[cols, :] = block.T.astype(BF16)

    @pl.loop(0, lay.rows // BLK)
    def _(t):
        cols = pl.ds(al(t * BLK, BLK), BLK)
        qn[cols, :] = qst[:, cols].astype(F32).T.astype(BF16)
        vn[cols, :] = pad_rows(vt[:, cols].astype(F32)).T.astype(BF16)
        dk[cols, :] = jnp.zeros((BLK, BLK), F32)
        dv[cols, :] = jnp.zeros((BLK, BLK), F32)

    ends = read_ends(len_ref)
    for unit in range(lay.hpd):
        base = lay.base(unit)
        row0 = unit * lay.size

        @pl.loop(0, lay.size // tile)
        def _(qi):
            cols = pl.ds(al(row0 + qi * tile, tile), tile)
            t_row = qi * tile + lax.broadcasted_iota(jnp.int32, (1, tile), 1)
            start = seq_start(ends, base, t_row)
            low = seq_start(ends, base, qi * tile) // tile
            dqt[:, cols] = jnp.zeros((HD, tile), F32)

            def visit(j, diagonal):
                keys = pl.ds(al(row0 + j * tile, tile), tile)
                s = dot(kn[keys, :], qst[:, cols])
                u = j * tile + lax.broadcasted_iota(jnp.int32, (tile, 1), 0)
                seen = u >= start
                if diagonal:
                    seen = seen & (u <= t_row)
                p = jnp.exp(jnp.where(seen, s - lse[:, cols], NEG))
                dp = dot(vn[keys, :], dost[:, cols])
                ds = (p * (dp - delta[:, cols])).astype(BF16)
                dv[keys, :] += dot(p.astype(BF16), don[cols, :])
                dk[keys, :] += dot(ds, qn[cols, :])
                dqt[:, cols] += dot(kt[:, keys], ds)

            @pl.loop(low, qi)
            def _(j):
                visit(j, False)

            visit(qi, True)

    sums[...] = jnp.zeros_like(sums)

    @pl.loop(0, lay.n)
    def _(d):
        for i in range(lay.hpd):
            cols = pl.ds(lay.nat(deal_ref, d, i), BLK)
            dqs = dqt[:, cols]
            dq = (dqs * c_ref[...]).astype(BF16)
            dkt = dk[cols, :].T[:HD].astype(BF16)
            dvt = dv[cols, :].T[:HD].astype(BF16)
            msg_out[d, 0, i] = dq
            msg_out[d, 1, i] = dkt
            msg_out[d, 2, i] = dvt
            sums[0, :HD] += dqs * qraw[:, cols]
            sums[1, :HD] += dq.astype(F32)
            sums[2, :HD] += dvt.astype(F32)

    small_out[...] = jnp.zeros_like(small_out)
    for r in range(3):
        small_out[r : r + 1, :] = jnp.sum(sums[r].T, axis=0, keepdims=True)


def attend_back(lay, deal, lengths, grad_t, kept, factor):
    rows = lay.rows
    return pl.pallas_call(
        functools.partial(bwd_kernel, lay),
        out_shape=(
            jax.ShapeDtypeStruct((lay.n, 3, lay.hpd, HD, BLK), BF16),
            jax.ShapeDtypeStruct((8, BLK), F32),
        ),
        in_specs=[in_smem(), in_smem()] + [in_vmem()] * 9,
        out_specs=tuple([in_vmem()] * 2),
        scratch_shapes=[
            VMEM((rows, BLK), BF16), VMEM((rows, BLK), BF16), VMEM((rows, BLK), BF16),
            VMEM((BLK, rows), BF16), VMEM((1, rows), F32),
            VMEM((rows, BLK), F32), VMEM((rows, BLK), F32), VMEM((HD, rows), F32),
            VMEM((3, BLK, BLK), F32),
        ],
        compiler_params=pltpu.CompilerParams(vmem_limit_bytes=58 * MIB),
        cost_estimate=cost(25),
        name="attend_back",
    )(deal, lengths, grad_t, *kept, factor)


WIDE = 256


def over_columns(body):
    @pl.loop(0, D // WIDE)
    def _(j):
        body(pl.ds(al(j * WIDE, WIDE), WIDE))


def ffn_kernel(
    x_ref, cot_ref, ot_ref, g2_ref, mats_ref,
    out_ref, dh_ref, gt_ref, ot, bt, zt, gb, du, dg2_ref,
    o_rows, hidden, nh, b, up, z, db, wide,
):
    tok = x_ref.shape[0]
    wo, w1, w2 = mats_ref.at[0], mats_ref.at[1], mats_ref.at[2]
    for i in range(2):
        for h in range(H):
            ot[pl.ds(h * HD, HD), pl.ds(i * BLK, BLK)] = ot_ref[h, i]
    @pl.loop(0, D // WIDE)
    def _(j):
        sl = pl.ds(al(j * WIDE, WIDE), WIDE)
        o_rows[:, sl] = ot[sl, :].astype(F32).T.astype(BF16)

    def body(sl):
        hidden[:, sl] = x_ref[:, sl].astype(F32) + dot(o_rows[...], wo[:, sl])
    over_columns(body)
    hid = hidden[...]
    r2 = lax.rsqrt(jnp.mean(hid * hid, axis=-1, keepdims=True) + EPS)
    nh[...] = hid * r2
    b[...] = (nh[...] * g2_ref[...]).astype(BF16)

    def body(sl):
        u = dot(b[...], w1[:, sl])
        up[:, sl] = u
        z[:, sl] = (u * jax.nn.sigmoid(u)).astype(BF16)
    over_columns(body)

    def body(sl):
        out_ref[:, sl] = (hidden[:, sl] + dot(z[...], w2[:, sl])).astype(BF16)
        dz = dot(cot_ref[...], w2[sl, :], NT)
        u = up[:, sl]
        sig = jax.nn.sigmoid(u)
        du[:, sl] = (dz * sig * (1.0 + u * (1.0 - sig))).astype(BF16)
    over_columns(body)

    def body(sl):
        g = dot(du[...], w1[sl, :], NT)
        db[:, sl] = g * g2_ref[:, sl]
        dg2_ref[:, sl] = jnp.sum(g * nh[:, sl], axis=0, keepdims=True)
    over_columns(body)
    scaled = db[...]
    mean = jnp.mean(scaled * nh[...], axis=-1, keepdims=True)
    dh = cot_ref[...].astype(F32) + r2 * (scaled - nh[...] * mean)
    dh_ref[...] = dh
    gb[...] = dh.astype(BF16)

    @pl.loop(0, D // WIDE)
    def _(j):
        sl = pl.ds(al(j * WIDE, WIDE), WIDE)
        wide[sl, :] = dot(wo[sl, :], gb[...], NT).astype(BF16)
    for i in range(2):
        for h in range(H):
            gt_ref[h, i] = wide[pl.ds(h * HD, HD), pl.ds(i * BLK, BLK)]

    @pl.loop(0, D // WIDE)
    def _(j):
        sl = pl.ds(al(j * WIDE, WIDE), WIDE)
        bt[sl, :] = b[:, sl].astype(F32).T.astype(BF16)
        zt[sl, :] = z[:, sl].astype(F32).T.astype(BF16)


def ffn(x, cot, ot, g2, mats):
    tok = x.shape[0]
    turned = jax.ShapeDtypeStruct((D, tok), BF16)
    plain = jax.ShapeDtypeStruct((tok, D), BF16)
    return pl.pallas_call(
        ffn_kernel,
        out_shape=(
            plain,
            jax.ShapeDtypeStruct((tok, D), F32),
            jax.ShapeDtypeStruct((H, 2, HD, BLK), BF16),
            turned, turned, turned, plain, plain,
            jax.ShapeDtypeStruct((1, D), F32),
        ),
        in_specs=[in_vmem()] * 5,
        out_specs=tuple([in_vmem()] * 9),
        scratch_shapes=[
            VMEM((tok, D), BF16), VMEM((tok, D), F32), VMEM((tok, D), F32),
            VMEM((tok, D), BF16), VMEM((tok, D), F32), VMEM((tok, D), BF16),
            VMEM((tok, D), F32), VMEM((D, tok), BF16),
        ],
        compiler_params=pltpu.CompilerParams(vmem_limit_bytes=56 * MIB),
        cost_estimate=cost(20),
        name="feed_forward",
    )(x, cot, ot, g2, mats)


VEC_ROWS = 24


def finish_kernel(
    n, nf, hpd, msg, a_ref, sums_ref, mine_ref, other_ref, got_ref, tgot_ref,
    x_ref, dh_ref, g1_ref, dg2_ref, small_ref,
    gx_out, dw_out, fw_out, vec_out,
    back, abuf, left, dw, dwsend, dwrecv, dwown, w, wide, dat, vx, vsum, vall,
    sw_send, sw_recv, sw_own, a_sem, w_sem, x_send, x_recv, own_sem, ag_send, ag_recv, v_send, v_recv, u_send, u_recv,
    fg_send, fg_recv, sums_sem, sums, *reduce_scratch,
):
    p = Place(n, nf)
    c, f = p.c, p.f
    rows = dwsend.shape[2]
    part = rows // 2
    load = pltpu.make_async_copy(sums_ref, sums, sums_sem)
    load.start()
    p.greet_all(True)
    swap = Swap(p, msg, back, sw_send, sw_recv, sw_own)
    swap.start()
    result = reduce_scratch[0]
    reduce = Reduce(p, sums, *reduce_scratch[:6], reduce_scratch[6:])
    load.wait()
    reduce.start_x()

    if hpd == 2:
        a_copy = pltpu.make_async_copy(a_ref, abuf, a_sem)
    else:
        a_copy = pltpu.make_async_copy(a_ref.at[:, pl.ds(c % 2, 1)], abuf, a_sem)
    a_copy.start()
    w_copies = []
    for m in range(3):
        def put(src, source, half):
            at = pl.ds(al(source * rows + half * part, 16), part)
            w_copies.append(pltpu.make_async_copy(src, w.at[m, at], w_sem.at[len(w_copies)]))
        put(mine_ref.at[m], f, p.core)
        put(other_ref.at[m], f, 1 - p.core)
        for s, source in enumerate(p.fsources):
            put(got_ref.at[s, m], source, p.core)
            put(tgot_ref.at[s, m], source, 1 - p.core)
    for copy in w_copies:
        copy.start()

    for d in range(n):
        for i in range(hpd):
            left[:, pl.ds((d * hpd + i) * BLK, BLK)] = msg[d, :, i].reshape(3 * HD, BLK)
    a_copy.wait()
    depth = n * hpd * BLK
    @pl.loop(0, D // WIDE)
    def _(j):
        sl = pl.ds(al(j * WIDE, WIDE), WIDE)
        dw[:, sl] = dot(left[...], abuf[:, :, :, sl].reshape(depth, WIDE))
    for source in range(nf):
        dwsend[source] = dw[:, source * rows : (source + 1) * rows].astype(BF16)

    def x_copy(s, peer):
        return pltpu.make_async_remote_copy(
            src_ref=dwsend.at[peer], dst_ref=dwrecv.at[s],
            send_sem=x_send.at[s], recv_sem=x_recv.at[s],
            device_id=(c, peer), device_id_type=MESH,
        )

    for s, peer in enumerate(p.fpeers):
        x_copy(s, peer).start()
    total = dwsend[f].astype(F32)
    for s, peer in enumerate(p.fpeers):
        x_copy(s, peer).wait_recv()
        total = total + dwrecv[s].astype(F32)
    dwown[...] = total.astype(BF16)
    own = pltpu.make_async_copy(dwown, dw_out.at[c], own_sem)
    own.start()
    own.wait()
    spread = Spread(p, dw_out, ag_send, ag_recv, 1)
    spread.start(0)

    zlen = p.zlen
    for t in range(2 * zlen - 1):
        if t < zlen:
            reduce.xy(t)
        if 1 <= t <= zlen:
            reduce.after_y(t - 1)
            reduce.chain(t - 1, 0)
        for hop in range(1, zlen - 1):
            if 0 <= t - 1 - hop < zlen:
                reduce.chain(t - 1 - hop, hop)
        if 1 <= t < zlen:
            spread.chain(t, 0)
            spread.pair(t - 1, 0)
    reduce.last()
    own = pltpu.make_async_copy(result, fw_out.at[c], own_sem)
    own.start()
    own.wait()
    spread2 = Spread(p, fw_out, fg_send, fg_recv, 1)
    spread2.start(0)

    swap.wait()
    for m in range(3):
        for i in range(2):
            for h in range(H):
                block = back[h, m, i] if hpd == 2 else back[2 * h + i, m, 0]
                wide[m, pl.ds(h * HD, HD), pl.ds(i * BLK, BLK)] = block
    for copy in w_copies:
        copy.wait()

    @pl.loop(0, D // WIDE)
    def _(j):
        sl = pl.ds(al(j * WIDE, WIDE), WIDE)
        total = dot(w[0, sl, :], wide[0]) + dot(w[1, sl, :], wide[1]) + dot(w[2, sl, :], wide[2])
        dat[:, sl] = total.T
    x = x_ref[...].astype(F32)
    r1 = lax.rsqrt(jnp.mean(x * x, axis=-1, keepdims=True) + EPS)
    na = x * r1
    da = dat[...]
    dg1 = jnp.sum(da * na, axis=0, keepdims=True)
    for r in range(D // BLK):
        vx[f, r : r + 1, :] = dg1[:, r * BLK : (r + 1) * BLK]
        vx[f, D // BLK + r : D // BLK + r + 1, :] = dg2_ref[:, r * BLK : (r + 1) * BLK]
    vx[f, 20:24, :] = small_ref[0:4, :]

    def v_copy(s, peer, source):
        return pltpu.make_async_remote_copy(
            src_ref=vx.at[f], dst_ref=vx.at[source],
            send_sem=v_send.at[s], recv_sem=v_recv.at[s],
            device_id=(c, peer), device_id_type=MESH,
        )

    for s, peer in enumerate(p.fpeers):
        v_copy(s, peer, f).start()
    scaled = da * g1_ref[...]
    mean = jnp.mean(scaled * na, axis=-1, keepdims=True)
    gx_out[...] = dh_ref[...] + r1 * (scaled - na * mean)
    for s, (peer, source) in enumerate(zip(p.fpeers, p.fsources)):
        v_copy(s, peer, source).wait_recv()
    vsum[...] = jnp.sum(vx[...], axis=0)
    vall[c] = vsum[...]

    def u_copy(s, block):
        return pltpu.make_async_remote_copy(
            src_ref=vsum, dst_ref=vall.at[block],
            send_sem=u_send.at[s], recv_sem=u_recv.at[s],
            device_id=((c + s) % n, f), device_id_type=MESH,
        )

    for s in range(1, n):
        u_copy(s, c).start()
    spread.pair(p.zlen - 1, 0)
    for k in range(1, zlen):
        spread2.chain(k, 0)
        spread2.pair(k - 1, 0)
    spread2.pair(zlen - 1, 0)
    for k in range(p.zlen):
        for zz, guard, _ in p.level(k):
            when(guard, lambda zz=zz: spread.from_twin(zz))
            when(guard, lambda zz=zz: spread2.from_twin(zz))
    for s in range(1, n):
        u_copy(s, (c + n - s) % n).wait_recv()
    vec_out[...] = vall[...]
    swap.drain()
    spread.drain()
    spread2.drain()
    reduce.drain()
    for s, peer in enumerate(p.fpeers):
        x_copy(s, peer).wait_send()
        v_copy(s, peer, f).wait_send()
    for s in range(1, n):
        u_copy(s, c).wait_send()


def finish(n, nf, hpd, msg, tokens, sums, mine, other, got, tgot, x, dh, g1, dg2, small):
    dma = pltpu.SemaphoreType.DMA
    rows = D // nf
    peers = max(nf - 1, 1)
    tok = x.shape[0]
    return pl.pallas_call(
        functools.partial(finish_kernel, n, nf, hpd),
        out_shape=(
            jax.ShapeDtypeStruct((tok, D), F32),
            jax.ShapeDtypeStruct((n, 3 * HD, rows), BF16),
            jax.ShapeDtypeStruct((n, sums.shape[1] * 4 // n, D // 2), BF16),
            jax.ShapeDtypeStruct((n, VEC_ROWS, BLK), F32),
        ),
        in_specs=[in_vmem()] + [in_any()] * 6 + [in_vmem()] * 5,
        out_specs=(in_vmem(), in_any(), in_any(), in_vmem()),
        scratch_shapes=[
            VMEM(msg.shape, BF16), VMEM((n, hpd, BLK, D), BF16), VMEM((3 * HD, n * hpd * BLK), BF16),
            VMEM((3 * HD, D), F32), VMEM((nf, 3 * HD, rows), BF16), VMEM((peers, 3 * HD, rows), BF16),
            VMEM((3 * HD, rows), BF16), VMEM((3, D, D), BF16), VMEM((3, D, tok), BF16), VMEM((tok, D), F32),
            VMEM((nf, VEC_ROWS, BLK), F32), VMEM((VEC_ROWS, BLK), F32), VMEM((n, VEC_ROWS, BLK), F32),
            dma((n,)), dma((n,)), dma, dma, dma((6 * nf,)), dma((peers,)), dma((peers,)), dma,
            dma((4, n, 1)), dma((n, 1)), dma((peers,)), dma((peers,)), dma((n,)), dma((n,)),
            dma((4, n, 1)), dma((n, 1)), dma, VMEM(sums.shape, BF16),
        ] + Reduce.scratch(nf, n // 4, sums.shape[1]),
        compiler_params=pltpu.CompilerParams(
            collective_id=3, has_side_effects=True, vmem_limit_bytes=60 * MIB
        ),
        cost_estimate=cost(60),
        name="finish",
    )(msg, tokens, sums, mine, other, got, tgot, x, dh, g1, dg2, small)


def turn_kernel(hpd, dw_ref, q_ref, k_ref, v_ref, wide):
    j = pl.program_id(0)

    @pl.when(j == 0)
    def _():
        for m in range(3):
            for h in range(H):
                at = pl.ds(m * HD, HD)
                if hpd == 2:
                    block = dw_ref[h, at, :].astype(F32)
                else:
                    block = dw_ref[2 * h, at, :].astype(F32) + dw_ref[2 * h + 1, at, :].astype(F32)
                wide[m, pl.ds(h * HD, HD), :] = block

    for m, out in enumerate((q_ref, k_ref, v_ref)):
        out[...] = wide[m, pl.ds(al(j * WIDE, WIDE), WIDE), :].T


def turn(hpd, dw):
    n, _, rows = dw.shape
    spec = pl.BlockSpec((rows, WIDE), lambda j: (0, j))
    return pl.pallas_call(
        functools.partial(turn_kernel, hpd),
        grid=(D // WIDE,),
        out_shape=tuple([jax.ShapeDtypeStruct((rows, D), F32)] * 3),
        in_specs=[pl.BlockSpec((n, 3 * HD, rows), lambda j: (0, 0, 0))],
        out_specs=(spec, spec, spec),
        scratch_shapes=[VMEM((3, D, rows), F32)],
        compiler_params=pltpu.CompilerParams(vmem_limit_bytes=48 * MIB),
        cost_estimate=cost(6),
        name="turn",
    )(dw)


def widen_kernel(zlen, part, in_ref, o_ref, u_ref, d_ref):
    j, y = pl.program_id(0), pl.program_id(1)
    height = in_ref.shape[3]
    for m, out in enumerate((o_ref, u_ref, d_ref)):
        for z in range(zlen):
            first, last = max(m * part, z * height), min((m + 1) * part, (z + 1) * height)
            if first < last:
                out[first - m * part : last - m * part, :] = in_ref[
                    z, y, j, first - z * height : last - z * height, :
                ].astype(F32)


def widen(zlen, part, pieces):
    height, half = pieces.shape[1:]
    spec = pl.BlockSpec((part, half), lambda j, y: (j, y))
    return pl.pallas_call(
        functools.partial(widen_kernel, zlen, part),
        grid=(2, 2),
        out_shape=tuple([jax.ShapeDtypeStruct((2 * part, D), F32)] * 3),
        in_specs=[pl.BlockSpec((zlen, 2, 2, height, half), lambda j, y: (0, 0, 0, 0, 0))],
        out_specs=(spec, spec, spec),
        compiler_params=pltpu.CompilerParams(vmem_limit_bytes=48 * MIB),
        cost_estimate=cost(5),
        name="widen",
    )(pieces.reshape(zlen, 2, 2, height, half))


def local(
    n, nf, tokens, cotangent, lengths, deal, gain_attn, query_weight, query_bias, key_weight,
    value_weight, value_bias, query_scale, proj_weight, gain_ffn, up_weight, down_weight,
):
    c = lax.axis_index("ctx")
    f = lax.axis_index("fsdp")
    lay = Layout(n, deal.shape[0])
    head = c * lay.hpd // 2
    rows = query_weight.shape[0]
    x, cot = tokens[0], cotangent[0]

    def low(v):
        return v.astype(BF16).astype(F32)

    g1_own = low(gain_attn)
    slices = [
        lax.dynamic_slice(w, (0, head * HD), (rows, HD)) for w in (query_weight, key_weight, value_weight)
    ]
    wh = jnp.pad(jnp.concatenate(slices, axis=1), ((0, 0), (0, 256 - 3 * HD))).astype(BF16)
    vec = jnp.stack([g1_own, low(query_bias), low(value_bias), low(gain_ffn)])
    vec = jnp.concatenate([vec, jnp.pad(low(query_scale), (0, rows - query_scale.shape[0]))[None]])
    vec = jnp.pad(vec, ((0, 3), (0, -rows % 128)))

    a_all, qkv, mats, vecs, mine, other = gather(
        n, nf, x, wh, vec, (proj_weight, up_weight, down_weight, query_weight, key_weight, value_weight)
    )
    whole = jnp.swapaxes(vecs[:, :5, :rows], 0, 1).reshape(5, nf * rows)
    g1, bq, bv, g2 = whole[0], whole[1], whole[2], whole[3]
    q_param = vecs[:, 4, : query_scale.shape[0]].reshape(HD)
    factor = jnp.log(1.0 + jnp.exp(q_param)) * (LOG2E / math.sqrt(HD))
    bias = jnp.concatenate([
        lax.dynamic_slice(bq, (head * HD,), (HD,)), jnp.zeros((HD,), F32),
        lax.dynamic_slice(bv, (head * HD,), (HD,)),
    ])
    bias = jnp.broadcast_to(bias[:, None], (3 * HD, BLK))
    factor_col = jnp.broadcast_to(factor[:, None], (HD, BLK))

    twins = [(i, i ^ 1) for i in range(n)]
    got = jnp.stack([
        lax.ppermute(mine, "fsdp", [(i, (i + s) % nf) for i in range(nf)]) for s in range(1, nf)
    ])
    tgot = lax.ppermute(got, "ctx", twins)

    ot, *kept = attend(lay, deal, lengths, qkv, bias, factor_col)
    ot = swap_out(n, nf, ot).reshape(H, 2, HD, BLK)
    layer_out, dh, gt, ott, bt, zt, gb, du, dg2 = ffn(x, cot, ot, g2[None], mats)
    gt, sums = swap_grad(n, nf, gt.reshape(n, lay.hpd, HD, BLK), ott, bt, zt, gb, du, cot)

    part = rows // 2
    zlen = n // 4
    sums = jnp.pad(sums.reshape(nf, 3 * part, D), ((0, 0), (0, -3 * part % (16 * zlen)), (0, 0)))

    msg, small = attend_back(lay, deal, lengths, gt, kept, factor_col)
    grad_x, dw, pieces, vectors = finish(
        n, nf, lay.hpd, msg, a_all, sums, mine, other, got, tgot, x, dh, g1[None], dg2, small
    )
    dwq, dwk, dwv = turn(lay.hpd, dw)
    grads = widen(zlen, part, pieces)

    def own(v):
        size = v.shape[0] // nf
        return lax.dynamic_slice(v, (f * size,), (size,))

    def of_heads(r):
        return vectors[:, r, :HD].reshape(H, 2 // lay.hpd, HD).sum(axis=1).reshape(D)

    gains = jnp.sum(vectors[:, : 2 * D // BLK], axis=0).reshape(2, D)
    grad_scale = jnp.sum(vectors[:, 20, :HD], axis=0) * jax.nn.sigmoid(q_param) * (LOG2E / math.sqrt(HD))
    return (
        layer_out[None],
        grad_x[None],
        own(gains[0]),
        dwq,
        own(of_heads(21)),
        dwk,
        dwv,
        own(of_heads(22)),
        own(grad_scale),
        grads[0],
        own(gains[1]),
        grads[1],
        grads[2],
    )


def solution(mesh):
    whole, vector, matrix = P("fsdp", "ctx", None), P("fsdp"), P("fsdp", None)
    return jax.shard_map(
        functools.partial(local, mesh.shape["ctx"], mesh.shape["fsdp"]),
        mesh=mesh,
        in_specs=(
            whole, whole, matrix, P(), vector, matrix, vector, matrix, matrix, vector, vector,
            matrix, vector, matrix, matrix,
        ),
        out_specs=(
            whole, whole, vector, matrix, vector, matrix, matrix, vector, vector, matrix, vector,
            matrix, matrix,
        ),
        check_vma=False,
    )
```

time: 613 us -> 445 us (0.73)
  waiting for transfers between devices: 224 us -> 54.3 us
  Pallas kernels: 231 us -> 354 us
  blocking collectives: 49.8 us -> 0 us
  other arithmetic: 46.9 us -> 7.86 us
  local copies, waits for them, and re-layouts: 44.5 us -> 24.5 us
  between operations: 14 us -> 0.8 us
    pallas_call x5 -> x6, Pallas kernels: 104 us -> 234 us  [the longest x1 172 us: finish(): pl.pallas_call(functools.partial(finish_kernel, n, nf, hpd), out_shape=(j...]
    all_gather x2 -> x0, waiting for transfers between devices: 122 us -> none  [the longest x1 65.2 us: local(): mine = lax.all_gather(mine, 'fsdp', axis=1)]
    psum x1 -> x0, waiting for transfers between devices: 93.8 us -> none  [local(): grads = lax.psum(grads, 'ctx').astype(F32)]
    ppermute x1 -> x2, waiting for transfers between devices: 0.01 us -> 54.3 us  [the longest x1 54.3 us: local(): lax.ppermute(mine, 'fsdp', [(i, (i + s) % nf) for i in range(nf)])]
    psum x1 -> x0, blocking collectives: 49.8 us -> none  [local(): vectors = lax.psum(vectors, ('ctx', 'fsdp'))]
    another operation x5 -> x0, other arithmetic: 11.8 us -> none  [the longest x1 9.46 us: local(): jnp.stack([dwo, dw1, dw2])]
    convert_element_type x3 -> x0, other arithmetic: 9.34 us -> none  [the longest x1 3.81 us: local(): lax.dynamic_slice(stacked, (0, core * part, 0), (3, part, D)).astype(BF16)]
    select_n x1 -> x0, other arithmetic: 8.39 us -> none  [local(): second = jnp.where(core == 0, other, mine)]
  transfers between devices with their start and end apart: 6 -> 2, of which waited for: 5 -> 1; matrix products, arithmetic and copies ran while one was open for 10% -> 1% of each run, Pallas kernels for 8% -> 23%
where the time goes in v2:
time: 445 us; the launch traced here: 443 us
  Pallas kernels  354 us (80%)
  waiting for transfers between devices  54.3 us (12%)
  local copies, waits for them, and re-layouts  24.5 us (6%)
  other arithmetic  7.86 us (2%)
    pallas_call x1, Pallas kernels, finish(): pl.pallas_call(functools.partial(finish_kernel, n, nf, hpd), out_shape=(j...  172 us
    pallas_call x1, Pallas kernels, gather(): pl.pallas_call(functools.partial(gather_kernel, n, nf), out_shape=(jax.Sh...  72.6 us
    ppermute x1, waiting for transfers between devices, local(): lax.ppermute(mine, 'fsdp', [(i, (i + s) % nf) for i in range(nf)])  54.3 us
    pallas_call x1, Pallas kernels, attend_back(): pl.pallas_call(functools.partial(bwd_kernel, lay), out_shape=(jax.ShapeDt...  27.3 us
    pallas_call x1, Pallas kernels, attend(): pl.pallas_call(functools.partial(fwd_kernel, lay), out_shape=(jax.ShapeDt...  20 us
    pallas_call x1, Pallas kernels, ffn(): pl.pallas_call(ffn_kernel, out_shape=(plain, jax.ShapeDtypeStruct((tok, D...  19.1 us
    pallas_call x1, Pallas kernels, swap_grad(): pl.pallas_call(functools.partial(swap_grad_kernel, n, nf), out_shape=(jax...  18.8 us
    pallas_call x1, Pallas kernels, swap_out(): pl.pallas_call(functools.partial(swap_kernel, n, nf), out_shape=jax.Shape...  15.4 us
  transfers between devices with their start and end apart: 2, of which 1 were waited for; matrix products, arithmetic and copies ran while one was open for 1% of the time, Pallas kernels for 23%

profile of v2, /device:TPU:0, one launch (start us, length us, event | category | flops | bytes accessed | tf_op | source)
XLA Modules:
  0.0 443.3 jit_solution(2377390678703357985)
XLA Ops:
  0.7 0.7 convert_element_type.15
  1.4 0.7 convert_element_type.28
  2.1 0.7 convert_element_type.29
  2.8 0.7 convert_element_type.30
  3.5 0.7 convert_element_type.31
  4.2 0.6 pad_convert_fusion.vec_ref
  4.8 1.2 dynamic-slice_convert_fusion.2
  6.0 1.5 dynamic-slice_convert_fusion
  7.4 0.9 fusion.4.wh_ref
  8.4 72.6 %gather_tokens.1 = (bf16[16,2,128,1280]{3,2,1,0:T(8,128)(2,1)}, f32[16,240,256]{2,1,0:T(8,128)}, bf16[3,1280,1280]{2,1,0:T(8,128)(2,1)}, f32[2,8,640]{2,1,0:T(8,...) custom-call(bf16[256,1280]{1,0:T(8,128)(2,1)} %bitcast.18, bf16[640,256]{1,0:T(8,128)(2,1)} %fusion.4.wh_ref, ...), custom_call_target="tpu_custom_call" | custom-call | bytes 180000000 | tf_op jit(solution)/shard_map/gather_tokens/pallas_call | solution.py:486
  81.0 1.6 collective-permute-start
  82.5 54.3 %collective-permute-done = bf16[3,320,1280]{2,1,0:T(8,128)(2,1)S(1)} collective-permute-done((bf16[3,320,1280]{2,1,0:T(8,128)(2,1)}, bf16[3,320,1280]{2,1,0:T(8,128)(2,1)S(1)}, u32[]{:S(2)}, u32[]{:S(2)}) %collective-permute-start) | collective-permute-done | bytes 2457632 | tf_op jit(solution)/shard_map/ppermute | solution.py:1283
  136.8 0.8 slice_bitcast_fusion
  137.6 0.6 fusion.5
  138.2 0.1 dynamic_slice.34
  138.4 0.7 divide_reduce_fusion
  139.1 0.1 mul.38
  139.2 0.1 pad_maximum_fusion
  139.3 0.8 broadcast_in_dim.27.bias_ref
  140.1 0.7 broadcast_in_dim.28.c_ref
  140.7 20.0 %attend.1 = (bf16[16,2,80,128]{3,2,1,0:T(8,128)(2,1)}, f32[80,4096]{1,0:T(8,128)}, bf16[128,4096]{1,0:T(8,128)(2,1)}, bf16[80,4096]{1,0:T(8,128)(2,1)}, bf16[80,...) custom-call(s32[32]{0:T(128)} %deal_ref.3, s32[1,8]{1,0:T(1,128)} %len_ref.3, ...), custom_call_target="tpu_custom_call" | custom-call | bytes 57000000 | tf_op jit(solution)/shard_map/attend/pallas_call | solution.py:760
  160.8 1.1 copy-done.10
  161.9 15.4 %swap_out.1.ot_ref = bf16[16,2,80,128]{3,2,1,0:T(8,128)(2,1)S(1)} custom-call(bf16[16,2,80,128]{3,2,1,0:T(8,128)(2,1)S(1)} %copy-done.10), custom_call_target="tpu_custom_call" | custom-call | bytes 45000000 | tf_op jit(solution)/shard_map/swap_out/pallas_call | solution.py:560
  177.3 0.8 copy-done.3
  178.1 0.1 div.18
  178.2 19.1 %feed_forward.1 = (bf16[256,1280]{1,0:T(8,128)(2,1)}, f32[256,1280]{1,0:T(8,128)}, bf16[16,2,80,128]{3,2,1,0:T(8,128)(2,1)}, bf16[1280,256]{1,0:T(8,128)(2,1)}, ...) custom-call(bf16[256,1280]{1,0:T(8,128)(2,1)} %bitcast.19, ...), custom_call_target="tpu_custom_call" | custom-call | bytes 60000000 | tf_op jit(solution)/shard_map/feed_forward/pallas_call | solution.py:961
  197.4 1.1 copy-done.4
  198.5 1.1 copy-done.5
  199.5 1.1 copy-done.6
  200.6 1.1 copy-done.7
  201.7 1.1 copy-done.8
  202.8 1.1 copy-done.9
  203.9 18.8 %swap_grad.1 = (bf16[16,2,80,128]{3,2,1,0:T(8,128)(2,1)S(1)}, bf16[2,3,320,1280]{3,2,1,0:T(8,128)(2,1)}) custom-call(bf16[16,2,80,128]{3,2,1,0:T(8,128)(2,1)S(1)} %copy-done.4, bf16[1280,256]{1,0:T(8,128)(2,1)S(1)} %copy-done.5, bf16[1280,256]{1,0:T(8,128)(2,1)S(1)} %copy-done.6, bf16[1280,256]{1,0:T(8,128)(2,1)S(1)} %copy-done.7, ...), custom_call_target="tpu_custom_call" | custom-call | bytes 54000000 | tf_op jit(solution)/shard_map/swap_grad/pallas_call | solution.py:629
  222.8 0.8 copy-done.11
  223.6 27.3 %attend_back.1 = (bf16[16,3,2,80,128]{4,3,2,1,0:T(8,128)(2,1)}, f32[8,128]{1,0:T(8,128)}) custom-call(s32[32]{0:T(128)} %deal_ref.3, s32[1,8]{1,0:T(1,128)} %len_ref.3, bf16[16,2,80,128]{3,2,1,0:T(8,128)(2,1)} %copy-done.11, f32[80,4096]{1,0:T(8,128)} %get-tuple-element.62.qraw, bf16[128,4096]{1,0:T(8,128)(2,1)} %get-tuple-element.63.qst, ...), custom_call_target="tpu_custom_call" | custom-call | bytes 75000000 | tf_op jit(solution)/shard_map/attend_back/pallas_call | solution.py:865
  251.0 171.5 %finish.1 = (f32[256,1280]{1,0:T(8,128)}, bf16[16,240,640]{2,1,0:T(8,128)(2,1)}, bf16[16,240,640]{2,1,0:T(8,128)(2,1)}, f32[16,24,128]{2,1,0:T(8,128)}) custom-call(bf16[16,3,2,80,128]{4,3,2,1,0:T(8,128)(2,1)} %get-tuple-element.69.msg, bf16[16,2,128,1280]{3,2,1,0:T(8,128)(2,1)} %get-tuple-element.70.a_ref, bf16[2,960,1280]{2,1,0:T(8,128)(2,1)} %bitcast.21, ...), custom_call_target="tpu_custom_call" | custom-call | bytes 180000000 | tf_op jit(solution)/shard_map/finish/pallas_call | solution.py:1156
  422.5 1.0 slice_reduce_fusion
  423.5 1.1 slice_reduce_fusion.1
  424.6 2.4 copy-done.1
  427.0 5.6 %turn.1 = (f32[640,1280]{1,0:T(8,128)}, f32[640,1280]{1,0:T(8,128)}, f32[640,1280]{1,0:T(8,128)}) custom-call(bf16[16,240,640]{2,1,0:T(8,128)(2,1)S(1)} %copy-done.1), custom_call_target="tpu_custom_call" | custom-call | bytes 18000000 | tf_op jit(solution)/shard_map/turn/pallas_call | solution.py:1204
  432.7 0.7 dynamic_slice.35
  433.3 0.7 dynamic_slice.36
  434.1 0.7 dynamic_slice.37
  434.7 2.4 copy-done
  437.1 3.8 widen.1
  441.0 0.7 dynamic_slice.39
  441.6 0.6 dynamic_slice.38
  442.2 1.1 copy.29
  (34 shorter events, 0.4 us)
Async XLA Ops:
  81.0 55.8 %collective-permute-start = (bf16[3,320,1280]{2,1,0:T(8,128)(2,1)}, bf16[3,320,1280]{2,1,0:T(8,128)(2,1)S(1)}, u32[]{:S(2)}, u32[]{:S(2)}) collective-permute-start(bf16[3,320,1280]{2,1,0:T(8,128)(2,1)} %get-tuple-element.72.mine_ref), channel_id=1, source_target_pairs={{0,1},{1,0},{2,3},{3,2},{4,5},{5,4},{6,7},{7,6},{8,9},{9,8},{10,11... | collective-permute-start | bytes 7372808 | tf_op jit(solution)/shard_map/ppermute | solution.py:1283
  136.8 60.6 %copy-start.12 = (bf16[3,320,1280]{2,1,0:T(8,128)(2,1)}, bf16[3,320,1280]{2,1,0:T(8,128)(2,1)S(1)}, u32[]{:S(2)}) copy-start(bf16[3,320,1280]{2,1,0:T(8,128)(2,1)S(1)} %collective-permute-done) | copy-start | bytes 7372804
  136.8 114.2 %collective-permute-start.1 = (bf16[1,3,320,1280]{3,2,1,0:T(8,128)(2,1)S(1)}, bf16[1,3,320,1280]{3,2,1,0:T(8,128)(2,1)}, u32[]{:S(2)}, u32[]{:S(2)}) collective-permute-start(bf16[1,3,320,1280]{3,2,1,0:T(8,128)(2,1)S(1)} %bitcast.22), channel_id=1, source_target_pairs={{0,2},{2,0},{4,6},{6,4},{8,10},{10,8},{12,14},{14,12},{16,18},{18,... | collective-permute-start | bytes 7372808 | tf_op jit(solution)/shard_map/ppermute | solution.py:1285
  160.8 1.1 copy-start.10
  177.3 0.8 copy-start.3
  178.2 19.1 %copy-start.2 = (bf16[1,256,1280]{2,1,0:T(8,128)(2,1)S(1)}, bf16[1,256,1280]{2,1,0:T(8,128)(2,1)}, u32[]{:S(2)}) copy-start(bf16[1,256,1280]{2,1,0:T(8,128)(2,1)} %param.16) | copy-start | bytes 1966084
  197.4 1.1 copy-start.4
  198.5 1.1 copy-start.5
  199.5 1.1 copy-start.6
  200.6 1.1 copy-start.7
  201.7 1.1 copy-start.8
  202.8 1.1 copy-start.9
  222.7 0.9 copy-start.11
  424.6 2.4 copy-start.1
  427.0 15.2 %copy-start.13 = (f32[256,1280]{1,0:T(8,128)S(1)}, f32[256,1280]{1,0:T(8,128)}, u32[]{:S(2)}) copy-start(f32[256,1280]{1,0:T(8,128)} %get-tuple-element.77) | copy-start | bytes 3932164
  434.7 2.4 copy-start

commit v3 on v2

--- a/solution.py
+++ b/solution.py
@@ -111,7 +111,7 @@
         self.p, self.buf, self.send_sem, self.recv_sem, self.pieces = place, buf, send_sem, recv_sem, pieces
 
     def copy(self, way, origin, i):
-        where = self.buf.at[origin, i] if self.pieces > 1 else self.buf.at[origin]
+        where = self.buf.at[origin, i]
         return pltpu.make_async_remote_copy(
             src_ref=where, dst_ref=where,
             send_sem=self.send_sem.at[way, origin, i], recv_sem=self.recv_sem.at[origin, i],
@@ -217,15 +217,15 @@
             self.xs.at[s, piece, turn], self.xr.at[s, piece, turn], self.p.c, peer,
         )
 
-    def start_x(self):
-        for piece in self.order:
-            for turn in range(2):
-                for s, peer in enumerate(self.p.fpeers):
-                    self.x_copy(s, peer, piece, turn).start()
-
-    def add(self, dst, terms):
-        step = 48 if self.height % 48 == 0 else 16
-        @pl.loop(0, self.height // step)
+    def start_x(self, t):
+        for turn in range(2):
+            for s, peer in enumerate(self.p.fpeers):
+                self.x_copy(s, peer, self.order[t], turn).start()
+
+    def add(self, dst, terms, count=None):
+        count = count or self.height
+        step = 48 if count % 48 == 0 else 16
+        @pl.loop(0, count // step)
         def _(t):
             at = pl.ds(al(t * step, 16), step)
             total = terms[0][at, :].astype(F32)
@@ -508,7 +508,7 @@
             dma((4,)), dma((6, 2)),
         ],
         compiler_params=pltpu.CompilerParams(
-            collective_id=0, has_side_effects=True, vmem_limit_bytes=56 * MIB
+            collective_id=0, has_side_effects=True, vmem_limit_bytes=60 * MIB
         ),
         cost_estimate=cost(60),
         name="gather_tokens",
@@ -523,13 +523,13 @@
     def copy(self, s, block):
         p = self.p
         return pltpu.make_async_remote_copy(
-            src_ref=self.src.at[(p.c + s) % p.n], dst_ref=self.dst.at[block],
+            src_ref=self.src((p.c + s) % p.n), dst_ref=self.dst(block),
             send_sem=self.send_sem.at[s], recv_sem=self.recv_sem.at[s],
             device_id=((p.c + s) % p.n, p.f), device_id_type=MESH,
         )
 
     def own(self):
-        return pltpu.make_async_copy(self.src.at[self.p.c], self.dst.at[self.p.c], self.own_sem)
+        return pltpu.make_async_copy(self.src(self.p.c), self.dst(self.p.c), self.own_sem)
 
     def start(self):
         for s in range(1, self.p.n):
@@ -549,7 +549,7 @@
 def swap_kernel(n, nf, src, dst, send_sem, recv_sem, own_sem):
     p = Place(n, nf)
     p.greet_all(False)
-    swap = Swap(p, src, dst, send_sem, recv_sem, own_sem)
+    swap = Swap(p, lambda d: src.at[d], lambda d: dst.at[d], send_sem, recv_sem, own_sem)
     swap.start()
     swap.wait()
     swap.drain()
@@ -564,86 +564,11 @@
         out_specs=in_vmem(),
         scratch_shapes=[dma((n,)), dma((n,)), dma],
         compiler_params=pltpu.CompilerParams(
-            collective_id=1, has_side_effects=True, vmem_limit_bytes=32 * MIB
+            collective_id=1, has_side_effects=True, vmem_limit_bytes=60 * MIB
         ),
         cost_estimate=cost(15),
         name="swap_out",
     )(blocks)
-
-
-def swap_grad_kernel(
-    n, nf, src, ot, bt, zt, gb, du, cot,
-    dst, sum_out,
-    mine, theirs, got, send_sem, recv_sem, own_sem, tw_send, tw_recv, out_sem,
-):
-    p = Place(n, nf)
-    p.greet_all(False)
-    swap = Swap(p, src, dst, send_sem, recv_sem, own_sem)
-    swap.start()
-    part = mine.shape[2]
-    rows = 2 * part
-    pairs = ((ot, gb), (bt, du), (zt, cot))
-
-    def twin_copy(m):
-        return pltpu.make_async_remote_copy(
-            src_ref=theirs.at[:, m], dst_ref=got.at[:, m],
-            send_sem=tw_send.at[m], recv_sem=tw_recv.at[m],
-            device_id=(p.twin, p.f), device_id_type=MESH,
-        )
-
-    def out_copy(m):
-        return pltpu.make_async_copy(mine.at[:, m], sum_out.at[:, m], out_sem.at[m])
-
-    for half, keep in ((1 - p.core, theirs), (p.core, mine)):
-        for m, (left, right) in enumerate(pairs):
-            @pl.loop(0, D // WIDE)
-            def _(j):
-                sl = pl.ds(al(j * WIDE, WIDE), WIDE)
-                for source in range(nf):
-                    where = pl.ds(al(source * rows + half * part, 16), part)
-                    keep[source, m, :, sl] = dot(left[where, :], right[:, sl]).astype(BF16)
-            if keep is theirs:
-                twin_copy(m).start()
-    for m in range(3):
-        twin_copy(m).wait_recv()
-        for source in range(nf):
-            chunk = part // 4 if part % 64 == 0 else part
-            @pl.loop(0, part // chunk)
-            def _(t):
-                where = pl.ds(al(t * chunk, 16), chunk)
-                mine[source, m, where, :] = (
-                    mine[source, m, where, :].astype(F32) + got[source, m, where, :].astype(F32)
-                ).astype(BF16)
-        out_copy(m).start()
-    swap.wait()
-    swap.drain()
-    for m in range(3):
-        twin_copy(m).wait_send()
-        out_copy(m).wait()
-
-
-def swap_grad(n, nf, blocks, ot, bt, zt, gb, du, cot):
-    dma = pltpu.SemaphoreType.DMA
-    part = D // nf // 2
-    shape = (nf, 3, part, D)
-    return pl.pallas_call(
-        functools.partial(swap_grad_kernel, n, nf),
-        out_shape=(
-            jax.ShapeDtypeStruct(blocks.shape, blocks.dtype),
-            jax.ShapeDtypeStruct(shape, BF16),
-        ),
-        in_specs=[in_vmem()] * 7,
-        out_specs=(in_vmem(), in_any()),
-        scratch_shapes=[
-            VMEM(shape, BF16), VMEM(shape, BF16), VMEM(shape, BF16),
-            dma((n,)), dma((n,)), dma, dma((3,)), dma((3,)), dma((3,)),
-        ],
-        compiler_params=pltpu.CompilerParams(
-            collective_id=2, has_side_effects=True, vmem_limit_bytes=48 * MIB
-        ),
-        cost_estimate=cost(18),
-        name="swap_grad",
-    )(blocks, ot, bt, zt, gb, du, cot)
 
 
 def seq_start(ends, base, token):
@@ -774,112 +699,10 @@
         scratch_shapes=[
             VMEM((1, lay.tile), F32), VMEM((1, lay.tile), F32), VMEM((HD, lay.tile), F32),
         ],
-        compiler_params=pltpu.CompilerParams(vmem_limit_bytes=56 * MIB),
+        compiler_params=pltpu.CompilerParams(vmem_limit_bytes=60 * MIB),
         cost_estimate=cost(19),
         name="attend",
     )(deal, lengths, qkv, bias, factor)
-
-
-def bwd_kernel(
-    lay, deal_ref, len_ref, dot_ref, qraw, qst, kt, vt, kn, ot, lse, c_ref,
-    msg_out, small_out,
-    qn, vn, don, dost, delta, dk, dv, dqt, sums,
-):
-    tile = lay.tile
-
-    @pl.loop(0, lay.n)
-    def _(d):
-        for i in range(lay.hpd):
-            cols = pl.ds(lay.nat(deal_ref, d, i), BLK)
-            block = dot_ref[d, i].astype(F32)
-            delta[:, cols] = jnp.sum(block * ot[:, cols], axis=0, keepdims=True)
-            block = pad_rows(block)
-            dost[:, cols] = block.astype(BF16)
-            don[cols, :] = block.T.astype(BF16)
-
-    @pl.loop(0, lay.rows // BLK)
-    def _(t):
-        cols = pl.ds(al(t * BLK, BLK), BLK)
-        qn[cols, :] = qst[:, cols].astype(F32).T.astype(BF16)
-        vn[cols, :] = pad_rows(vt[:, cols].astype(F32)).T.astype(BF16)
-        dk[cols, :] = jnp.zeros((BLK, BLK), F32)
-        dv[cols, :] = jnp.zeros((BLK, BLK), F32)
-
-    ends = read_ends(len_ref)
-    for unit in range(lay.hpd):
-        base = lay.base(unit)
-        row0 = unit * lay.size
-
-        @pl.loop(0, lay.size // tile)
-        def _(qi):
-            cols = pl.ds(al(row0 + qi * tile, tile), tile)
-            t_row = qi * tile + lax.broadcasted_iota(jnp.int32, (1, tile), 1)
-            start = seq_start(ends, base, t_row)
-            low = seq_start(ends, base, qi * tile) // tile
-            dqt[:, cols] = jnp.zeros((HD, tile), F32)
-
-            def visit(j, diagonal):
-                keys = pl.ds(al(row0 + j * tile, tile), tile)
-                s = dot(kn[keys, :], qst[:, cols])
-                u = j * tile + lax.broadcasted_iota(jnp.int32, (tile, 1), 0)
-                seen = u >= start
-                if diagonal:
-                    seen = seen & (u <= t_row)
-                p = jnp.exp(jnp.where(seen, s - lse[:, cols], NEG))
-                dp = dot(vn[keys, :], dost[:, cols])
-                ds = (p * (dp - delta[:, cols])).astype(BF16)
-                dv[keys, :] += dot(p.astype(BF16), don[cols, :])
-                dk[keys, :] += dot(ds, qn[cols, :])
-                dqt[:, cols] += dot(kt[:, keys], ds)
-
-            @pl.loop(low, qi)
-            def _(j):
-                visit(j, False)
-
-            visit(qi, True)
-
-    sums[...] = jnp.zeros_like(sums)
-
-    @pl.loop(0, lay.n)
-    def _(d):
-        for i in range(lay.hpd):
-            cols = pl.ds(lay.nat(deal_ref, d, i), BLK)
-            dqs = dqt[:, cols]
-            dq = (dqs * c_ref[...]).astype(BF16)
-            dkt = dk[cols, :].T[:HD].astype(BF16)
-            dvt = dv[cols, :].T[:HD].astype(BF16)
-            msg_out[d, 0, i] = dq
-            msg_out[d, 1, i] = dkt
-            msg_out[d, 2, i] = dvt
-            sums[0, :HD] += dqs * qraw[:, cols]
-            sums[1, :HD] += dq.astype(F32)
-            sums[2, :HD] += dvt.astype(F32)
-
-    small_out[...] = jnp.zeros_like(small_out)
-    for r in range(3):
-        small_out[r : r + 1, :] = jnp.sum(sums[r].T, axis=0, keepdims=True)
-
-
-def attend_back(lay, deal, lengths, grad_t, kept, factor):
-    rows = lay.rows
-    return pl.pallas_call(
-        functools.partial(bwd_kernel, lay),
-        out_shape=(
-            jax.ShapeDtypeStruct((lay.n, 3, lay.hpd, HD, BLK), BF16),
-            jax.ShapeDtypeStruct((8, BLK), F32),
-        ),
-        in_specs=[in_smem(), in_smem()] + [in_vmem()] * 9,
-        out_specs=tuple([in_vmem()] * 2),
-        scratch_shapes=[
-            VMEM((rows, BLK), BF16), VMEM((rows, BLK), BF16), VMEM((rows, BLK), BF16),
-            VMEM((BLK, rows), BF16), VMEM((1, rows), F32),
-            VMEM((rows, BLK), F32), VMEM((rows, BLK), F32), VMEM((HD, rows), F32),
-            VMEM((3, BLK, BLK), F32),
-        ],
-        compiler_params=pltpu.CompilerParams(vmem_limit_bytes=58 * MIB),
-        cost_estimate=cost(25),
-        name="attend_back",
-    )(deal, lengths, grad_t, *kept, factor)
 
 
 WIDE = 256
@@ -974,7 +797,7 @@
             VMEM((tok, D), BF16), VMEM((tok, D), F32), VMEM((tok, D), BF16),
             VMEM((tok, D), F32), VMEM((D, tok), BF16),
         ],
-        compiler_params=pltpu.CompilerParams(vmem_limit_bytes=56 * MIB),
+        compiler_params=pltpu.CompilerParams(vmem_limit_bytes=60 * MIB),
         cost_estimate=cost(20),
         name="feed_forward",
     )(x, cot, ot, g2, mats)
@@ -983,55 +806,231 @@
 VEC_ROWS = 24
 
 
-def finish_kernel(
-    n, nf, hpd, msg, a_ref, sums_ref, mine_ref, other_ref, got_ref, tgot_ref,
-    x_ref, dh_ref, g1_ref, dg2_ref, small_ref,
-    gx_out, dw_out, fw_out, vec_out,
-    back, abuf, left, dw, dwsend, dwrecv, dwown, w, wide, dat, vx, vsum, vall,
-    sw_send, sw_recv, sw_own, a_sem, w_sem, x_send, x_recv, own_sem, ag_send, ag_recv, v_send, v_recv, u_send, u_recv,
-    fg_send, fg_recv, sums_sem, sums, *reduce_scratch,
+class Loads:
+    def __init__(self, sems):
+        self.sems, self.count = sems, 0
+
+    def start(self, src, dst):
+        copy = pltpu.make_async_copy(src, dst, self.sems.at[self.count])
+        self.count += 1
+        copy.start()
+        return copy
+
+
+def backward_kernel(
+    lay, n, nf,
+    rel_ref, inv_ref, len_ref, gt, c_ref, g1_ref, dg2_ref,
+    ot_t_in, bt_in, zt_in, gb_in, du_in, cot_in,
+    qraw_in, qst_in, kt_in, vt_in, kn_in, ot_in, lse_in,
+    a_ref, mine_ref, other_ref, got_ref, x_in, dh_in,
+    gx_out, dw_out, fw_out, vec_out, tg_out,
+    big, sums, wide, abuf, qraw, qst, kt, vt, kn, ot, lse, x_ref, dh_ref,
+    qn, vn, don, dost, delta, dk, dv, dqt, natural, part_sums, left, back, dw, dwsend, dwrecv, dwown, vx, vsum, vall,
+    ld_sem, do_send, do_recv, do_own, dq_send, dq_recv, dq_own, tw_send, tw_recv, tg_send, tg_recv, a_sem,
+    x_send, x_recv, own_sem, ag_send, ag_recv, fg_send, fg_recv, v_send, v_recv, u_send, u_recv,
+    *rest,
 ):
     p = Place(n, nf)
-    c, f = p.c, p.f
-    rows = dwsend.shape[2]
+    c, f, zlen, hpd, tile = p.c, p.f, p.zlen, lay.hpd, lay.tile
+    dob, reduce_scratch = rest[:hpd], rest[hpd:]
+    rows = D // nf
     part = rows // 2
-    load = pltpu.make_async_copy(sums_ref, sums, sums_sem)
-    load.start()
+    loads = Loads(ld_sem)
+    ffn_rows = [abuf.at[1, pl.ds(i * 2 * BLK, 2 * BLK)] for i in range(3)]
+    ffn_loads = [loads.start(src, wide.at[m]) for m, src in enumerate((ot_t_in, bt_in, zt_in))]
+    ffn_loads += [loads.start(src, dst) for src, dst in zip((gb_in, du_in, cot_in), ffn_rows)]
+    att_loads = [
+        loads.start(src, dst) for src, dst in zip(
+            (qraw_in, qst_in, kt_in, vt_in, kn_in, ot_in, lse_in), (qraw, qst, kt, vt, kn, ot, lse))
+    ]
+    row_loads = [loads.start(x_in, x_ref), loads.start(dh_in, dh_ref)]
     p.greet_all(True)
-    swap = Swap(p, msg, back, sw_send, sw_recv, sw_own)
-    swap.start()
-    result = reduce_scratch[0]
+
+    do_swaps = [
+        Swap(p, lambda d, u=u: gt.at[d, u], lambda d, u=u: dob[u].at[d],
+             do_send.at[u], do_recv.at[u], do_own.at[u])
+        for u in range(hpd)
+    ]
+    for swap in do_swaps:
+        swap.start()
+
+    def tg_copy(s):
+        return pltpu.make_async_remote_copy(
+            src_ref=got_ref.at[s], dst_ref=tg_out.at[s], send_sem=tg_send.at[s], recv_sem=tg_recv.at[s],
+            device_id=(p.twin, f), device_id_type=MESH,
+        )
+
+    for s in range(nf - 1):
+        tg_copy(s).start()
+
+    height = sums.shape[1]
+    flat = 3 * part
+    if height > flat:
+        for source in range(nf):
+            sums[source, flat:, :] = jnp.zeros((height - flat, D), BF16)
+    for copy in ffn_loads:
+        copy.wait()
+    theirs = lambda source: pl.ds(al(source * flat, 16), flat)
+    got = lambda source: pl.ds(al((nf + source) * flat, 16), flat)
+
+    def weight_grads(source, half, put):
+        for m in range(3):
+            @pl.loop(0, D // WIDE)
+            def _(j):
+                sl = pl.ds(al(j * WIDE, WIDE), WIDE)
+                where = pl.ds(al(source * rows + half * part, 16), part)
+                put(m, sl, dot(wide[m, where, :], ffn_rows[m][:, sl]).astype(BF16))
+
+    def twin_copy(s, source):
+        return pltpu.make_async_remote_copy(
+            src_ref=big.at[theirs(source)], dst_ref=big.at[got(source)],
+            send_sem=tw_send.at[s], recv_sem=tw_recv.at[s],
+            device_id=(p.twin, f), device_id_type=MESH,
+        )
+
+    shards = list(enumerate(p.fpeers)) + [(nf - 1, f)]
+    for s, source in shards:
+        def put(m, sl, value, source=source):
+            big[pl.ds(al(source * flat + m * part, 16), part), sl] = value
+        weight_grads(source, 1 - p.core, put)
+        twin_copy(s, source).start()
     reduce = Reduce(p, sums, *reduce_scratch[:6], reduce_scratch[6:])
-    load.wait()
-    reduce.start_x()
-
-    if hpd == 2:
-        a_copy = pltpu.make_async_copy(a_ref, abuf, a_sem)
-    else:
-        a_copy = pltpu.make_async_copy(a_ref.at[:, pl.ds(c % 2, 1)], abuf, a_sem)
-    a_copy.start()
-    w_copies = []
+    for s, source in shards:
+        def put(m, sl, value, source=source):
+            sums[source, pl.ds(m * part, part), sl] = value
+        weight_grads(source, p.core, put)
+        twin_copy(s, source).wait_recv()
+        reduce.add(
+            sums.at[source, pl.ds(0, flat)],
+            [sums.at[source, pl.ds(0, flat)], big.at[got(source)]], flat)
+        if s == max(nf - 2, 0):
+            for t in range(zlen - 1):
+                reduce.start_x(t)
+    for s, source in shards:
+        twin_copy(s, source).wait_send()
+
+    for s in range(nf - 1):
+        tg_copy(s).wait_recv()
+    w_loads = []
     for m in range(3):
-        def put(src, source, half):
-            at = pl.ds(al(source * rows + half * part, 16), part)
-            w_copies.append(pltpu.make_async_copy(src, w.at[m, at], w_sem.at[len(w_copies)]))
-        put(mine_ref.at[m], f, p.core)
-        put(other_ref.at[m], f, 1 - p.core)
+        def load_w(src, source, half, m=m):
+            at = pl.ds(al(m * D + source * rows + half * part, 16), part)
+            w_loads.append(loads.start(src, big.at[at]))
+        load_w(mine_ref.at[m], f, p.core)
+        load_w(other_ref.at[m], f, 1 - p.core)
         for s, source in enumerate(p.fsources):
-            put(got_ref.at[s, m], source, p.core)
-            put(tgot_ref.at[s, m], source, 1 - p.core)
-    for copy in w_copies:
-        copy.start()
-
-    for d in range(n):
-        for i in range(hpd):
-            left[:, pl.ds((d * hpd + i) * BLK, BLK)] = msg[d, :, i].reshape(3 * HD, BLK)
-    a_copy.wait()
-    depth = n * hpd * BLK
-    @pl.loop(0, D // WIDE)
-    def _(j):
-        sl = pl.ds(al(j * WIDE, WIDE), WIDE)
-        dw[:, sl] = dot(left[...], abuf[:, :, :, sl].reshape(depth, WIDE))
+            load_w(got_ref.at[s, m], source, p.core)
+            load_w(tg_out.at[s, m], source, 1 - p.core)
+
+    for copy in att_loads:
+        copy.wait()
+    ends = read_ends(len_ref)
+    part_sums[...] = jnp.zeros_like(part_sums)
+    step = 8
+    steps = [(u, q) for u in range(hpd) for q in range(n // step)]
+
+    def a_copy(k):
+        u, q = steps[k]
+        half = lay.half(u)
+        return pltpu.make_async_copy(
+            a_ref.at[pl.ds(q * step, step), half], abuf.at[k % 2].reshape(step, BLK, D), a_sem.at[k % 2])
+
+    def weights_of_head(k):
+        u, q = steps[k]
+        a_copy(k).wait()
+        if k + 1 < len(steps):
+            a_copy(k + 1).start()
+        @pl.loop(0, D // WIDE)
+        def _(j):
+            sl = pl.ds(al(j * WIDE, WIDE), WIDE)
+            term = dot(left[u, :, q * step * BLK : (q + 1) * step * BLK], abuf[k % 2, :, sl])
+            dw[:, sl] = term if k == 0 else dw[:, sl] + term
+
+    def gradient_swap(u):
+        return Swap(
+            p, lambda d: left.at[u, :, pl.ds(al(d * BLK, BLK), BLK)], lambda d: back.at[u, d],
+            dq_send.at[u], dq_recv.at[u], dq_own.at[u])
+
+    a_copy(0).start()
+    for u in range(hpd):
+        base = lay.base(u)
+        row0 = u * lay.size
+        do_swaps[u].wait()
+
+        @pl.loop(0, lay.half_blocks)
+        def _(b):
+            cols = pl.ds(al(b * BLK, BLK), BLK)
+            here = pl.ds(al(row0 + b * BLK, BLK), BLK)
+            block = dob[u][inv_ref[b + lay.half(u) * lay.half_blocks]].astype(F32)
+            delta[:, cols] = jnp.sum(block * ot[:, here], axis=0, keepdims=True)
+            block = pad_rows(block)
+            dost[:, cols] = block.astype(BF16)
+            don[cols, :] = block.T.astype(BF16)
+            qn[cols, :] = qst[:, here].astype(F32).T.astype(BF16)
+            vn[cols, :] = pad_rows(vt[:, here].astype(F32)).T.astype(BF16)
+            dk[cols, :] = jnp.zeros((BLK, BLK), F32)
+            dv[cols, :] = jnp.zeros((BLK, BLK), F32)
+
+        @pl.loop(0, lay.size // tile)
+        def _(qi):
+            cols = pl.ds(al(qi * tile, tile), tile)
+            here = pl.ds(al(row0 + qi * tile, tile), tile)
+            t_row = qi * tile + lax.broadcasted_iota(jnp.int32, (1, tile), 1)
+            start = seq_start(ends, base, t_row)
+            dqt[:, cols] = jnp.zeros((HD, tile), F32)
+
+            @pl.loop(0, qi + 1)
+            def _(j):
+                keys = pl.ds(al(j * tile, tile), tile)
+                keys_here = pl.ds(al(row0 + j * tile, tile), tile)
+                s = dot(kn[keys_here, :], qst[:, here])
+                token = j * tile + lax.broadcasted_iota(jnp.int32, (tile, 1), 0)
+                seen = (token >= start) & (token <= t_row)
+                prob = jnp.exp(jnp.where(seen, s - lse[:, here], NEG))
+                dp = dot(vn[keys, :], dost[:, cols])
+                ds = (prob * (dp - delta[:, cols])).astype(BF16)
+                dv[keys, :] += dot(prob.astype(BF16), don[cols, :])
+                dk[keys, :] += dot(ds, qn[cols, :])
+                dqt[:, cols] += dot(kt[:, keys_here], ds)
+
+            if u == hpd - 1:
+                @pl.when(qi == lay.size // tile // 2 - 1)
+                def _():
+                    if hpd == 1:
+                        reduce.xy(0)
+                    reduce.after_y(0)
+                    reduce.chain(0, 0)
+
+        @pl.loop(0, lay.half_blocks)
+        def _(b):
+            cols = pl.ds(al(b * BLK, BLK), BLK)
+            here = pl.ds(al(row0 + b * BLK, BLK), BLK)
+            dqs = dqt[:, cols]
+            dq = (dqs * c_ref[...]).astype(BF16)
+            dkt = dk[cols, :].T[:HD].astype(BF16)
+            dvt = dv[cols, :].T[:HD].astype(BF16)
+            natural[b, 0:HD] = dq
+            natural[b, HD : 2 * HD] = dkt
+            natural[b, 2 * HD : 3 * HD] = dvt
+            part_sums[0, :HD] += dqs * qraw[:, here]
+            part_sums[1, :HD] += dq.astype(F32)
+            part_sums[2, :HD] += dvt.astype(F32)
+
+        @pl.loop(0, n)
+        def _(d):
+            left[u, :, pl.ds(al(d * BLK, BLK), BLK)] = natural[rel_ref[2 * d + lay.half(u)]]
+
+        gradient_swap(u).start()
+        if u < hpd - 1:
+            reduce.xy(0)
+            for k, (unit, _) in enumerate(steps):
+                if unit == u:
+                    weights_of_head(k)
+    reduce.xy(1)
+
+    for k, (unit, _) in enumerate(steps):
+        if unit == hpd - 1:
+            weights_of_head(k)
     for source in range(nf):
         dwsend[source] = dw[:, source * rows : (source + 1) * rows].astype(BF16)
 
@@ -1044,60 +1043,93 @@
 
     for s, peer in enumerate(p.fpeers):
         x_copy(s, peer).start()
-    total = dwsend[f].astype(F32)
-    for s, peer in enumerate(p.fpeers):
-        x_copy(s, peer).wait_recv()
-        total = total + dwrecv[s].astype(F32)
-    dwown[...] = total.astype(BF16)
-    own = pltpu.make_async_copy(dwown, dw_out.at[c], own_sem)
-    own.start()
-    own.wait()
-    spread = Spread(p, dw_out, ag_send, ag_recv, 1)
-    spread.start(0)
-
-    zlen = p.zlen
-    for t in range(2 * zlen - 1):
+    reduce.start_x(zlen - 1)
+
+    spread = Spread(p, dw_out, ag_send, ag_recv, 3)
+    spread2 = Spread(p, fw_out, fg_send, fg_recv, fw_out.shape[1])
+
+    def start_spread():
+        total = dwsend[f].astype(F32)
+        for s, peer in enumerate(p.fpeers):
+            x_copy(s, peer).wait_recv()
+            total = total + dwrecv[s].astype(F32)
+        for i in range(3):
+            dwown[i] = total[i * HD : (i + 1) * HD].astype(BF16)
+        own = pltpu.make_async_copy(dwown, dw_out.at[c], own_sem)
+        own.start()
+        own.wait()
+        for i in range(3):
+            spread.start(i)
+
+    for t in range(2, 2 * zlen - 1):
         if t < zlen:
             reduce.xy(t)
-        if 1 <= t <= zlen:
+        if t <= zlen:
             reduce.after_y(t - 1)
             reduce.chain(t - 1, 0)
         for hop in range(1, zlen - 1):
             if 0 <= t - 1 - hop < zlen:
                 reduce.chain(t - 1 - hop, hop)
-        if 1 <= t < zlen:
-            spread.chain(t, 0)
-            spread.pair(t - 1, 0)
+        if t == 2:
+            start_spread()
+        if 1 <= t - 2 < zlen:
+            for i in range(3):
+                spread.chain(t - 2, i)
+                spread.pair(t - 3, i)
     reduce.last()
-    own = pltpu.make_async_copy(result, fw_out.at[c], own_sem)
-    own.start()
-    own.wait()
-    spread2 = Spread(p, fw_out, fg_send, fg_recv, 1)
-    spread2.start(0)
-
-    swap.wait()
+    result = reduce_scratch[0]
+    pieces = fw_out.shape[1]
+    own = [
+        pltpu.make_async_copy(result.at[pl.ds(i * (height // zlen // pieces), height // zlen // pieces)],
+                              fw_out.at[c, i], own_sem)
+        for i in range(pieces)
+    ]
+    for i in range(pieces):
+        own[i].start()
+        own[i].wait()
+        spread2.start(i)
+    done = max(2 * zlen - 4, 0)
+    for k in range(1, zlen):
+        if k > min(done, zlen - 1):
+            for i in range(3):
+                spread.chain(k, i)
+                spread.pair(k - 1, i)
+
+    for u in range(hpd):
+        gradient_swap(u).wait()
     for m in range(3):
         for i in range(2):
             for h in range(H):
-                block = back[h, m, i] if hpd == 2 else back[2 * h + i, m, 0]
-                wide[m, pl.ds(h * HD, HD), pl.ds(i * BLK, BLK)] = block
-    for copy in w_copies:
+                block = back[i, h] if hpd == 2 else back[0, 2 * h + i]
+                wide[m, pl.ds(h * HD, HD), pl.ds(i * BLK, BLK)] = block[m * HD : (m + 1) * HD]
+    for copy in w_loads:
         copy.wait()
 
     @pl.loop(0, D // WIDE)
     def _(j):
-        sl = pl.ds(al(j * WIDE, WIDE), WIDE)
-        total = dot(w[0, sl, :], wide[0]) + dot(w[1, sl, :], wide[1]) + dot(w[2, sl, :], wide[2])
-        dat[:, sl] = total.T
+        def rows_of(m):
+            return big[pl.ds(al(m * D + j * WIDE, WIDE), WIDE), :]
+        total = dot(rows_of(0), wide[0]) + dot(rows_of(1), wide[1]) + dot(rows_of(2), wide[2])
+        gx_out[:, pl.ds(al(j * WIDE, WIDE), WIDE)] = total.T
+
+    for i in range(3):
+        spread.pair(zlen - 1, i)
+    for i in range(pieces):
+        spread2.chain(1, i)
+        spread2.pair(0, i)
+    for copy in row_loads:
+        copy.wait()
     x = x_ref[...].astype(F32)
     r1 = lax.rsqrt(jnp.mean(x * x, axis=-1, keepdims=True) + EPS)
     na = x * r1
-    da = dat[...]
+    da = gx_out[...]
     dg1 = jnp.sum(da * na, axis=0, keepdims=True)
     for r in range(D // BLK):
         vx[f, r : r + 1, :] = dg1[:, r * BLK : (r + 1) * BLK]
         vx[f, D // BLK + r : D // BLK + r + 1, :] = dg2_ref[:, r * BLK : (r + 1) * BLK]
-    vx[f, 20:24, :] = small_ref[0:4, :]
+    for r in range(3):
+        vx[f, 20 + r : 21 + r, :] = jnp.sum(part_sums[r].T, axis=0, keepdims=True)
+    vx[f, 23:24, :] = jnp.zeros((1, BLK), F32)
 
     def v_copy(s, peer, source):
         return pltpu.make_async_remote_copy(
@@ -1125,59 +1157,79 @@
 
     for s in range(1, n):
         u_copy(s, c).start()
-    spread.pair(p.zlen - 1, 0)
-    for k in range(1, zlen):
-        spread2.chain(k, 0)
-        spread2.pair(k - 1, 0)
-    spread2.pair(zlen - 1, 0)
-    for k in range(p.zlen):
+    for k in range(2, zlen):
+        for i in range(pieces):
+            spread2.chain(k, i)
+            spread2.pair(k - 1, i)
+    for i in range(pieces):
+        spread2.pair(zlen - 1, i)
+    for k in range(zlen):
         for zz, guard, _ in p.level(k):
             when(guard, lambda zz=zz: spread.from_twin(zz))
             when(guard, lambda zz=zz: spread2.from_twin(zz))
     for s in range(1, n):
         u_copy(s, (c + n - s) % n).wait_recv()
     vec_out[...] = vall[...]
-    swap.drain()
+
+    for u in range(hpd):
+        do_swaps[u].drain()
+        gradient_swap(u).drain()
     spread.drain()
     spread2.drain()
     reduce.drain()
     for s, peer in enumerate(p.fpeers):
+        tg_copy(s).wait_send()
         x_copy(s, peer).wait_send()
         v_copy(s, peer, f).wait_send()
     for s in range(1, n):
         u_copy(s, c).wait_send()
 
 
-def finish(n, nf, hpd, msg, tokens, sums, mine, other, got, tgot, x, dh, g1, dg2, small):
+def backward(lay, nf, within, inverse, lengths, gt, factor, g1, dg2, ffn_parts, cot, kept, tokens, mine, other, got, x, dh):
+    n, hpd, rows, size = lay.n, lay.hpd, lay.rows, lay.size
     dma = pltpu.SemaphoreType.DMA
-    rows = D // nf
+    shard = D // nf
+    part = shard // 2
+    zlen = n // 4
+    height = -(-3 * part // (16 * zlen)) * 16 * zlen
+    piece = height // zlen
+    pieces = 3 if piece % 48 == 0 else 1
     peers = max(nf - 1, 1)
     tok = x.shape[0]
     return pl.pallas_call(
-        functools.partial(finish_kernel, n, nf, hpd),
+        functools.partial(backward_kernel, lay, n, nf),
         out_shape=(
             jax.ShapeDtypeStruct((tok, D), F32),
-            jax.ShapeDtypeStruct((n, 3 * HD, rows), BF16),
-            jax.ShapeDtypeStruct((n, sums.shape[1] * 4 // n, D // 2), BF16),
+            jax.ShapeDtypeStruct((n, 3, HD, shard), BF16),
+            jax.ShapeDtypeStruct((n, pieces, piece // pieces, D // 2), BF16),
             jax.ShapeDtypeStruct((n, VEC_ROWS, BLK), F32),
+            jax.ShapeDtypeStruct((peers, 3, part, D), BF16),
         ),
-        in_specs=[in_vmem()] + [in_any()] * 6 + [in_vmem()] * 5,
-        out_specs=(in_vmem(), in_any(), in_any(), in_vmem()),
+        in_specs=[in_smem()] * 3 + [in_vmem()] * 4 + [in_any()] * 19,
+        out_specs=(in_vmem(), in_any(), in_any(), in_vmem(), in_any()),
         scratch_shapes=[
-            VMEM(msg.shape, BF16), VMEM((n, hpd, BLK, D), BF16), VMEM((3 * HD, n * hpd * BLK), BF16),
-            VMEM((3 * HD, D), F32), VMEM((nf, 3 * HD, rows), BF16), VMEM((peers, 3 * HD, rows), BF16),
-            VMEM((3 * HD, rows), BF16), VMEM((3, D, D), BF16), VMEM((3, D, tok), BF16), VMEM((tok, D), F32),
+            VMEM((3 * D, D), BF16), VMEM((nf, height, D), BF16), VMEM((3, D, tok), BF16),
+            VMEM((2, 8 * BLK, D), BF16),
+            VMEM((HD, rows), F32), VMEM((BLK, rows), BF16), VMEM((HD, rows), BF16), VMEM((HD, rows), BF16),
+            VMEM((rows, BLK), BF16), VMEM((HD, rows), F32), VMEM((1, rows), F32),
+            VMEM((tok, D), BF16), VMEM((tok, D), F32),
+            VMEM((size, BLK), BF16), VMEM((size, BLK), BF16), VMEM((size, BLK), BF16), VMEM((BLK, size), BF16),
+            VMEM((1, size), F32), VMEM((size, BLK), F32), VMEM((size, BLK), F32), VMEM((HD, size), F32),
+            VMEM((size // BLK, 3 * HD, BLK), BF16), VMEM((3, BLK, BLK), F32), VMEM((hpd, 3 * HD, n * BLK), BF16),
+            VMEM((hpd, n, 3 * HD, BLK), BF16), VMEM((3 * HD, D), F32), VMEM((nf, 3 * HD, shard), BF16),
+            VMEM((peers, 3 * HD, shard), BF16), VMEM((3, HD, shard), BF16),
             VMEM((nf, VEC_ROWS, BLK), F32), VMEM((VEC_ROWS, BLK), F32), VMEM((n, VEC_ROWS, BLK), F32),
-            dma((n,)), dma((n,)), dma, dma, dma((6 * nf,)), dma((peers,)), dma((peers,)), dma,
-            dma((4, n, 1)), dma((n, 1)), dma((peers,)), dma((peers,)), dma((n,)), dma((n,)),
-            dma((4, n, 1)), dma((n, 1)), dma, VMEM(sums.shape, BF16),
-        ] + Reduce.scratch(nf, n // 4, sums.shape[1]),
+            dma((15 + 6 * nf,)), dma((hpd, n)), dma((hpd, n)), dma((hpd,)), dma((hpd, n)), dma((hpd, n)), dma((hpd,)),
+            dma((nf,)), dma((nf,)), dma((peers,)), dma((peers,)), dma((2,)),
+            dma((peers,)), dma((peers,)), dma, dma((4, n, 3)), dma((n, 3)), dma((4, n, pieces)), dma((n, pieces)),
+            dma((peers,)), dma((peers,)), dma((n,)), dma((n,)),
+        ] + [VMEM((n, HD, BLK), BF16)] * hpd + Reduce.scratch(nf, zlen, height),
         compiler_params=pltpu.CompilerParams(
-            collective_id=3, has_side_effects=True, vmem_limit_bytes=60 * MIB
+            collective_id=2, has_side_effects=True, vmem_limit_bytes=62 * MIB
         ),
-        cost_estimate=cost(60),
-        name="finish",
-    )(msg, tokens, sums, mine, other, got, tgot, x, dh, g1, dg2, small)
+        cost_estimate=cost(130),
+        name="backward",
+    )(within, inverse, lengths, gt, factor, g1, dg2, *ffn_parts, cot, *kept, tokens, mine, other, got, x, dh)
 
 
 def turn_kernel(hpd, dw_ref, q_ref, k_ref, v_ref, wide):
@@ -1187,11 +1239,10 @@
     def _():
         for m in range(3):
             for h in range(H):
-                at = pl.ds(m * HD, HD)
                 if hpd == 2:
-                    block = dw_ref[h, at, :].astype(F32)
+                    block = dw_ref[h, m].astype(F32)
                 else:
-                    block = dw_ref[2 * h, at, :].astype(F32) + dw_ref[2 * h + 1, at, :].astype(F32)
+                    block = dw_ref[2 * h, m].astype(F32) + dw_ref[2 * h + 1, m].astype(F32)
                 wide[m, pl.ds(h * HD, HD), :] = block
 
     for m, out in enumerate((q_ref, k_ref, v_ref)):
@@ -1199,16 +1250,16 @@
 
 
 def turn(hpd, dw):
-    n, _, rows = dw.shape
+    n, _, _, rows = dw.shape
     spec = pl.BlockSpec((rows, WIDE), lambda j: (0, j))
     return pl.pallas_call(
         functools.partial(turn_kernel, hpd),
         grid=(D // WIDE,),
         out_shape=tuple([jax.ShapeDtypeStruct((rows, D), F32)] * 3),
-        in_specs=[pl.BlockSpec((n, 3 * HD, rows), lambda j: (0, 0, 0))],
+        in_specs=[pl.BlockSpec((n, 3, HD, rows), lambda j: (0, 0, 0, 0))],
         out_specs=(spec, spec, spec),
         scratch_shapes=[VMEM((3, D, rows), F32)],
-        compiler_params=pltpu.CompilerParams(vmem_limit_bytes=48 * MIB),
+        compiler_params=pltpu.CompilerParams(vmem_limit_bytes=60 * MIB),
         cost_estimate=cost(6),
         name="turn",
     )(dw)
@@ -1227,7 +1278,8 @@
 
 
 def widen(zlen, part, pieces):
-    height, half = pieces.shape[1:]
+    half = pieces.shape[-1]
+    height = pieces.shape[1] * pieces.shape[2]
     spec = pl.BlockSpec((part, half), lambda j, y: (j, y))
     return pl.pallas_call(
         functools.partial(widen_kernel, zlen, part),
@@ -1235,7 +1287,7 @@
         out_shape=tuple([jax.ShapeDtypeStruct((2 * part, D), F32)] * 3),
         in_specs=[pl.BlockSpec((zlen, 2, 2, height, half), lambda j, y: (0, 0, 0, 0, 0))],
         out_specs=(spec, spec, spec),
-        compiler_params=pltpu.CompilerParams(vmem_limit_bytes=48 * MIB),
+        compiler_params=pltpu.CompilerParams(vmem_limit_bytes=60 * MIB),
         cost_estimate=cost(5),
         name="widen",
     )(pieces.reshape(zlen, 2, 2, height, half))
@@ -1278,24 +1330,20 @@
     bias = jnp.broadcast_to(bias[:, None], (3 * HD, BLK))
     factor_col = jnp.broadcast_to(factor[:, None], (HD, BLK))
 
-    twins = [(i, i ^ 1) for i in range(n)]
     got = jnp.stack([
         lax.ppermute(mine, "fsdp", [(i, (i + s) % nf) for i in range(nf)]) for s in range(1, nf)
     ])
-    tgot = lax.ppermute(got, "ctx", twins)
 
     ot, *kept = attend(lay, deal, lengths, qkv, bias, factor_col)
     ot = swap_out(n, nf, ot).reshape(H, 2, HD, BLK)
     layer_out, dh, gt, ott, bt, zt, gb, du, dg2 = ffn(x, cot, ot, g2[None], mats)
-    gt, sums = swap_grad(n, nf, gt.reshape(n, lay.hpd, HD, BLK), ott, bt, zt, gb, du, cot)
-
     part = rows // 2
     zlen = n // 4
-    sums = jnp.pad(sums.reshape(nf, 3 * part, D), ((0, 0), (0, -3 * part % (16 * zlen)), (0, 0)))
-
-    msg, small = attend_back(lay, deal, lengths, gt, kept, factor_col)
-    grad_x, dw, pieces, vectors = finish(
-        n, nf, lay.hpd, msg, a_all, sums, mine, other, got, tgot, x, dh, g1[None], dg2, small
+    blocks = jnp.arange(deal.shape[0], dtype=jnp.int32)
+    inverse = jnp.sum(jnp.where(deal[None, :] == blocks[:, None], blocks[None, :] // 2, 0), axis=1, dtype=jnp.int32)
+    grad_x, dw, pieces, vectors, _ = backward(
+        lay, nf, deal % lay.half_blocks, inverse, lengths, gt.reshape(n, lay.hpd, HD, BLK), factor_col, g1[None], dg2,
+        (ott, bt, zt, gb, du), cot, kept, a_all, mine, other, got, x, dh,
     )
     dwq, dwk, dwv = turn(lay.hpd, dw)
     grads = widen(zlen, part, pieces)

time: 445 us -> 324 us (0.73)
  waiting for transfers between devices: 54.3 us -> 0.01 us
  Pallas kernels: 354 us -> 302 us
  local copies, waits for them, and re-layouts: 24.5 us -> 10.4 us
    pallas_call x3 -> x1, Pallas kernels: 218 us -> 160 us  [backward(): pl.pallas_call(functools.partial(backward_kernel, lay, n, nf), out_shape=...]
    ppermute x1, waiting for transfers between devices: 54.3 us -> 0.01 us  [local(): lax.ppermute(mine, 'fsdp', [(i, (i + s) % nf) for i in range(nf)])]
    unnamed x29 -> x5, local copies, waits for them, and re-layouts: 15.1 us -> 1.06 us
  transfers between devices with their start and end apart: 2 -> 1, of which waited for: 1 -> 0; matrix products, arithmetic and copies ran while one was open for 1% -> 2% of each run, Pallas kernels for 23% -> 17%
where the time goes in v3:
time: 324 us; the launch traced here: 323 us
  Pallas kernels  302 us (93%)
  local copies, waits for them, and re-layouts  10.4 us (3%)
  other arithmetic  8.91 us (3%)
    pallas_call x1, Pallas kernels, backward(): pl.pallas_call(functools.partial(backward_kernel, lay, n, nf), out_shape=...  160 us
    pallas_call x1, Pallas kernels, gather(): pl.pallas_call(functools.partial(gather_kernel, n, nf), out_shape=(jax.Sh...  72.7 us
    pallas_call x1, Pallas kernels, attend(): pl.pallas_call(functools.partial(fwd_kernel, lay), out_shape=(jax.ShapeDt...  19.2 us
    pallas_call x1, Pallas kernels, ffn(): pl.pallas_call(ffn_kernel, out_shape=(plain, jax.ShapeDtypeStruct((tok, D...  19.1 us
    pallas_call x1, Pallas kernels, swap_out(): pl.pallas_call(functools.partial(swap_kernel, n, nf), out_shape=jax.Shape...  16.5 us
    pallas_call x1, Pallas kernels, turn(): pl.pallas_call(functools.partial(turn_kernel, hpd), grid=(D // WIDE,), ou...  8.01 us
  transfers between devices with their start and end apart: 1, of which 0 were waited for; matrix products, arithmetic and copies ran while one was open for 2% of the time, Pallas kernels for 17%

profile of v3, /device:TPU:0, one launch (start us, length us, event | category | flops | bytes accessed | tf_op | source)
XLA Modules:
  0.0 323.3 jit_solution(14423429939149425454)
XLA Ops:
  0.7 0.7 convert_element_type.15
  1.4 0.7 convert_element_type.28
  2.1 0.7 convert_element_type.29
  2.8 0.7 convert_element_type.30
  3.4 0.7 convert_element_type.31
  4.2 0.6 pad_convert_fusion.vec_ref
  4.8 1.2 dynamic-slice_convert_fusion.2
  6.0 1.5 dynamic-slice_convert_fusion
  7.4 0.9 fusion.4.wh_ref
  8.4 72.7 %gather_tokens.1 = (bf16[16,2,128,1280]{3,2,1,0:T(8,128)(2,1)}, f32[16,240,256]{2,1,0:T(8,128)}, bf16[3,1280,1280]{2,1,0:T(8,128)(2,1)}, f32[2,8,640]{2,1,0:T(8,...) custom-call(bf16[256,1280]{1,0:T(8,128)(2,1)} %bitcast.14, bf16[640,256]{1,0:T(8,128)(2,1)} %fusion.4.wh_ref, ...), custom_call_target="tpu_custom_call" | custom-call | bytes 180000000 | tf_op jit(solution)/shard_map/gather_tokens/pallas_call | solution.py:486
  81.1 1.6 collective-permute-start
  82.7 0.8 slice_bitcast_fusion
  83.5 0.6 fusion.6
  84.1 0.1 dynamic_slice.34
  84.2 0.1 dynamic_slice.33
  84.3 0.7 divide_reduce_fusion
  85.0 0.1 mul.38
  85.1 0.1 pad_maximum_fusion
  85.2 0.8 broadcast_in_dim.42.bias_ref
  85.9 0.7 broadcast_in_dim.43.c_ref
  86.6 19.2 %attend.1 = (bf16[16,2,80,128]{3,2,1,0:T(8,128)(2,1)}, f32[80,4096]{1,0:T(8,128)}, bf16[128,4096]{1,0:T(8,128)(2,1)}, bf16[80,4096]{1,0:T(8,128)(2,1)}, bf16[80,...) custom-call(s32[32]{0:T(128)} %deal_ref.1, s32[1,8]{1,0:T(1,128)} %len_ref.3, ...), custom_call_target="tpu_custom_call" | custom-call | bytes 57000000 | tf_op jit(solution)/shard_map/attend/pallas_call | solution.py:685
  105.8 16.5 %swap_out.1.ot_ref = bf16[16,2,80,128]{3,2,1,0:T(8,128)(2,1)} custom-call(bf16[16,2,80,128]{3,2,1,0:T(8,128)(2,1)} %get-tuple-element.48.src), custom_call_target="tpu_custom_call" | custom-call | bytes 45000000 | tf_op jit(solution)/shard_map/swap_out/pallas_call | solution.py:560
  122.3 0.1 div.25
  122.4 0.0 copy-start.1
  122.4 19.1 %feed_forward.1 = (bf16[256,1280]{1,0:T(8,128)(2,1)}, f32[256,1280]{1,0:T(8,128)}, bf16[16,2,80,128]{3,2,1,0:T(8,128)(2,1)}, bf16[1280,256]{1,0:T(8,128)(2,1)}, ...) custom-call(bf16[256,1280]{1,0:T(8,128)(2,1)} %bitcast.15, ...), custom_call_target="tpu_custom_call" | custom-call | bytes 60000000 | tf_op jit(solution)/shard_map/feed_forward/pallas_call | solution.py:784
  141.4 0.0 copy-done.1
  141.4 0.5 and_select_fusion
  142.0 0.6 select_reduce_fusion.inv_ref
  142.6 0.0 collective-permute-done
  142.6 160.0 %backward.1 = (f32[256,1280]{1,0:T(8,128)}, bf16[16,3,80,640]{3,2,1,0:T(8,128)(2,1)}, bf16[16,3,80,640]{3,2,1,0:T(8,128)(2,1)}, f32[16,24,128]{2,1,0:T(8,128)}, bf16[1,3,320,1280]{3,2,1,0:T(8,128)(2,1)}) custom-call(s32[32]{0:T(128)} %get-tuple-element.93.rel_ref, s32[32]{0:T(128)} %select_reduce_fusion.inv_ref, s32[1,8]{1,0:T(1,128)} %len_ref.3, ...), custom_call_target="tpu_custom_call" | custom-call | bytes 390000000 | tf_op jit(solution)/shard_map/backward/pallas_call | solution.py:1199
  302.6 1.0 slice_reduce_fusion
  303.6 1.0 slice_reduce_fusion.1
  304.6 8.0 %turn.1 = (f32[640,1280]{1,0:T(8,128)}, f32[640,1280]{1,0:T(8,128)}, f32[640,1280]{1,0:T(8,128)}) custom-call(bf16[16,3,80,640]{3,2,1,0:T(8,128)(2,1)} %get-tuple-element.71.dw_ref), custom_call_target="tpu_custom_call" | custom-call | bytes 18000000 | tf_op jit(solution)/shard_map/turn/pallas_call | solution.py:1255
  312.6 0.0 copy-start
  312.6 0.1 reshape.110
  312.7 0.7 dynamic_slice.35
  313.4 0.7 dynamic_slice.36
  314.0 0.1 reshape.111
  314.1 0.7 dynamic_slice.37
  314.8 6.2 %widen.1 = (f32[640,1280]{1,0:T(8,128)}, f32[640,1280]{1,0:T(8,128)}, f32[640,1280]{1,0:T(8,128)}) custom-call(bf16[4,2,2,240,640]{4,3,2,1,0:T(8,128)(2,1)} %bitcast.17), custom_call_target="tpu_custom_call" | custom-call | bytes 15000000 | tf_op jit(solution)/shard_map/widen/pallas_call | solution.py:1284
  321.0 0.7 dynamic_slice.39
  321.7 0.6 dynamic_slice.38
  322.3 0.0 copy-done
  322.3 1.1 copy.29
  (12 shorter events, 0.1 us)
Async XLA Ops:
  81.1 61.5 %collective-permute-start = (bf16[3,320,1280]{2,1,0:T(8,128)(2,1)}, bf16[3,320,1280]{2,1,0:T(8,128)(2,1)}, u32[]{:S(2)}, u32[]{:S(2)}) collective-permute-start(bf16[3,320,1280]{2,1,0:T(8,128)(2,1)} %get-tuple-element.66.mine_ref), channel_id=1, source_target_pairs={{0,1},{1,0},{2,3},{3,2},{4,5},{5,4},{6,7},{7,6},{8,9},{9,8},{10,11... | collective-permute-start | bytes 7372808 | tf_op jit(solution)/shard_map/ppermute | solution.py:1334
  122.4 19.1 %copy-start.1 = (s32[32]{0:T(128)S(1)}, s32[32]{0:T(128)}, u32[]{:S(2)}) copy-start(s32[32]{0:T(128)} %deal_ref.1) | copy-start | bytes 388
  312.6 9.7 %copy-start = (f32[256,1280]{1,0:T(8,128)S(1)}, f32[256,1280]{1,0:T(8,128)}, u32[]{:S(2)}) copy-start(f32[256,1280]{1,0:T(8,128)} %get-tuple-element.69) | copy-start | bytes 3932164

commit v4 on v3

--- a/solution.py
+++ b/solution.py
@@ -148,10 +148,10 @@
                 self.send(3, origin, i)
             when(guard, body)
 
-    def from_twin(self, zz):
+    def from_twin(self, zz, pieces=None):
         p = self.p
         for yy in (p.y, 1 - p.y):
-            for i in range(self.pieces):
+            for i in range(self.pieces) if pieces is None else pieces:
                 self.arrive(p.idx(zz, yy, 1 - p.core), i)
 
     def drain(self):
@@ -311,23 +311,187 @@
             pl.when(p.z > piece)(lambda piece=piece: self.d_copy(piece).wait_send())
 
 
-def gather_kernel(
-    n, nf, x_ref, wh_ref, vec_ref, wo_ref, w1_ref, w2_ref, wq_ref, wk_ref, wv_ref,
-    a_out, qkv_out, mats_out, vecs_out, mine_out, other_out,
-    abuf, norm, whbuf, wht, vecbuf, g1_ref, stage, wcast,
-    ag_send, ag_recv, wh_send, wh_recv, vec_send, vec_recv,
-    ld_sem, own_sem, mx_send, mx_recv, ms_send, ms_recv, a_sem, keep_sem,
+class Loads:
+    def __init__(self, sems):
+        self.sems, self.copies = sems, []
+
+    def start(self, src, dst):
+        copy = pltpu.make_async_copy(src, dst, self.sems.at[len(self.copies)])
+        self.copies.append(copy)
+        copy.start()
+        return copy
+
+    def wait(self):
+        for copy in self.copies:
+            copy.wait()
+
+
+class Swap:
+    def __init__(self, place, src, dst, send_sem, recv_sem, own_sem):
+        self.p, self.src, self.dst = place, src, dst
+        self.send_sem, self.recv_sem, self.own_sem = send_sem, recv_sem, own_sem
+
+    def copy(self, s, block):
+        p = self.p
+        return pltpu.make_async_remote_copy(
+            src_ref=self.src((p.c + s) % p.n), dst_ref=self.dst(block),
+            send_sem=self.send_sem.at[s], recv_sem=self.recv_sem.at[s],
+            device_id=((p.c + s) % p.n, p.f), device_id_type=MESH,
+        )
+
+    def own(self):
+        return pltpu.make_async_copy(self.src(self.p.c), self.dst(self.p.c), self.own_sem)
+
+    def start(self):
+        for s in range(1, self.p.n):
+            self.copy(s, self.p.c).start()
+        self.own().start()
+
+    def wait(self):
+        self.own().wait()
+        for s in range(1, self.p.n):
+            self.copy(s, (self.p.c + self.p.n - s) % self.p.n).wait_recv()
+
+    def drain(self):
+        for s in range(1, self.p.n):
+            self.copy(s, self.p.c).wait_send()
+
+
+def seq_start(ends, base, token):
+    start = jnp.zeros_like(token)
+    for e in ends:
+        start = jnp.where(e - base <= token, jnp.maximum(start, e - base), start)
+    return start
+
+
+def read_ends(lengths_ref):
+    ends, total = [], jnp.int32(0)
+    for i in range(lengths_ref.shape[1]):
+        total = total + lengths_ref[0, i]
+        ends.append(total)
+    return ends
+
+
+def pad_rows(block):
+    return jnp.concatenate([block, jnp.zeros((BLK - HD, block.shape[1]), block.dtype)], axis=0)
+
+
+class Layout:
+    def __init__(self, n, total_blocks):
+        self.n = n
+        self.hpd = 2 * H // n
+        self.half_blocks = total_blocks // 2
+        self.size = self.half_blocks * BLK
+        self.rows = self.hpd * self.size
+        self.tile = 512
+
+    def half(self, i):
+        return i if self.hpd == 2 else lax.axis_index("ctx") % 2
+
+    def base(self, unit):
+        return self.half(unit) * self.size if self.hpd == 1 else unit * self.size
+
+
+WIDE = 256
+
+
+def over_columns(body):
+    @pl.loop(0, D // WIDE)
+    def _(j):
+        body(pl.ds(al(j * WIDE, WIDE), WIDE))
+
+
+def token_rows(
+    x_ref, cot_ref, oswap, rows_ref, weights, w_loads,
+    out_ref, dh_ref, gt_ref, ot, bt, zt, gb, du, dg2_ref,
+    o_rows, hidden, nh, b, up, z, db, wide,
 ):
+    wo, w1, w2 = weights
+    hpd = oswap.shape[1]
+    for i in range(2):
+        for h in range(H):
+            ot[pl.ds(h * HD, HD), pl.ds(i * BLK, BLK)] = oswap[h, i] if hpd == 2 else oswap[2 * h + i, 0]
+    @pl.loop(0, D // WIDE)
+    def _(j):
+        sl = pl.ds(al(j * WIDE, WIDE), WIDE)
+        o_rows[:, sl] = ot[sl, :].astype(F32).T.astype(BF16)
+
+    def body(sl):
+        hidden[:, sl] = x_ref[:, sl].astype(F32) + dot(o_rows[...], wo[:, sl])
+    over_columns(body)
+    hid = hidden[...]
+    r2 = lax.rsqrt(jnp.mean(hid * hid, axis=-1, keepdims=True) + EPS)
+    nh[...] = hid * r2
+    b[...] = (nh[...] * rows_ref[3:4, :]).astype(BF16)
+    w_loads[1].wait()
+
+    def body(sl):
+        u = dot(b[...], w1[:, sl])
+        up[:, sl] = u
+        z[:, sl] = (u * jax.nn.sigmoid(u)).astype(BF16)
+    over_columns(body)
+
+    w_loads[2].wait()
+
+    def body(sl):
+        out_ref[:, sl] = (hidden[:, sl] + dot(z[...], w2[:, sl])).astype(BF16)
+        dz = dot(cot_ref[...], w2[sl, :], NT)
+        u = up[:, sl]
+        sig = jax.nn.sigmoid(u)
+        du[:, sl] = (dz * sig * (1.0 + u * (1.0 - sig))).astype(BF16)
+    over_columns(body)
+
+    def body(sl):
+        g = dot(du[...], w1[sl, :], NT)
+        db[:, sl] = g * rows_ref[3:4, sl]
+        dg2_ref[:, sl] = jnp.sum(g * nh[:, sl], axis=0, keepdims=True)
+    over_columns(body)
+    scaled = db[...]
+    mean = jnp.mean(scaled * nh[...], axis=-1, keepdims=True)
+    dh = cot_ref[...].astype(F32) + r2 * (scaled - nh[...] * mean)
+    dh_ref[...] = dh
+    gb[...] = dh.astype(BF16)
+
+    @pl.loop(0, D // WIDE)
+    def _(j):
+        sl = pl.ds(al(j * WIDE, WIDE), WIDE)
+        wide[sl, :] = dot(wo[sl, :], gb[...], NT).astype(BF16)
+    for i in range(2):
+        for h in range(H):
+            gt_ref[h, i] = wide[pl.ds(h * HD, HD), pl.ds(i * BLK, BLK)]
+
+    @pl.loop(0, D // WIDE)
+    def _(j):
+        sl = pl.ds(al(j * WIDE, WIDE), WIDE)
+        bt[sl, :] = b[:, sl].astype(F32).T.astype(BF16)
+        zt[sl, :] = z[:, sl].astype(F32).T.astype(BF16)
+
+
+def forward_kernel(
+    lay, n, nf,
+    rel_ref, inv_ref, len_ref, x_ref, cot_ref, wh_ref, vec_ref, *rest,
+):
+    mat_refs, rest = rest[:6], rest[6:]
+    (a_out, mats_out, mine_out, other_out, rows_out, factor_out, dg2_out, *stored) = rest[: 7 + 15]
+    (abuf, norm, whbuf, wht, vecbuf, vcol, stage, wcast, qkv, osend, onat, oswap,
+     qraw, qst, kt, vt, kn, ot, lse, layer, dh, gt, ot_t, bt, zt, gb, du,
+     o_rows, hidden, nh, b_rows, up, z, db, wide, m_ref, l_ref, acc_ref,
+     ag_send, ag_recv, wh_send, wh_recv, vec_send, vec_recv,
+     ld_sem, mx_send, mx_recv, ms_send, ms_recv, a_sem, keep_sem, o_send, o_recv, o_own,
+     st_sem, w_sem) = rest[7 + 15 :]
+    kept = (qraw, qst, kt, vt, kn, ot, lse)
+    made = (layer, dh, gt, ot_t, bt, zt, gb, du)
+    stores = Loads(st_sem)
     p = Place(n, nf)
-    c, f, core, zlen = p.c, p.f, p.core, p.zlen
+    c, f, core, zlen, hpd, tile = p.c, p.f, p.core, p.zlen, lay.hpd, lay.tile
     rows = wh_ref.shape[0]
     part = rows // 2
-    p.greet_neighbours()
+    p.greet_all(True)
     spread = Spread(p, abuf, ag_send, ag_recv, 2)
 
     for i in range(2):
         abuf[c, i] = x_ref[pl.ds(i * BLK, BLK), :]
-        spread.start(i)
+    spread.start(0)
 
     def wh_copy(s, peer):
         return pltpu.make_async_remote_copy(
@@ -349,8 +513,9 @@
     whbuf[pl.ds(al(f * rows, 16), rows), :] = wh_ref[...]
     vecbuf[f] = vec_ref[...]
 
-    shards = (wo_ref, w1_ref, w2_ref, wq_ref, wk_ref, wv_ref)
-    steps = [(m, h) for h in range(2) for m in range(3)] + [(m, h) for h in range(2) for m in range(3, 6)]
+    shards = mat_refs
+    moved = len(mat_refs) - 1
+    steps = [(m, 0) for m in range(moved)] + [(m, 1) for m in range(moved)] + [(moved, 0), (moved, 1)]
 
     def half_of(h):
         return (core + h) % 2
@@ -371,7 +536,7 @@
         )
 
     def keep_copies(m):
-        if m < 3:
+        if m < moved:
             return [
                 pltpu.make_async_copy(
                     wcast.at[m, h], mats_out.at[m, pl.ds(al(f * rows + h * part, 16), part)],
@@ -379,7 +544,7 @@
                 ) for h in range(2)
             ]
         return [
-            pltpu.make_async_copy(wcast.at[m, half_of(h)], out.at[m - 3], keep_sem.at[m, h])
+            pltpu.make_async_copy(wcast.at[m, half_of(h)], out, keep_sem.at[m, h])
             for h, out in enumerate((mine_out, other_out))
         ]
 
@@ -394,7 +559,7 @@
             wcast[m, half_of(h), pl.ds(al(t * chunk, 16), chunk), :] = stage[
                 step % 2, pl.ds(al(t * chunk, 16), chunk), :
             ].astype(BF16)
-        if h == 0 and m < 3:
+        if h == 0 and m < moved:
             for s, peer in enumerate(p.fpeers):
                 mx_copy(m, s, peer, f).start()
         if h == 1:
@@ -404,37 +569,6 @@
     load(0).start()
     for step in range(len(steps)):
         cast(step)
-
-    for s, peer in enumerate(p.fpeers):
-        wh_copy(s, peer).wait_recv()
-        vec_copy(s, peer).wait_recv()
-    wht[...] = whbuf[...].astype(F32).T.astype(BF16)
-    vecs_out[...] = vecbuf[...]
-    for source in range(nf):
-        g1_ref[:, pl.ds(source * rows, rows)] = vecbuf[source, 0:1, 0:rows]
-
-    def a_copy(slot, origin):
-        return pltpu.make_async_copy(norm.at[slot], a_out.at[origin], a_sem.at[slot])
-
-    def project(slot, origin):
-        for i in range(2):
-            x = abuf[origin, i].astype(F32)
-            scale = lax.rsqrt(jnp.mean(x * x, axis=-1, keepdims=True) + EPS)
-            norm[slot, i] = (x * scale * g1_ref[...]).astype(BF16)
-        a_copy(slot, origin).start()
-        block = norm[slot].reshape(2 * BLK, D)
-        qkv_out[origin] = dot(wht[: 3 * HD, :], block, NT)
-
-    def compute(k):
-        for zz, guard, _ in p.level(k):
-            def body(zz=zz):
-                spread.from_twin(zz)
-                @pl.loop(0, 4)
-                def _(t):
-                    if k:
-                        a_copy(t, zz * 4 + t).wait()
-                    project(t, zz * 4 + t)
-            when(guard, body)
 
     def ms_copy(m, s, source, half):
         where = mats_out.at[m, pl.ds(al(source * rows + half * part, 16), part)]
@@ -449,372 +583,238 @@
             mx_copy(m, s, peer, source).wait_recv()
             ms_copy(m, s, source, core).start()
 
-    for k in range(1, zlen):
-        for i in range(2):
-            spread.chain(k, i)
-            spread.pair(k - 1, i)
-        compute(k - 1)
-        if k == 2:
-            pass_matrix(0)
-    for i in range(2):
-        spread.pair(zlen - 1, i)
-    pass_matrix(1)
-    compute(zlen - 1)
-    pass_matrix(2)
-
-    for m in range(6):
-        for copy in keep_copies(m):
-            copy.wait()
-    for m in range(3):
-        for s, (peer, source) in enumerate(zip(p.fpeers, p.fsources)):
-            mx_copy(m, s, peer, f).wait_send()
-            ms_copy(m, s, source, core).wait_send()
-            ms_copy(m, s, source, 1 - core).wait_recv()
     for s, peer in enumerate(p.fpeers):
-        wh_copy(s, peer).wait_send()
-        vec_copy(s, peer).wait_send()
-    spread.drain()
-    for slot in range(4):
-        a_copy(slot, slot).wait()
-
-
-def gather(n, nf, x, wh, vec, mats):
-    rows = wh.shape[0]
-    dma = pltpu.SemaphoreType.DMA
-    peers = max(nf - 1, 1)
-    half = jax.ShapeDtypeStruct((3, rows // 2, D), BF16)
-    return pl.pallas_call(
-        functools.partial(gather_kernel, n, nf),
-        out_shape=(
-            jax.ShapeDtypeStruct((n, 2, BLK, D), BF16),
-            jax.ShapeDtypeStruct((n, 3 * HD, 2 * BLK), F32),
-            jax.ShapeDtypeStruct((3, nf * rows, D), BF16),
-            jax.ShapeDtypeStruct((nf,) + vec.shape, F32),
-            half, half,
-        ),
-        in_specs=[in_vmem(), in_vmem(), in_vmem()] + [in_any()] * 6,
-        out_specs=(in_any(), in_vmem(), in_any(), in_vmem(), in_any(), in_any()),
-        scratch_shapes=[
-            VMEM((n, 2, BLK, D), BF16),
-            VMEM((4, 2, BLK, D), BF16),
-            VMEM((nf * rows, 256), BF16),
-            VMEM((256, nf * rows), BF16),
-            VMEM((nf,) + vec.shape, F32),
-            VMEM((1, nf * rows), F32),
-            VMEM((2, rows // 2, D), F32),
-            VMEM((6, 2, rows // 2, D), BF16),
-            dma((4, n, 2)), dma((n, 2)), dma((peers,)), dma((peers,)), dma((peers,)), dma((peers,)),
-            dma((2,)), dma((3,)), dma((3, peers)), dma((3, peers)), dma((3, peers)), dma((3, peers)),
-            dma((4,)), dma((6, 2)),
-        ],
-        compiler_params=pltpu.CompilerParams(
-            collective_id=0, has_side_effects=True, vmem_limit_bytes=60 * MIB
-        ),
-        cost_estimate=cost(60),
-        name="gather_tokens",
-    )(x, wh, vec, *mats)
-
-
-class Swap:
-    def __init__(self, place, src, dst, send_sem, recv_sem, own_sem):
-        self.p, self.src, self.dst = place, src, dst
-        self.send_sem, self.recv_sem, self.own_sem = send_sem, recv_sem, own_sem
-
-    def copy(self, s, block):
-        p = self.p
-        return pltpu.make_async_remote_copy(
-            src_ref=self.src((p.c + s) % p.n), dst_ref=self.dst(block),
-            send_sem=self.send_sem.at[s], recv_sem=self.recv_sem.at[s],
-            device_id=((p.c + s) % p.n, p.f), device_id_type=MESH,
-        )
-
-    def own(self):
-        return pltpu.make_async_copy(self.src(self.p.c), self.dst(self.p.c), self.own_sem)
-
-    def start(self):
-        for s in range(1, self.p.n):
-            self.copy(s, self.p.c).start()
-        self.own().start()
-
-    def wait(self):
-        self.own().wait()
-        for s in range(1, self.p.n):
-            self.copy(s, (self.p.c + self.p.n - s) % self.p.n).wait_recv()
-
-    def drain(self):
-        for s in range(1, self.p.n):
-            self.copy(s, self.p.c).wait_send()
-
-
-def swap_kernel(n, nf, src, dst, send_sem, recv_sem, own_sem):
-    p = Place(n, nf)
-    p.greet_all(False)
-    swap = Swap(p, lambda d: src.at[d], lambda d: dst.at[d], send_sem, recv_sem, own_sem)
-    swap.start()
-    swap.wait()
-    swap.drain()
-
-
-def swap_out(n, nf, blocks):
-    dma = pltpu.SemaphoreType.DMA
-    return pl.pallas_call(
-        functools.partial(swap_kernel, n, nf),
-        out_shape=jax.ShapeDtypeStruct(blocks.shape, blocks.dtype),
-        in_specs=[in_vmem()],
-        out_specs=in_vmem(),
-        scratch_shapes=[dma((n,)), dma((n,)), dma],
-        compiler_params=pltpu.CompilerParams(
-            collective_id=1, has_side_effects=True, vmem_limit_bytes=60 * MIB
-        ),
-        cost_estimate=cost(15),
-        name="swap_out",
-    )(blocks)
-
-
-def seq_start(ends, base, token):
-    start = jnp.zeros_like(token)
-    for e in ends:
-        start = jnp.where(e - base <= token, jnp.maximum(start, e - base), start)
-    return start
-
-
-def read_ends(lengths_ref):
-    ends, total = [], jnp.int32(0)
-    for i in range(lengths_ref.shape[1]):
-        total = total + lengths_ref[0, i]
-        ends.append(total)
-    return ends
-
-
-def pad_rows(block):
-    return jnp.concatenate([block, jnp.zeros((BLK - HD, block.shape[1]), block.dtype)], axis=0)
-
-
-class Layout:
-    def __init__(self, n, total_blocks):
-        self.n = n
-        self.hpd = 2 * H // n
-        self.half_blocks = total_blocks // 2
-        self.size = self.half_blocks * BLK
-        self.rows = self.hpd * self.size
-        self.tile = 512
-
-    def half(self, i):
-        return i if self.hpd == 2 else lax.axis_index("ctx") % 2
-
-    def nat(self, deal_ref, d, i):
-        half = self.half(i)
-        block = deal_ref[2 * d + half]
-        if self.hpd == 1:
-            block = block - half * self.half_blocks
-        return al(block * BLK, BLK)
-
-    def base(self, unit):
-        return self.half(unit) * self.size if self.hpd == 1 else unit * self.size
-
-
-def fwd_kernel(
-    lay, deal_ref, len_ref, qkv_ref, bias_ref, c_ref,
-    ot_out, qraw, qst, kt, vt, kn, ot, lse,
-    m_ref, l_ref, acc_ref,
-):
-    tile = lay.tile
-
-    @pl.loop(0, lay.n)
-    def _(d):
-        for i in range(lay.hpd):
-            nat = lay.nat(deal_ref, d, i)
-            cols = pl.ds(nat, BLK)
-            half = lay.half(i)
-            src = pl.ds(half * BLK if lay.hpd == 2 else al(half * BLK, BLK), BLK)
-            block = qkv_ref[d, :, src] + bias_ref[...]
-            qr, kr, vr = block[:HD], block[HD : 2 * HD], block[2 * HD :]
+        vec_copy(s, peer).wait_recv()
+        wh_copy(s, peer).wait_recv()
+    wht[...] = whbuf[...].astype(F32).T.astype(BF16)
+    for source in range(nf):
+        rows_out[:, pl.ds(source * rows, rows)] = vecbuf[source, :, 0:rows]
+    for r in (4, 5):
+        shares = vecbuf[0, r : r + 1, 0:BLK]
+        for source in range(1, nf):
+            shares = shares + vecbuf[source, r : r + 1, 0:BLK]
+        rows_out[r : r + 1, 0:BLK] = shares
+    vcol[...] = rows_out[...].T
+    head = c * hpd // 2
+    here = pl.ds(al(head * HD, 16), HD)
+    bias_q, bias_v = vcol[here, 1:2], vcol[here, 2:3]
+    factor = vcol[0:HD, 4:5]
+    factor_out[...] = jnp.broadcast_to(factor, (HD, BLK))
+
+    def a_copy(slot, origin, half):
+        return pltpu.make_async_copy(norm.at[slot], a_out.at[pl.ds(origin, 2), half], a_sem.at[slot])
+
+    def project(u, k, first=False):
+        half = lay.half(u)
+        for zz, guard, _ in p.level(k):
+            def body(zz=zz):
+                spread.from_twin(zz, [u] if hpd == 2 else range(2))
+                for t in range(2):
+                    origin = zz * 4 + 2 * t
+                    if not first:
+                        a_copy(t, origin, half).wait()
+                    for i in range(2):
+                        x = abuf[origin + i, half].astype(F32)
+                        scale = lax.rsqrt(jnp.mean(x * x, axis=-1, keepdims=True) + EPS)
+                        norm[t, i] = (x * scale * rows_out[0:1, :]).astype(BF16)
+                    a_copy(t, origin, half).start()
+                    value = dot(wht[: 3 * HD, :], norm[t].reshape(2 * BLK, D), NT)
+                    qkv[origin] = value[:, :BLK]
+                    qkv[origin + 1] = value[:, BLK:]
+            when(guard, body)
+
+    ends = read_ends(len_ref)
+
+    def attend(u, during):
+        base, row0 = lay.base(u), u * lay.size
+
+        @pl.loop(0, lay.half_blocks)
+        def _(b):
+            cols = pl.ds(al(row0 + b * BLK, BLK), BLK)
+            block = qkv[inv_ref[b + lay.half(u) * lay.half_blocks]]
+            qr, kr, vr = block[:HD] + bias_q, block[HD : 2 * HD], block[2 * HD :] + bias_v
             qraw[:, cols] = qr
-            qst[:, cols] = pad_rows(qr * c_ref[...]).astype(BF16)
+            qst[:, cols] = pad_rows(qr * factor).astype(BF16)
             kt[:, cols] = kr.astype(BF16)
             vt[:, cols] = vr.astype(BF16)
             kn[cols, :] = pad_rows(kr).T.astype(BF16)
-
-    ends = read_ends(len_ref)
-    for unit in range(lay.hpd):
-        base = lay.base(unit)
-        row0 = unit * lay.size
 
         @pl.loop(0, lay.size // tile)
         def _(qi):
             cols = pl.ds(al(row0 + qi * tile, tile), tile)
             t_row = qi * tile + lax.broadcasted_iota(jnp.int32, (1, tile), 1)
             start = seq_start(ends, base, t_row)
-            low = seq_start(ends, base, qi * tile) // tile
             m_ref[...] = jnp.full_like(m_ref, NEG)
             l_ref[...] = jnp.zeros_like(l_ref)
             acc_ref[...] = jnp.zeros_like(acc_ref)
 
-            def visit(j, diagonal):
+            @pl.loop(0, qi + 1)
+            def _(j):
                 keys = pl.ds(al(row0 + j * tile, tile), tile)
                 s = dot(kn[keys, :], qst[:, cols])
-                u = j * tile + lax.broadcasted_iota(jnp.int32, (tile, 1), 0)
-                seen = u >= start
-                if diagonal:
-                    seen = seen & (u <= t_row)
-                s = jnp.where(seen, s, NEG)
+                token = j * tile + lax.broadcasted_iota(jnp.int32, (tile, 1), 0)
+                s = jnp.where((token >= start) & (token <= t_row), s, NEG)
                 m_old = m_ref[...]
                 m_new = jnp.maximum(m_old, jnp.max(s, axis=0, keepdims=True))
-                p = jnp.exp(s - m_new)
+                prob = jnp.exp(s - m_new)
                 shrink = jnp.exp(m_old - m_new)
                 m_ref[...] = m_new
-                l_ref[...] = l_ref[...] * shrink + jnp.sum(p, axis=0, keepdims=True)
-                acc_ref[...] = acc_ref[...] * shrink + dot(vt[:, keys], p.astype(BF16))
-
-            @pl.loop(low, qi)
-            def _(j):
-                visit(j, False)
-
-            visit(qi, True)
-            ot[:, cols] = acc_ref[...] / l_ref[...]
+                l_ref[...] = l_ref[...] * shrink + jnp.sum(prob, axis=0, keepdims=True)
+                acc_ref[...] = acc_ref[...] * shrink + dot(vt[:, keys], prob.astype(BF16))
+
+            out = acc_ref[...] / l_ref[...]
+            ot[:, cols] = out
             lse[:, cols] = m_ref[...] + jnp.log(l_ref[...])
-
-    @pl.loop(0, lay.n)
-    def _(d):
-        for i in range(lay.hpd):
-            ot_out[d, i] = ot[:, pl.ds(lay.nat(deal_ref, d, i), BLK)].astype(BF16)
-
-
-def attend(lay, deal, lengths, qkv, bias, factor):
-    rows = lay.rows
+            for b in range(tile // BLK):
+                onat[qi * (tile // BLK) + b] = out[:, b * BLK : (b + 1) * BLK].astype(BF16)
+            for at, event in during:
+                pl.when(qi == at)(event)
+
+        @pl.loop(0, n)
+        def _(d):
+            osend[u, d] = onat[rel_ref[2 * d + lay.half(u)]]
+
+        o_swaps[u].start()
+
+    o_swaps = [
+        Swap(p, lambda d, u=u: osend.at[u, d], lambda d, u=u: oswap.at[d, u],
+             o_send.at[u], o_recv.at[u], o_own.at[u])
+        for u in range(hpd)
+    ]
+
+    def gather_events(i, first, last):
+        for k in range(first, last):
+            if k < zlen:
+                spread.chain(k, i)
+            spread.pair(k - 1, i)
+
+    later = min(2, zlen - 1)
+    for k in range(1, zlen + 1):
+        gather_events(0, k, k + 1)
+        if k == later:
+            spread.start(1)
+        if hpd == 2:
+            project(0, k - 1, first=k == 1)
+    pass_matrix(0)
+    if hpd == 2:
+        gather_events(1, 1, 2)
+        attend(0, [(lay.size // tile // 2, lambda: gather_events(1, 2, 3))])
+        pass_matrix(1)
+        for k in range(3, zlen + 1):
+            gather_events(1, k, k + 1)
+            project(1, k - 3)
+        for k in range(zlen - 2, zlen):
+            project(1, k)
+        attend(1, [])
+    else:
+        for k in range(1, zlen + 1):
+            gather_events(1, k, k + 1)
+            project(0, k - 1, first=k == 1)
+        attend(0, [])
+        pass_matrix(1)
+    pass_matrix(2)
+    for src, dst in zip(kept, stored[: len(kept)]):
+        stores.start(src, dst)
+
+    def handed(m):
+        for s, (peer, source) in enumerate(zip(p.fpeers, p.fsources)):
+            ms_copy(m, s, source, 1 - core).wait_recv()
+    for m in range(3):
+        for copy in keep_copies(m):
+            copy.wait()
+        handed(m)
+    spread.drain()
+    weights = [abuf.at[pl.ds(5 * m, 5)].reshape(5 * 2 * BLK, D) for m in range(3)]
+    w_loads = [
+        pltpu.make_async_copy(mats_out.at[m], weights[m], w_sem.at[m]) for m in range(3)
+    ]
+    for copy in w_loads:
+        copy.start()
+    for u in range(hpd):
+        o_swaps[u].wait()
+    w_loads[0].wait()
+    token_rows(
+        x_ref, cot_ref, oswap, rows_out, weights, w_loads,
+        layer, dh, gt, ot_t, bt, zt, gb, du, dg2_out, o_rows, hidden, nh, b_rows, up, z, db, wide)
+    for src, dst in zip(made, stored[len(kept) :]):
+        stores.start(src, dst)
+
+    for m in range(3, moved):
+        pass_matrix(m)
+    for m in range(3, moved):
+        for copy in keep_copies(m):
+            copy.wait()
+        handed(m)
+    for copy in keep_copies(moved):
+        copy.wait()
+    for m in range(moved):
+        for s, (peer, source) in enumerate(zip(p.fpeers, p.fsources)):
+            mx_copy(m, s, peer, f).wait_send()
+            ms_copy(m, s, source, core).wait_send()
+    for s, peer in enumerate(p.fpeers):
+        wh_copy(s, peer).wait_send()
+        vec_copy(s, peer).wait_send()
+    for u in range(hpd):
+        o_swaps[u].drain()
+    for slot in range(2):
+        a_copy(slot, 2 * slot, lay.half(0)).wait()
+    stores.wait()
+
+
+def forward(lay, nf, within, inverse, lengths, x, cot, wh, vec, mats):
+    n, hpd, total = lay.n, lay.hpd, lay.rows
+    rows, tok, count = wh.shape[0], x.shape[0], len(mats)
+    dma = pltpu.SemaphoreType.DMA
+    peers = max(nf - 1, 1)
+    half = ((rows // 2, D), BF16)
+    kept = [
+        ((HD, total), F32), ((BLK, total), BF16), ((HD, total), BF16), ((HD, total), BF16), ((total, BLK), BF16),
+        ((HD, total), F32), ((1, total), F32),
+    ]
+    plain, turned, wide = ((tok, D), BF16), ((D, tok), BF16), ((tok, D), F32)
+    made = [plain, wide, ((H, 2, HD, BLK), BF16), turned, turned, turned, plain, plain]
+    outs = [
+        ((n, 2, BLK, D), BF16), ((count - 1, nf * rows, D), BF16), half, half,
+        ((8, D), F32), ((HD, BLK), F32), ((1, D), F32),
+    ] + kept + made
+    places = [in_any()] * 4 + [in_vmem()] * 3 + [in_any()] * (len(kept) + len(made))
+    moves = dma((count - 1, peers))
     return pl.pallas_call(
-        functools.partial(fwd_kernel, lay),
-        out_shape=(
-            jax.ShapeDtypeStruct((lay.n, lay.hpd, HD, BLK), BF16),
-            jax.ShapeDtypeStruct((HD, rows), F32),
-            jax.ShapeDtypeStruct((BLK, rows), BF16),
-            jax.ShapeDtypeStruct((HD, rows), BF16),
-            jax.ShapeDtypeStruct((HD, rows), BF16),
-            jax.ShapeDtypeStruct((rows, BLK), BF16),
-            jax.ShapeDtypeStruct((HD, rows), F32),
-            jax.ShapeDtypeStruct((1, rows), F32),
+        functools.partial(forward_kernel, lay, n, nf),
+        out_shape=tuple(jax.ShapeDtypeStruct(*out) for out in outs),
+        in_specs=[in_smem()] * 3 + [in_vmem()] * 4 + [in_any()] * count,
+        out_specs=tuple(places),
+        scratch_shapes=[
+            VMEM((n, 2, BLK, D), BF16),
+            VMEM((2, 2, BLK, D), BF16),
+            VMEM((nf * rows, 256), BF16),
+            VMEM((256, nf * rows), BF16),
+            VMEM((nf,) + vec.shape, F32),
+            VMEM((D, 8), F32),
+            VMEM((2, rows // 2, D), F32),
+            VMEM((count, 2, rows // 2, D), BF16),
+            VMEM((n, 3 * HD, BLK), F32),
+            VMEM((hpd, n, HD, BLK), BF16),
+            VMEM((lay.half_blocks, HD, BLK), BF16),
+            VMEM((n, hpd, HD, BLK), BF16),
+        ] + [VMEM(*item) for item in kept + made] + [
+            VMEM(*plain), VMEM(*wide), VMEM(*wide), VMEM(*plain), VMEM(*wide), VMEM(*plain), VMEM(*wide),
+            VMEM(*turned),
+            VMEM((1, lay.tile), F32), VMEM((1, lay.tile), F32), VMEM((HD, lay.tile), F32),
+            dma((4, n, 2)), dma((n, 2)), dma((peers,)), dma((peers,)), dma((peers,)), dma((peers,)),
+            dma((2,)), moves, moves, moves, moves,
+            dma((2,)), dma((count, 2)), dma((hpd, n)), dma((hpd, n)), dma((hpd,)),
+            dma((len(kept) + len(made),)), dma((3,)),
+        ],
+        compiler_params=pltpu.CompilerParams(
+            collective_id=0, has_side_effects=True, vmem_limit_bytes=61 * MIB
         ),
-        in_specs=[in_smem(), in_smem()] + [in_vmem()] * 3,
-        out_specs=tuple([in_vmem()] * 8),
-        scratch_shapes=[
-            VMEM((1, lay.tile), F32), VMEM((1, lay.tile), F32), VMEM((HD, lay.tile), F32),
-        ],
-        compiler_params=pltpu.CompilerParams(vmem_limit_bytes=60 * MIB),
-        cost_estimate=cost(19),
-        name="attend",
-    )(deal, lengths, qkv, bias, factor)
-
-
-WIDE = 256
-
-
-def over_columns(body):
-    @pl.loop(0, D // WIDE)
-    def _(j):
-        body(pl.ds(al(j * WIDE, WIDE), WIDE))
-
-
-def ffn_kernel(
-    x_ref, cot_ref, ot_ref, g2_ref, mats_ref,
-    out_ref, dh_ref, gt_ref, ot, bt, zt, gb, du, dg2_ref,
-    o_rows, hidden, nh, b, up, z, db, wide,
-):
-    tok = x_ref.shape[0]
-    wo, w1, w2 = mats_ref.at[0], mats_ref.at[1], mats_ref.at[2]
-    for i in range(2):
-        for h in range(H):
-            ot[pl.ds(h * HD, HD), pl.ds(i * BLK, BLK)] = ot_ref[h, i]
-    @pl.loop(0, D // WIDE)
-    def _(j):
-        sl = pl.ds(al(j * WIDE, WIDE), WIDE)
-        o_rows[:, sl] = ot[sl, :].astype(F32).T.astype(BF16)
-
-    def body(sl):
-        hidden[:, sl] = x_ref[:, sl].astype(F32) + dot(o_rows[...], wo[:, sl])
-    over_columns(body)
-    hid = hidden[...]
-    r2 = lax.rsqrt(jnp.mean(hid * hid, axis=-1, keepdims=True) + EPS)
-    nh[...] = hid * r2
-    b[...] = (nh[...] * g2_ref[...]).astype(BF16)
-
-    def body(sl):
-        u = dot(b[...], w1[:, sl])
-        up[:, sl] = u
-        z[:, sl] = (u * jax.nn.sigmoid(u)).astype(BF16)
-    over_columns(body)
-
-    def body(sl):
-        out_ref[:, sl] = (hidden[:, sl] + dot(z[...], w2[:, sl])).astype(BF16)
-        dz = dot(cot_ref[...], w2[sl, :], NT)
-        u = up[:, sl]
-        sig = jax.nn.sigmoid(u)
-        du[:, sl] = (dz * sig * (1.0 + u * (1.0 - sig))).astype(BF16)
-    over_columns(body)
-
-    def body(sl):
-        g = dot(du[...], w1[sl, :], NT)
-        db[:, sl] = g * g2_ref[:, sl]
-        dg2_ref[:, sl] = jnp.sum(g * nh[:, sl], axis=0, keepdims=True)
-    over_columns(body)
-    scaled = db[...]
-    mean = jnp.mean(scaled * nh[...], axis=-1, keepdims=True)
-    dh = cot_ref[...].astype(F32) + r2 * (scaled - nh[...] * mean)
-    dh_ref[...] = dh
-    gb[...] = dh.astype(BF16)
-
-    @pl.loop(0, D // WIDE)
-    def _(j):
-        sl = pl.ds(al(j * WIDE, WIDE), WIDE)
-        wide[sl, :] = dot(wo[sl, :], gb[...], NT).astype(BF16)
-    for i in range(2):
-        for h in range(H):
-            gt_ref[h, i] = wide[pl.ds(h * HD, HD), pl.ds(i * BLK, BLK)]
-
-    @pl.loop(0, D // WIDE)
-    def _(j):
-        sl = pl.ds(al(j * WIDE, WIDE), WIDE)
-        bt[sl, :] = b[:, sl].astype(F32).T.astype(BF16)
-        zt[sl, :] = z[:, sl].astype(F32).T.astype(BF16)
-
-
-def ffn(x, cot, ot, g2, mats):
-    tok = x.shape[0]
-    turned = jax.ShapeDtypeStruct((D, tok), BF16)
-    plain = jax.ShapeDtypeStruct((tok, D), BF16)
-    return pl.pallas_call(
-        ffn_kernel,
-        out_shape=(
-            plain,
-            jax.ShapeDtypeStruct((tok, D), F32),
-            jax.ShapeDtypeStruct((H, 2, HD, BLK), BF16),
-            turned, turned, turned, plain, plain,
-            jax.ShapeDtypeStruct((1, D), F32),
-        ),
-        in_specs=[in_vmem()] * 5,
-        out_specs=tuple([in_vmem()] * 9),
-        scratch_shapes=[
-            VMEM((tok, D), BF16), VMEM((tok, D), F32), VMEM((tok, D), F32),
-            VMEM((tok, D), BF16), VMEM((tok, D), F32), VMEM((tok, D), BF16),
-            VMEM((tok, D), F32), VMEM((D, tok), BF16),
-        ],
-        compiler_params=pltpu.CompilerParams(vmem_limit_bytes=60 * MIB),
-        cost_estimate=cost(20),
-        name="feed_forward",
-    )(x, cot, ot, g2, mats)
+        cost_estimate=cost(100),
+        name="forward",
+    )(within, inverse, lengths, x, cot, wh, vec, *mats)
 
 
 VEC_ROWS = 24
-
-
-class Loads:
-    def __init__(self, sems):
-        self.sems, self.count = sems, 0
-
-    def start(self, src, dst):
-        copy = pltpu.make_async_copy(src, dst, self.sems.at[self.count])
-        self.count += 1
-        copy.start()
-        return copy
 
 
 def backward_kernel(
@@ -822,11 +822,11 @@
     rel_ref, inv_ref, len_ref, gt, c_ref, g1_ref, dg2_ref,
     ot_t_in, bt_in, zt_in, gb_in, du_in, cot_in,
     qraw_in, qst_in, kt_in, vt_in, kn_in, ot_in, lse_in,
-    a_ref, mine_ref, other_ref, got_ref, x_in, dh_in,
-    gx_out, dw_out, fw_out, vec_out, tg_out,
+    a_ref, mats_ref, mine_ref, other_ref, x_in, dh_in,
+    gx_out, dw_out, fw_out, vec_out, xw_out, tw_out,
     big, sums, wide, abuf, qraw, qst, kt, vt, kn, ot, lse, x_ref, dh_ref,
     qn, vn, don, dost, delta, dk, dv, dqt, natural, part_sums, left, back, dw, dwsend, dwrecv, dwown, vx, vsum, vall,
-    ld_sem, do_send, do_recv, do_own, dq_send, dq_recv, dq_own, tw_send, tw_recv, tg_send, tg_recv, a_sem,
+    ld_sem, do_send, do_recv, do_own, dq_send, dq_recv, dq_own, tw_send, tw_recv, xw_send, xw_recv, tg_send, tg_recv, a_sem,
     x_send, x_recv, own_sem, ag_send, ag_recv, fg_send, fg_recv, v_send, v_recv, u_send, u_recv,
     *rest,
 ):
@@ -854,14 +854,17 @@
     for swap in do_swaps:
         swap.start()
 
+    def xw_copy(s, peer):
+        return pltpu.make_async_remote_copy(
+            src_ref=mine_ref, dst_ref=xw_out.at[s], send_sem=xw_send.at[s], recv_sem=xw_recv.at[s],
+            device_id=(c, peer), device_id_type=MESH,
+        )
+
     def tg_copy(s):
         return pltpu.make_async_remote_copy(
-            src_ref=got_ref.at[s], dst_ref=tg_out.at[s], send_sem=tg_send.at[s], recv_sem=tg_recv.at[s],
+            src_ref=xw_out.at[s], dst_ref=tw_out.at[s], send_sem=tg_send.at[s], recv_sem=tg_recv.at[s],
             device_id=(p.twin, f), device_id_type=MESH,
         )
-
-    for s in range(nf - 1):
-        tg_copy(s).start()
 
     height = sums.shape[1]
     flat = 3 * part
@@ -909,18 +912,14 @@
     for s, source in shards:
         twin_copy(s, source).wait_send()
 
-    for s in range(nf - 1):
-        tg_copy(s).wait_recv()
-    w_loads = []
-    for m in range(3):
-        def load_w(src, source, half, m=m):
-            at = pl.ds(al(m * D + source * rows + half * part, 16), part)
-            w_loads.append(loads.start(src, big.at[at]))
-        load_w(mine_ref.at[m], f, p.core)
-        load_w(other_ref.at[m], f, 1 - p.core)
-        for s, source in enumerate(p.fsources):
-            load_w(got_ref.at[s, m], source, p.core)
-            load_w(tg_out.at[s, m], source, 1 - p.core)
+    w_loads = [loads.start(mats_ref.at[3 + m], big.at[pl.ds(m * D, D)]) for m in range(2)]
+
+    def load_w(src, source, half):
+        at = pl.ds(al(2 * D + source * rows + half * part, 16), part)
+        w_loads.append(loads.start(src, big.at[at]))
+
+    load_w(mine_ref, f, p.core)
+    load_w(other_ref, f, 1 - p.core)
 
     for copy in att_loads:
         copy.wait()
@@ -1044,6 +1043,8 @@
     for s, peer in enumerate(p.fpeers):
         x_copy(s, peer).start()
     reduce.start_x(zlen - 1)
+    for s, peer in enumerate(p.fpeers):
+        xw_copy(s, peer).start()
 
     spread = Spread(p, dw_out, ag_send, ag_recv, 3)
     spread2 = Spread(p, fw_out, fg_send, fg_recv, fw_out.shape[1])
@@ -1095,6 +1096,11 @@
                 spread.chain(k, i)
                 spread.pair(k - 1, i)
 
+    for s, (peer, source) in enumerate(zip(p.fpeers, p.fsources)):
+        xw_copy(s, peer).wait_recv()
+        tg_copy(s).start()
+        load_w(xw_out.at[s], source, p.core)
+
     for u in range(hpd):
         gradient_swap(u).wait()
     for m in range(3):
@@ -1102,6 +1108,9 @@
             for h in range(H):
                 block = back[i, h] if hpd == 2 else back[0, 2 * h + i]
                 wide[m, pl.ds(h * HD, HD), pl.ds(i * BLK, BLK)] = block[m * HD : (m + 1) * HD]
+    for s, source in enumerate(p.fsources):
+        tg_copy(s).wait_recv()
+        load_w(tw_out.at[s], source, 1 - p.core)
     for copy in w_loads:
         copy.wait()
 
@@ -1178,6 +1187,7 @@
     spread2.drain()
     reduce.drain()
     for s, peer in enumerate(p.fpeers):
+        xw_copy(s, peer).wait_send()
         tg_copy(s).wait_send()
         x_copy(s, peer).wait_send()
         v_copy(s, peer, f).wait_send()
@@ -1185,7 +1195,7 @@
         u_copy(s, c).wait_send()
 
 
-def backward(lay, nf, within, inverse, lengths, gt, factor, g1, dg2, ffn_parts, cot, kept, tokens, mine, other, got, x, dh):
+def backward(lay, nf, within, inverse, lengths, gt, factor, g1, dg2, ffn_parts, cot, kept, tokens, mats, mine, other, x, dh):
     n, hpd, rows, size = lay.n, lay.hpd, lay.rows, lay.size
     dma = pltpu.SemaphoreType.DMA
     shard = D // nf
@@ -1203,10 +1213,11 @@
             jax.ShapeDtypeStruct((n, 3, HD, shard), BF16),
             jax.ShapeDtypeStruct((n, pieces, piece // pieces, D // 2), BF16),
             jax.ShapeDtypeStruct((n, VEC_ROWS, BLK), F32),
-            jax.ShapeDtypeStruct((peers, 3, part, D), BF16),
+            jax.ShapeDtypeStruct((peers, part, D), BF16),
+            jax.ShapeDtypeStruct((peers, part, D), BF16),
         ),
         in_specs=[in_smem()] * 3 + [in_vmem()] * 4 + [in_any()] * 19,
-        out_specs=(in_vmem(), in_any(), in_any(), in_vmem(), in_any()),
+        out_specs=(in_vmem(), in_any(), in_any(), in_vmem(), in_any(), in_any()),
         scratch_shapes=[
             VMEM((3 * D, D), BF16), VMEM((nf, height, D), BF16), VMEM((3, D, tok), BF16),
             VMEM((2, 8 * BLK, D), BF16),
@@ -1220,7 +1231,7 @@
             VMEM((peers, 3 * HD, shard), BF16), VMEM((3, HD, shard), BF16),
             VMEM((nf, VEC_ROWS, BLK), F32), VMEM((VEC_ROWS, BLK), F32), VMEM((n, VEC_ROWS, BLK), F32),
             dma((15 + 6 * nf,)), dma((hpd, n)), dma((hpd, n)), dma((hpd,)), dma((hpd, n)), dma((hpd, n)), dma((hpd,)),
-            dma((nf,)), dma((nf,)), dma((peers,)), dma((peers,)), dma((2,)),
+            dma((nf,)), dma((nf,)), dma((peers,)), dma((peers,)), dma((peers,)), dma((peers,)), dma((2,)),
             dma((peers,)), dma((peers,)), dma, dma((4, n, 3)), dma((n, 3)), dma((4, n, pieces)), dma((n, pieces)),
             dma((peers,)), dma((peers,)), dma((n,)), dma((n,)),
         ] + [VMEM((n, HD, BLK), BF16)] * hpd + Reduce.scratch(nf, zlen, height),
@@ -1229,7 +1240,7 @@
         ),
         cost_estimate=cost(130),
         name="backward",
-    )(within, inverse, lengths, gt, factor, g1, dg2, *ffn_parts, cot, *kept, tokens, mine, other, got, x, dh)
+    )(within, inverse, lengths, gt, factor, g1, dg2, *ffn_parts, cot, *kept, tokens, mats, mine, other, x, dh)
 
 
 def turn_kernel(hpd, dw_ref, q_ref, k_ref, v_ref, wide):
@@ -1305,48 +1316,38 @@
     x, cot = tokens[0], cotangent[0]
 
     def low(v):
-        return v.astype(BF16).astype(F32)
+        return lax.reduce_precision(v, exponent_bits=8, mantissa_bits=7)
 
     g1_own = low(gain_attn)
     slices = [
         lax.dynamic_slice(w, (0, head * HD), (rows, HD)) for w in (query_weight, key_weight, value_weight)
     ]
     wh = jnp.pad(jnp.concatenate(slices, axis=1), ((0, 0), (0, 256 - 3 * HD))).astype(BF16)
-    vec = jnp.stack([g1_own, low(query_bias), low(value_bias), low(gain_ffn)])
-    vec = jnp.concatenate([vec, jnp.pad(low(query_scale), (0, rows - query_scale.shape[0]))[None]])
-    vec = jnp.pad(vec, ((0, 3), (0, -rows % 128)))
-
-    a_all, qkv, mats, vecs, mine, other = gather(
-        n, nf, x, wh, vec, (proj_weight, up_weight, down_weight, query_weight, key_weight, value_weight)
-    )
-    whole = jnp.swapaxes(vecs[:, :5, :rows], 0, 1).reshape(5, nf * rows)
-    g1, bq, bv, g2 = whole[0], whole[1], whole[2], whole[3]
-    q_param = vecs[:, 4, : query_scale.shape[0]].reshape(HD)
-    factor = jnp.log(1.0 + jnp.exp(q_param)) * (LOG2E / math.sqrt(HD))
-    bias = jnp.concatenate([
-        lax.dynamic_slice(bq, (head * HD,), (HD,)), jnp.zeros((HD,), F32),
-        lax.dynamic_slice(bv, (head * HD,), (HD,)),
-    ])
-    bias = jnp.broadcast_to(bias[:, None], (3 * HD, BLK))
-    factor_col = jnp.broadcast_to(factor[:, None], (HD, BLK))
-
-    got = jnp.stack([
-        lax.ppermute(mine, "fsdp", [(i, (i + s) % nf) for i in range(nf)]) for s in range(1, nf)
-    ])
-
-    ot, *kept = attend(lay, deal, lengths, qkv, bias, factor_col)
-    ot = swap_out(n, nf, ot).reshape(H, 2, HD, BLK)
-    layer_out, dh, gt, ott, bt, zt, gb, du, dg2 = ffn(x, cot, ot, g2[None], mats)
-    part = rows // 2
-    zlen = n // 4
+    scale = low(query_scale)
+    factor = jnp.log(1.0 + jnp.exp(scale)) * (LOG2E / math.sqrt(HD))
+    shares = lax.dynamic_update_slice(
+        jnp.zeros((2, rows), F32), jnp.stack([factor, scale]), (0, f * query_scale.shape[0]))
+    vec = jnp.concatenate(
+        [jnp.stack([g1_own, low(query_bias), low(value_bias), low(gain_ffn)]), shares])
+    vec = jnp.pad(vec, ((0, 2), (0, -rows % 128)))
     blocks = jnp.arange(deal.shape[0], dtype=jnp.int32)
     inverse = jnp.sum(jnp.where(deal[None, :] == blocks[:, None], blocks[None, :] // 2, 0), axis=1, dtype=jnp.int32)
-    grad_x, dw, pieces, vectors, _ = backward(
-        lay, nf, deal % lay.half_blocks, inverse, lengths, gt.reshape(n, lay.hpd, HD, BLK), factor_col, g1[None], dg2,
-        (ott, bt, zt, gb, du), cot, kept, a_all, mine, other, got, x, dh,
+    within = deal % lay.half_blocks
+
+    a_all, mats, mine, other, whole, factor_col, dg2, *stored = forward(
+        lay, nf, within, inverse, lengths, x, cot, wh, vec,
+        (proj_weight, up_weight, down_weight, query_weight, key_weight, value_weight),
+    )
+    kept, (layer_out, dh, gt, ott, bt, zt, gb, du) = stored[:7], stored[7:]
+    g1 = whole[0:1]
+    q_param = whole[5, :HD]
+
+    grad_x, dw, pieces, vectors, *_ = backward(
+        lay, nf, within, inverse, lengths, gt.reshape(n, lay.hpd, HD, BLK), factor_col, g1, dg2,
+        (ott, bt, zt, gb, du), cot, kept, a_all, mats, mine, other, x, dh,
     )
     dwq, dwk, dwv = turn(lay.hpd, dw)
-    grads = widen(zlen, part, pieces)
+    grads = widen(n // 4, rows // 2, pieces)
 
     def own(v):
         size = v.shape[0] // nf

time: 324 us -> 315 us (0.972)
  Pallas kernels: 302 us -> 294 us
    pallas_call x4 -> x1, Pallas kernels: 127 us -> 117 us  [forward(): pl.pallas_call(functools.partial(forward_kernel, lay, n, nf), out_shape=t...]
    convert_element_type x5 -> x0, other arithmetic: 3.41 us -> none  [low(): return v.astype(BF16).astype(F32)]
  transfers between devices with their start and end apart: 1 -> 0, of which waited for: 0 -> 0; matrix products, arithmetic and copies ran while one was open for 2% -> 0% of each run, Pallas kernels for 17% -> 0%
where the time goes in v4:
time: 315 us; the launch traced here: 314 us
  Pallas kernels  294 us (93%)
  local copies, waits for them, and re-layouts  10.1 us (3%)
  other arithmetic  9.49 us (3%)
    pallas_call x1, Pallas kernels, backward(): pl.pallas_call(functools.partial(backward_kernel, lay, n, nf), out_shape=...  162 us
    pallas_call x1, Pallas kernels, forward(): pl.pallas_call(functools.partial(forward_kernel, lay, n, nf), out_shape=t...  117 us
    pallas_call x1, Pallas kernels, turn(): pl.pallas_call(functools.partial(turn_kernel, hpd), grid=(D // WIDE,), ou...  7.98 us
    pallas_call x1, Pallas kernels, widen(): pl.pallas_call(functools.partial(widen_kernel, zlen, part), grid=(2, 2),...  6.4 us

profile of v4, /device:TPU:0, one launch (start us, length us, event | category | flops | bytes accessed | tf_op | source)
XLA Modules:
  0.0 313.9 jit_solution(1735389049720545861)
XLA Ops:
  0.7 0.7 multiply_bitcast_fusion
  1.3 1.2 and_select_fusion
  2.5 1.3 select_reduce_fusion.inv_ref
  3.8 0.7 reduce_precision.15
  4.5 0.7 reduce_precision.16
  5.2 0.7 reduce_precision.17
  5.9 0.7 reduce_precision.18
  6.6 0.1 dynamic_update_slice.3
  6.8 0.6 pad.10.vec_ref
  7.4 1.2 dynamic-slice_convert_fusion.2
  8.6 1.5 dynamic-slice_convert_fusion
  10.0 0.9 fusion.4.wh_ref
  11.0 117.2 %forward.1 = (bf16[16,2,128,1280]{3,2,1,0:T(8,128)(2,1)}, bf16[5,1280,1280]{2,1,0:T(8,128)(2,1)}, bf16[320,1280]{1,0:T(8,128)(2,1)}, bf16[320,1280]{1,0:T(8,128)...) custom-call(s32[32]{0:T(128)} %get-tuple-element.85.rel_ref, ...), custom_call_target="tpu_custom_call" | custom-call | bytes 300000000 | tf_op jit(solution)/shard_map/forward/pallas_call | solution.py:782
  128.2 1.4 slice.26.g1_ref
  129.6 161.9 %backward.1 = (f32[256,1280]{1,0:T(8,128)}, bf16[16,3,80,640]{3,2,1,0:T(8,128)(2,1)}, bf16[16,3,80,640]{3,2,1,0:T(8,128)(2,1)}, f32[16,24,128]{2,1,0:T(8,128)}, ...) custom-call(s32[32]{0:T(128)} %get-tuple-element.85.rel_ref, s32[32]{0:T(128)} %select_reduce_fusion.inv_ref, ...), custom_call_target="tpu_custom_call" | custom-call | bytes 390000000 | tf_op jit(solution)/shard_map/backward/pallas_call | solution.py:1209
  291.5 1.0 slice_reduce_fusion
  292.5 1.0 slice_reduce_fusion.1
  293.5 0.7 fusion.6
  294.2 0.6 dynamic_slice.30
  294.8 0.7 dynamic_slice.31
  295.5 0.7 dynamic_slice.27
  296.1 0.1 reshape.89
  296.2 0.7 dynamic_slice.29
  296.9 0.1 reshape.88
  296.9 0.7 dynamic_slice.28
  297.6 8.0 %turn.1 = (f32[640,1280]{1,0:T(8,128)}, f32[640,1280]{1,0:T(8,128)}, f32[640,1280]{1,0:T(8,128)}) custom-call(bf16[16,3,80,640]{3,2,1,0:T(8,128)(2,1)} %get-tuple-element.69.dw_ref), custom_call_target="tpu_custom_call" | custom-call | bytes 18000000 | tf_op jit(solution)/shard_map/turn/pallas_call | solution.py:1266
  305.6 0.0 copy-start.1
  305.6 0.0 copy-start
  305.6 6.4 %widen.1 = (f32[640,1280]{1,0:T(8,128)}, f32[640,1280]{1,0:T(8,128)}, f32[640,1280]{1,0:T(8,128)}) custom-call(bf16[4,2,2,240,640]{4,3,2,1,0:T(8,128)(2,1)} %bitcast.17), custom_call_target="tpu_custom_call" | custom-call | bytes 15000000 | tf_op jit(solution)/shard_map/widen/pallas_call | solution.py:1295
  312.0 0.0 copy-done.1
  312.0 0.8 copy.31
  312.8 0.0 copy-done
  312.8 1.1 copy.32
  (8 shorter events, 0.1 us)
Async XLA Ops:
  305.6 6.4 %copy-start.1 = (bf16[256,1280]{1,0:T(8,128)(2,1)S(1)}, bf16[256,1280]{1,0:T(8,128)(2,1)}, u32[]{:S(2)}) copy-start(bf16[256,1280]{1,0:T(8,128)(2,1)} %get-tuple-element.45) | copy-start | bytes 1966084
  305.6 7.2 %copy-start = (f32[256,1280]{1,0:T(8,128)S(1)}, f32[256,1280]{1,0:T(8,128)}, u32[]{:S(2)}) copy-start(f32[256,1280]{1,0:T(8,128)} %get-tuple-element.67) | copy-start | bytes 3932164

commit v5 on v4

--- a/solution.py
+++ b/solution.py
@@ -92,7 +92,7 @@
         barrier = pltpu.get_barrier_semaphore()
         for s in range(1, self.n):
             pl.semaphore_signal(
-                barrier, inc=1, device_id=((self.c + s) % self.n, self.f), device_id_type=MESH)
+                barrier, inc=1, device_id=(self.c ^ s, self.f), device_id_type=MESH)
         if with_fsdp:
             for peer in self.fpeers:
                 pl.semaphore_signal(barrier, inc=1, device_id=(self.c, peer), device_id_type=MESH)
@@ -107,13 +107,14 @@
 
 
 class Spread:
-    def __init__(self, place, buf, send_sem, recv_sem, pieces):
+    def __init__(self, place, buf, send_sem, recv_sem, pieces, own=None, own_sem=None):
         self.p, self.buf, self.send_sem, self.recv_sem, self.pieces = place, buf, send_sem, recv_sem, pieces
-
-    def copy(self, way, origin, i):
+        self.own, self.own_sem = own, own_sem
+
+    def copy(self, way, origin, i, src=None):
         where = self.buf.at[origin, i]
         return pltpu.make_async_remote_copy(
-            src_ref=where, dst_ref=where,
+            src_ref=where if src is None else src, dst_ref=where,
             send_sem=self.send_sem.at[way, origin, i], recv_sem=self.recv_sem.at[origin, i],
             device_id=(self.p.targets[way], self.p.f), device_id_type=MESH,
         )
@@ -124,9 +125,15 @@
     def arrive(self, origin, i):
         self.copy(3, origin, i).wait_recv()
 
+    def keep(self, i):
+        return pltpu.make_async_copy(self.own(i), self.buf.at[self.p.c, i], self.own_sem.at[i])
+
     def start(self, i):
+        src = self.own(i) if self.own else None
         for way in range(4):
-            self.send(way, self.p.c, i)
+            when(self.p.guards[way], lambda way=way: self.copy(way, self.p.c, i, src).start())
+        if self.own:
+            self.keep(i).start()
 
     def chain(self, k, i):
         p = self.p
@@ -157,6 +164,8 @@
     def drain(self):
         p = self.p
         for i in range(self.pieces):
+            if self.own:
+                self.keep(i).wait()
             for way in range(4):
                 when(p.guards[way], lambda way=way, i=i: self.copy(way, p.c, i).wait_send())
             for k in range(p.zlen):
@@ -173,10 +182,10 @@
 
 
 class Reduce:
-    def __init__(self, place, mine, result, acc, xrecv, yrecv, urecv, drecv, sems):
+    def __init__(self, place, mine, result, acc, xrecv, yrecv, zsend, zrecv, sems):
         self.p, self.mine, self.result, self.acc = place, mine, result, acc
-        self.xrecv, self.yrecv, self.urecv, self.drecv = xrecv, yrecv, urecv, drecv
-        (self.xs, self.xr, self.ys, self.yr, self.us, self.ur, self.ds, self.dr) = sems
+        self.xrecv, self.yrecv, self.zsend, self.zrecv = xrecv, yrecv, zsend, zrecv
+        (self.xs, self.xr, self.ys, self.yr, self.zs, self.zr) = sems
         self.height = acc.shape[0] // place.zlen
         self.width = D // 2
         zlen = place.zlen
@@ -194,7 +203,7 @@
             VMEM((height // zlen, D // 2), BF16), VMEM((height, D), BF16), VMEM((peers, height, D), BF16),
             piece, piece, piece,
             dma((peers, zlen, 2)), dma((peers, zlen, 2)), dma((zlen,)), dma((zlen,)),
-            dma((zlen,)), dma((zlen,)), dma((zlen,)), dma((zlen,)),
+            dma((zlen,)), dma((zlen,)),
         ]
 
     def at(self, piece, side):
@@ -247,18 +256,11 @@
         return self.remote(
             src, self.yrecv.at[piece], self.ys.at[piece], self.yr.at[piece], self.p.ypeer, self.p.f)
 
-    def u_copy(self, piece):
-        src = self.acc.at[self.at(piece, self.p.y)]
+    def z_copy(self, piece, slot):
+        p = self.p
         return self.remote(
-            src, self.urecv.at[piece], self.us.at[piece], self.ur.at[piece], self.p.targets[0], self.p.f)
-
-    def d_copy(self, piece):
-        src = self.acc.at[self.at(piece, self.p.y)]
-        return self.remote(
-            src, self.drecv.at[piece], self.ds.at[piece], self.dr.at[piece], self.p.targets[1], self.p.f)
-
-    def mine_of(self, piece):
-        return self.acc.at[self.at(piece, self.p.y)]
+            self.zsend.at[piece], self.zrecv.at[slot], self.zs.at[piece], self.zr.at[slot],
+            p.idx(piece, p.y, p.core), p.f)
 
     def xy(self, t):
         piece = self.order[t]
@@ -267,38 +269,19 @@
         self.sum_x(piece, 1)
 
     def after_y(self, t):
-        piece = self.order[t]
+        p, piece = self.p, self.order[t]
         self.y_copy(piece).wait_recv()
-        self.add(self.mine_of(piece), [self.mine_of(piece), self.yrecv.at[piece]])
-
-    def chain(self, t, hop):
-        p, piece = self.p, self.order[t]
-        if hop < piece:
-            @pl.when(p.z == hop)
-            def _():
-                if hop:
-                    self.u_copy(piece).wait_recv()
-                    self.add(self.mine_of(piece), [self.mine_of(piece), self.urecv.at[piece]])
-                self.u_copy(piece).start()
-        if p.zlen - 1 - hop > piece:
-            @pl.when(p.z == p.zlen - 1 - hop)
-            def _():
-                if hop:
-                    self.d_copy(piece).wait_recv()
-                    self.add(self.mine_of(piece), [self.mine_of(piece), self.drecv.at[piece]])
-                self.d_copy(piece).start()
+        self.add(self.zsend.at[piece], [self.acc.at[self.at(piece, p.y)], self.yrecv.at[piece]])
+        pl.when(p.z != piece)(lambda: self.z_copy(piece, p.z).start())
 
     def last(self):
         p = self.p
-        @pl.when(p.z > 0)
-        def _():
-            self.u_copy(p.z).wait_recv()
-            self.add(self.mine_of(p.z), [self.mine_of(p.z), self.urecv.at[p.z]])
-        @pl.when(p.z < p.zlen - 1)
-        def _():
-            self.d_copy(p.z).wait_recv()
-            self.add(self.mine_of(p.z), [self.mine_of(p.z), self.drecv.at[p.z]])
-        self.add(self.result, [self.mine_of(p.z)])
+        terms = [self.zsend.at[p.z]]
+        for k in range(1, p.zlen):
+            other = lax.rem(p.z + k, p.zlen)
+            self.z_copy(0, other).wait_recv()
+            terms.append(self.zrecv.at[other])
+        self.add(self.result, terms)
 
     def drain(self):
         p = self.p
@@ -307,8 +290,7 @@
                 for s, peer in enumerate(p.fpeers):
                     self.x_copy(s, peer, piece, turn).wait_send()
             self.y_copy(piece).wait_send()
-            pl.when(p.z < piece)(lambda piece=piece: self.u_copy(piece).wait_send())
-            pl.when(p.z > piece)(lambda piece=piece: self.d_copy(piece).wait_send())
+            pl.when(p.z != piece)(lambda piece=piece: self.z_copy(piece, p.z).wait_send())
 
 
 class Loads:
@@ -334,9 +316,9 @@
     def copy(self, s, block):
         p = self.p
         return pltpu.make_async_remote_copy(
-            src_ref=self.src((p.c + s) % p.n), dst_ref=self.dst(block),
+            src_ref=self.src(p.c ^ s), dst_ref=self.dst(block),
             send_sem=self.send_sem.at[s], recv_sem=self.recv_sem.at[s],
-            device_id=((p.c + s) % p.n, p.f), device_id_type=MESH,
+            device_id=(p.c ^ s, p.f), device_id_type=MESH,
         )
 
     def own(self):
@@ -350,7 +332,7 @@
     def wait(self):
         self.own().wait()
         for s in range(1, self.p.n):
-            self.copy(s, (self.p.c + self.p.n - s) % self.p.n).wait_recv()
+            self.copy(s, self.p.c ^ s).wait_recv()
 
     def drain(self):
         for s in range(1, self.p.n):
@@ -388,6 +370,9 @@
     def half(self, i):
         return i if self.hpd == 2 else lax.axis_index("ctx") % 2
 
+    def within(self, deal_ref, d, u):
+        return deal_ref[2 * d + self.half(u)] & (self.half_blocks - 1)
+
     def base(self, unit):
         return self.half(unit) * self.size if self.hpd == 1 else unit * self.size
 
@@ -404,7 +389,7 @@
 def token_rows(
     x_ref, cot_ref, oswap, rows_ref, weights, w_loads,
     out_ref, dh_ref, gt_ref, ot, bt, zt, gb, du, dg2_ref,
-    o_rows, hidden, nh, b, up, z, db, wide,
+    o_rows, hidden, nh, b, up, z, db, wide, stage,
 ):
     wo, w1, w2 = weights
     hpd = oswap.shape[1]
@@ -415,6 +400,7 @@
     def _(j):
         sl = pl.ds(al(j * WIDE, WIDE), WIDE)
         o_rows[:, sl] = ot[sl, :].astype(F32).T.astype(BF16)
+    stage("ot")
 
     def body(sl):
         hidden[:, sl] = x_ref[:, sl].astype(F32) + dot(o_rows[...], wo[:, sl])
@@ -428,8 +414,13 @@
     def body(sl):
         u = dot(b[...], w1[:, sl])
         up[:, sl] = u
-        z[:, sl] = (u * jax.nn.sigmoid(u)).astype(BF16)
+        act = u * jax.nn.sigmoid(u)
+        z[:, sl] = act.astype(BF16)
+        zt[sl, :] = act.T.astype(BF16)
+        bt[sl, :] = b[:, sl].astype(F32).T.astype(BF16)
     over_columns(body)
+    stage("z")
+    stage("b")
 
     w_loads[2].wait()
 
@@ -440,6 +431,8 @@
         sig = jax.nn.sigmoid(u)
         du[:, sl] = (dz * sig * (1.0 + u * (1.0 - sig))).astype(BF16)
     over_columns(body)
+    stage("out")
+    stage("du")
 
     def body(sl):
         g = dot(du[...], w1[sl, :], NT)
@@ -451,6 +444,7 @@
     dh = cot_ref[...].astype(F32) + r2 * (scaled - nh[...] * mean)
     dh_ref[...] = dh
     gb[...] = dh.astype(BF16)
+    stage("gb")
 
     @pl.loop(0, D // WIDE)
     def _(j):
@@ -459,33 +453,41 @@
     for i in range(2):
         for h in range(H):
             gt_ref[h, i] = wide[pl.ds(h * HD, HD), pl.ds(i * BLK, BLK)]
-
-    @pl.loop(0, D // WIDE)
-    def _(j):
-        sl = pl.ds(al(j * WIDE, WIDE), WIDE)
-        bt[sl, :] = b[:, sl].astype(F32).T.astype(BF16)
-        zt[sl, :] = z[:, sl].astype(F32).T.astype(BF16)
+    stage("gt")
 
 
 def forward_kernel(
     lay, n, nf,
-    rel_ref, inv_ref, len_ref, x_ref, cot_ref, wh_ref, vec_ref, *rest,
+    deal_ref, inv_ref, len_ref, x_ref, cot_ref, *rest,
 ):
-    mat_refs, rest = rest[:6], rest[6:]
-    (a_out, mats_out, mine_out, other_out, rows_out, factor_out, dg2_out, *stored) = rest[: 7 + 15]
-    (abuf, norm, whbuf, wht, vecbuf, vcol, stage, wcast, qkv, osend, onat, oswap,
+    row_refs, mat_refs, rest = rest[:5], rest[5:11], rest[11:]
+    (a_out, mats_out, mine_out, other_out, twin_t, twin_r, rows_out, factor_out, dg2_out, *stored) = rest[: 9 + 12]
+    (abuf, norm, windows, wh_ref, whbuf, wht, vec_ref, vecbuf, vcol, stage, wcast, qkv, osend, onat, oswap,
      qraw, qst, kt, vt, kn, ot, lse, layer, dh, gt, ot_t, bt, zt, gb, du,
      o_rows, hidden, nh, b_rows, up, z, db, wide, m_ref, l_ref, acc_ref,
      ag_send, ag_recv, wh_send, wh_recv, vec_send, vec_recv,
      ld_sem, mx_send, mx_recv, ms_send, ms_recv, a_sem, keep_sem, o_send, o_recv, o_own,
-     st_sem, w_sem) = rest[7 + 15 :]
+     st_sem, w_sem, tt_send, tt_recv, tr_send, tr_recv, win_sem) = rest[9 + 12 :]
     kept = (qraw, qst, kt, vt, kn, ot, lse)
-    made = (layer, dh, gt, ot_t, bt, zt, gb, du)
     stores = Loads(st_sem)
     p = Place(n, nf)
     c, f, core, zlen, hpd, tile = p.c, p.f, p.core, p.zlen, lay.hpd, lay.tile
     rows = wh_ref.shape[0]
     part = rows // 2
+
+    head = c * hpd // 2
+    first = jnp.minimum(head * HD // BLK * BLK, D - 2 * BLK)
+    window_loads = [
+        pltpu.make_async_copy(
+            mat_refs[3 + m].at[:, pl.ds(al(first, BLK), 2 * BLK)], windows.at[m], win_sem.at[m])
+        for m in range(3)
+    ]
+    for copy in window_loads:
+        copy.start()
+    vec_ref[...] = jnp.zeros_like(vec_ref)
+    for r, ref in enumerate(row_refs):
+        for k in range(ref.shape[0]):
+            vec_ref[r : r + 1, k * BLK : (k + 1) * BLK] = ref[k : k + 1, :]
     p.greet_all(True)
     spread = Spread(p, abuf, ag_send, ag_recv, 2)
 
@@ -509,6 +511,21 @@
 
     for s, peer in enumerate(p.fpeers):
         vec_copy(s, peer).start()
+    for copy in window_loads:
+        copy.wait()
+    strip = 128 if rows % 128 == 0 else 32
+
+    @pl.loop(0, rows // strip)
+    def _(t):
+        at = pl.ds(al(t * strip, 32), strip)
+        lane = lax.broadcasted_iota(jnp.int32, (strip, 2 * BLK), 1)
+        value = jnp.zeros((strip, 2 * BLK), F32)
+        for m in range(3):
+            turned = pltpu.roll(windows[m, at, :], lax.rem(m * HD + 2 * BLK - (head * HD - first), 2 * BLK), 1)
+            value = jnp.where((lane >= m * HD) & (lane < (m + 1) * HD), turned, value)
+        wh_ref[at, :] = value.astype(BF16)
+
+    for s, peer in enumerate(p.fpeers):
         wh_copy(s, peer).start()
     whbuf[pl.ds(al(f * rows, 16), rows), :] = wh_ref[...]
     vecbuf[f] = vec_ref[...]
@@ -567,8 +584,20 @@
                 copy.start()
 
     load(0).start()
-    for step in range(len(steps)):
-        cast(step)
+    done = [0]
+
+    def casts(count):
+        for step in range(done[0], min(done[0] + count, len(steps))):
+            cast(step)
+        done[0] += count
+
+    casts(2)
+
+    def gather_events(i, first, last):
+        for k in range(first, last):
+            if k < zlen:
+                spread.chain(k, i)
+            spread.pair(k - 1, i)
 
     def ms_copy(m, s, source, half):
         where = mats_out.at[m, pl.ds(al(source * rows + half * part, 16), part)]
@@ -583,22 +612,47 @@
             mx_copy(m, s, peer, source).wait_recv()
             ms_copy(m, s, source, core).start()
 
+    def t_copy(m, source):
+        mat = (ot_t, bt, zt)[m]
+        return pltpu.make_async_remote_copy(
+            src_ref=mat.at[pl.ds(al(source * rows + (1 - core) * part, 16), part)],
+            dst_ref=twin_t.at[m, pl.ds(source * part, part)],
+            send_sem=tt_send.at[m, source], recv_sem=tt_recv.at[m, source],
+            device_id=(p.twin, f), device_id_type=MESH,
+        )
+
+    def r_copy(m):
+        return pltpu.make_async_remote_copy(
+            src_ref=(gb, du, cot_ref)[m], dst_ref=twin_r.at[m], send_sem=tr_send.at[m], recv_sem=tr_recv.at[m],
+            device_id=(p.twin, f), device_id_type=MESH,
+        )
+
+    own_t, own_r = stored[10], stored[11]
+
+    def to_twin(m, src):
+        for source in range(nf):
+            t_copy(m, source).start()
+            stores.start(
+                src.at[pl.ds(al(source * rows + core * part, 16), part)], own_t.at[m, pl.ds(source * part, part)])
+
+    r_copy(2).start()
+    gather_events(0, 1, 2)
+    casts(1)
+
     for s, peer in enumerate(p.fpeers):
         vec_copy(s, peer).wait_recv()
         wh_copy(s, peer).wait_recv()
     wht[...] = whbuf[...].astype(F32).T.astype(BF16)
     for source in range(nf):
-        rows_out[:, pl.ds(source * rows, rows)] = vecbuf[source, :, 0:rows]
-    for r in (4, 5):
-        shares = vecbuf[0, r : r + 1, 0:BLK]
-        for source in range(1, nf):
-            shares = shares + vecbuf[source, r : r + 1, 0:BLK]
-        rows_out[r : r + 1, 0:BLK] = shares
+        rows_out[:, pl.ds(source * rows, rows)] = vecbuf[source, :, 0:rows].astype(BF16).astype(F32)
+    share = HD // nf
+    shares = [vecbuf[source, 4:5, 0:share].astype(BF16).astype(F32) for source in range(nf)]
+    for source in range(nf):
+        rows_out[4:5, source * share : (source + 1) * share] = shares[source]
     vcol[...] = rows_out[...].T
-    head = c * hpd // 2
     here = pl.ds(al(head * HD, 16), HD)
     bias_q, bias_v = vcol[here, 1:2], vcol[here, 2:3]
-    factor = vcol[0:HD, 4:5]
+    factor = jnp.log(1.0 + jnp.exp(vcol[0:HD, 4:5])) * (LOG2E / math.sqrt(HD))
     factor_out[...] = jnp.broadcast_to(factor, (HD, BLK))
 
     def a_copy(slot, origin, half):
@@ -672,7 +726,7 @@
 
         @pl.loop(0, n)
         def _(d):
-            osend[u, d] = onat[rel_ref[2 * d + lay.half(u)]]
+            osend[u, d] = onat[lay.within(deal_ref, d, u)]
 
         o_swaps[u].start()
 
@@ -682,68 +736,85 @@
         for u in range(hpd)
     ]
 
-    def gather_events(i, first, last):
-        for k in range(first, last):
-            if k < zlen:
-                spread.chain(k, i)
-            spread.pair(k - 1, i)
-
-    later = min(2, zlen - 1)
-    for k in range(1, zlen + 1):
-        gather_events(0, k, k + 1)
-        if k == later:
-            spread.start(1)
-        if hpd == 2:
-            project(0, k - 1, first=k == 1)
-    pass_matrix(0)
-    if hpd == 2:
-        gather_events(1, 1, 2)
-        attend(0, [(lay.size // tile // 2, lambda: gather_events(1, 2, 3))])
-        pass_matrix(1)
-        for k in range(3, zlen + 1):
-            gather_events(1, k, k + 1)
-            project(1, k - 3)
-        for k in range(zlen - 2, zlen):
-            project(1, k)
-        attend(1, [])
-    else:
-        for k in range(1, zlen + 1):
-            gather_events(1, k, k + 1)
-            project(0, k - 1, first=k == 1)
-        attend(0, [])
-        pass_matrix(1)
-    pass_matrix(2)
-    for src, dst in zip(kept, stored[: len(kept)]):
-        stores.start(src, dst)
-
     def handed(m):
         for s, (peer, source) in enumerate(zip(p.fpeers, p.fsources)):
             ms_copy(m, s, source, 1 - core).wait_recv()
-    for m in range(3):
         for copy in keep_copies(m):
             copy.wait()
-        handed(m)
-    spread.drain()
+
     weights = [abuf.at[pl.ds(5 * m, 5)].reshape(5 * 2 * BLK, D) for m in range(3)]
     w_loads = [
         pltpu.make_async_copy(mats_out.at[m], weights[m], w_sem.at[m]) for m in range(3)
     ]
-    for copy in w_loads:
-        copy.start()
+
+    if hpd == 2:
+        project(0, 0, first=True)
+        for k in range(2, zlen + 1):
+            gather_events(0, k, k + 1)
+            if k == 2:
+                spread.start(1)
+            casts(2)
+            project(0, k - 1)
+        pass_matrix(0)
+        gather_events(1, 1, 2)
+        attend(0, [(lay.size // tile // 2, lambda: gather_events(1, 2, 3))])
+        pass_matrix(1)
+        casts(len(steps))
+        project(1, 0)
+        for k in range(3, zlen + 1):
+            gather_events(1, k, k + 1)
+            project(1, k - 2)
+        project(1, zlen - 1)
+    else:
+        spread.start(1)
+        casts(len(steps))
+        for k in range(1, zlen + 1):
+            if k > 1:
+                gather_events(0, k, k + 1)
+            gather_events(1, k, k + 1)
+            project(0, k - 1, first=k == 1)
+        pass_matrix(0)
+        pass_matrix(1)
+    spread.drain()
+    for m in range(2):
+        handed(m)
+        w_loads[m].start()
+    attend(hpd - 1, [])
+    for src, dst in zip(kept, stored):
+        stores.start(src, dst)
+    pass_matrix(2)
+    handed(2)
+    w_loads[2].start()
     for u in range(hpd):
         o_swaps[u].wait()
     w_loads[0].wait()
+
+    def stage(name):
+        if name == "ot":
+            to_twin(0, ot_t)
+        elif name == "z":
+            to_twin(2, zt)
+        elif name == "b":
+            to_twin(1, bt)
+        elif name == "out":
+            stores.start(layer, stored[7])
+        elif name == "du":
+            r_copy(1).start()
+            stores.start(du, own_r.at[1])
+        elif name == "gb":
+            r_copy(0).start()
+            stores.start(gb, own_r.at[0])
+            stores.start(dh, stored[8])
+        elif name == "gt":
+            stores.start(gt, stored[9])
+
     token_rows(
         x_ref, cot_ref, oswap, rows_out, weights, w_loads,
-        layer, dh, gt, ot_t, bt, zt, gb, du, dg2_out, o_rows, hidden, nh, b_rows, up, z, db, wide)
-    for src, dst in zip(made, stored[len(kept) :]):
-        stores.start(src, dst)
+        layer, dh, gt, ot_t, bt, zt, gb, du, dg2_out, o_rows, hidden, nh, b_rows, up, z, db, wide, stage)
 
     for m in range(3, moved):
         pass_matrix(m)
     for m in range(3, moved):
-        for copy in keep_copies(m):
-            copy.wait()
         handed(m)
     for copy in keep_copies(moved):
         copy.wait()
@@ -751,6 +822,10 @@
         for s, (peer, source) in enumerate(zip(p.fpeers, p.fsources)):
             mx_copy(m, s, peer, f).wait_send()
             ms_copy(m, s, source, core).wait_send()
+    for m in range(3):
+        r_copy(m).wait()
+        for source in range(nf):
+            t_copy(m, source).wait()
     for s, peer in enumerate(p.fpeers):
         wh_copy(s, peer).wait_send()
         vec_copy(s, peer).wait_send()
@@ -761,9 +836,9 @@
     stores.wait()
 
 
-def forward(lay, nf, within, inverse, lengths, x, cot, wh, vec, mats):
+def forward(lay, nf, deal, inverse, lengths, x, cot, vectors, mats):
     n, hpd, total = lay.n, lay.hpd, lay.rows
-    rows, tok, count = wh.shape[0], x.shape[0], len(mats)
+    rows, tok, count = mats[0].shape[0], x.shape[0], len(mats)
     dma = pltpu.SemaphoreType.DMA
     peers = max(nf - 1, 1)
     half = ((rows // 2, D), BF16)
@@ -773,23 +848,28 @@
     ]
     plain, turned, wide = ((tok, D), BF16), ((D, tok), BF16), ((tok, D), F32)
     made = [plain, wide, ((H, 2, HD, BLK), BF16), turned, turned, turned, plain, plain]
+    shared = ((3, D // 2, tok), BF16)
+    results = made[:3] + [shared, ((2, tok, D), BF16)]
     outs = [
-        ((n, 2, BLK, D), BF16), ((count - 1, nf * rows, D), BF16), half, half,
+        ((n, 2, BLK, D), BF16), ((count - 1, nf * rows, D), BF16), half, half, shared, ((3, tok, D), BF16),
         ((8, D), F32), ((HD, BLK), F32), ((1, D), F32),
-    ] + kept + made
-    places = [in_any()] * 4 + [in_vmem()] * 3 + [in_any()] * (len(kept) + len(made))
+    ] + kept + results
+    places = [in_any()] * 6 + [in_vmem()] * 3 + [in_any()] * (len(kept) + len(results))
     moves = dma((count - 1, peers))
     return pl.pallas_call(
         functools.partial(forward_kernel, lay, n, nf),
         out_shape=tuple(jax.ShapeDtypeStruct(*out) for out in outs),
-        in_specs=[in_smem()] * 3 + [in_vmem()] * 4 + [in_any()] * count,
+        in_specs=[in_smem()] * 3 + [in_vmem()] * (2 + len(vectors)) + [in_any()] * count,
         out_specs=tuple(places),
         scratch_shapes=[
             VMEM((n, 2, BLK, D), BF16),
             VMEM((2, 2, BLK, D), BF16),
-            VMEM((nf * rows, 256), BF16),
-            VMEM((256, nf * rows), BF16),
-            VMEM((nf,) + vec.shape, F32),
+            VMEM((3, rows, 2 * BLK), F32),
+            VMEM((rows, 2 * BLK), BF16),
+            VMEM((nf * rows, 2 * BLK), BF16),
+            VMEM((2 * BLK, nf * rows), BF16),
+            VMEM((8, -(-rows // BLK) * BLK), F32),
+            VMEM((nf, 8, -(-rows // BLK) * BLK), F32),
             VMEM((D, 8), F32),
             VMEM((2, rows // 2, D), F32),
             VMEM((count, 2, rows // 2, D), BF16),
@@ -804,14 +884,15 @@
             dma((4, n, 2)), dma((n, 2)), dma((peers,)), dma((peers,)), dma((peers,)), dma((peers,)),
             dma((2,)), moves, moves, moves, moves,
             dma((2,)), dma((count, 2)), dma((hpd, n)), dma((hpd, n)), dma((hpd,)),
-            dma((len(kept) + len(made),)), dma((3,)),
+            dma((len(kept) + 6 + 3 * nf,)), dma((3,)), dma((3, nf)), dma((3, nf)), dma((3,)), dma((3,)),
+            dma((3,)),
         ],
         compiler_params=pltpu.CompilerParams(
             collective_id=0, has_side_effects=True, vmem_limit_bytes=61 * MIB
         ),
         cost_estimate=cost(100),
         name="forward",
-    )(within, inverse, lengths, x, cot, wh, vec, *mats)
+    )(deal, inverse, lengths, x, cot, *vectors, *mats)
 
 
 VEC_ROWS = 24
@@ -819,14 +900,14 @@
 
 def backward_kernel(
     lay, n, nf,
-    rel_ref, inv_ref, len_ref, gt, c_ref, g1_ref, dg2_ref,
-    ot_t_in, bt_in, zt_in, gb_in, du_in, cot_in,
+    deal_ref, inv_ref, len_ref, gt, c_ref, g1_ref, dg2_ref,
+    own_t, own_r, twin_t, twin_r, cot_in,
     qraw_in, qst_in, kt_in, vt_in, kn_in, ot_in, lse_in,
     a_ref, mats_ref, mine_ref, other_ref, x_in, dh_in,
     gx_out, dw_out, fw_out, vec_out, xw_out, tw_out,
     big, sums, wide, abuf, qraw, qst, kt, vt, kn, ot, lse, x_ref, dh_ref,
     qn, vn, don, dost, delta, dk, dv, dqt, natural, part_sums, left, back, dw, dwsend, dwrecv, dwown, vx, vsum, vall,
-    ld_sem, do_send, do_recv, do_own, dq_send, dq_recv, dq_own, tw_send, tw_recv, xw_send, xw_recv, tg_send, tg_recv, a_sem,
+    ld_sem, do_send, do_recv, do_own, dq_send, dq_recv, dq_own, xw_send, xw_recv, tg_send, tg_recv, a_sem,
     x_send, x_recv, own_sem, ag_send, ag_recv, fg_send, fg_recv, v_send, v_recv, u_send, u_recv,
     *rest,
 ):
@@ -836,9 +917,24 @@
     rows = D // nf
     part = rows // 2
     loads = Loads(ld_sem)
-    ffn_rows = [abuf.at[1, pl.ds(i * 2 * BLK, 2 * BLK)] for i in range(3)]
-    ffn_loads = [loads.start(src, wide.at[m]) for m, src in enumerate((ot_t_in, bt_in, zt_in))]
-    ffn_loads += [loads.start(src, dst) for src, dst in zip((gb_in, du_in, cot_in), ffn_rows)]
+    flat = 3 * part
+    deep = 4 * BLK
+
+    def left_rows(m, source):
+        return pl.ds(al(3 * deep + m * nf * part + source * part, 16), part)
+
+    def right_rows(m):
+        return pl.ds(m * deep, deep)
+
+    ffn_loads = []
+    for m in range(3):
+        at = pl.ds(3 * deep + m * nf * part, nf * part)
+        ffn_loads += [
+            loads.start(own_t.at[m], big.at[at, pl.ds(0, 2 * BLK)]),
+            loads.start(twin_t.at[m], big.at[at, pl.ds(2 * BLK, 2 * BLK)]),
+            loads.start(own_r.at[m] if m < 2 else cot_in, big.at[pl.ds(m * deep, 2 * BLK)]),
+            loads.start(twin_r.at[m], big.at[pl.ds(m * deep + 2 * BLK, 2 * BLK)]),
+        ]
     att_loads = [
         loads.start(src, dst) for src, dst in zip(
             (qraw_in, qst_in, kt_in, vt_in, kn_in, ot_in, lse_in), (qraw, qst, kt, vt, kn, ot, lse))
@@ -867,59 +963,39 @@
         )
 
     height = sums.shape[1]
-    flat = 3 * part
     if height > flat:
         for source in range(nf):
             sums[source, flat:, :] = jnp.zeros((height - flat, D), BF16)
     for copy in ffn_loads:
         copy.wait()
-    theirs = lambda source: pl.ds(al(source * flat, 16), flat)
-    got = lambda source: pl.ds(al((nf + source) * flat, 16), flat)
-
-    def weight_grads(source, half, put):
+    reduce = Reduce(p, sums, *reduce_scratch[:6], reduce_scratch[6:])
+
+    def weight_grads(source):
         for m in range(3):
             @pl.loop(0, D // WIDE)
             def _(j):
                 sl = pl.ds(al(j * WIDE, WIDE), WIDE)
-                where = pl.ds(al(source * rows + half * part, 16), part)
-                put(m, sl, dot(wide[m, where, :], ffn_rows[m][:, sl]).astype(BF16))
-
-    def twin_copy(s, source):
-        return pltpu.make_async_remote_copy(
-            src_ref=big.at[theirs(source)], dst_ref=big.at[got(source)],
-            send_sem=tw_send.at[s], recv_sem=tw_recv.at[s],
-            device_id=(p.twin, f), device_id_type=MESH,
-        )
-
-    shards = list(enumerate(p.fpeers)) + [(nf - 1, f)]
-    for s, source in shards:
-        def put(m, sl, value, source=source):
-            big[pl.ds(al(source * flat + m * part, 16), part), sl] = value
-        weight_grads(source, 1 - p.core, put)
-        twin_copy(s, source).start()
-    reduce = Reduce(p, sums, *reduce_scratch[:6], reduce_scratch[6:])
-    for s, source in shards:
-        def put(m, sl, value, source=source):
-            sums[source, pl.ds(m * part, part), sl] = value
-        weight_grads(source, p.core, put)
-        twin_copy(s, source).wait_recv()
-        reduce.add(
-            sums.at[source, pl.ds(0, flat)],
-            [sums.at[source, pl.ds(0, flat)], big.at[got(source)]], flat)
-        if s == max(nf - 2, 0):
-            for t in range(zlen - 1):
-                reduce.start_x(t)
-    for s, source in shards:
-        twin_copy(s, source).wait_send()
-
-    w_loads = [loads.start(mats_ref.at[3 + m], big.at[pl.ds(m * D, D)]) for m in range(2)]
+                sums[source, pl.ds(m * part, part), sl] = dot(
+                    big[left_rows(m, source), 0:deep], big[right_rows(m), sl]).astype(BF16)
+
+    for peer in p.fpeers:
+        weight_grads(peer)
+    reduce.start_x(0)
+    reduce.start_x(1)
+
+    w_loads = []
+
 
     def load_w(src, source, half):
         at = pl.ds(al(2 * D + source * rows + half * part, 16), part)
         w_loads.append(loads.start(src, big.at[at]))
 
-    load_w(mine_ref, f, p.core)
-    load_w(other_ref, f, 1 - p.core)
+    def own_weight_grads():
+        weight_grads(f)
+        for m in range(2):
+            w_loads.append(loads.start(mats_ref.at[3 + m], big.at[pl.ds(m * D, D)]))
+        load_w(mine_ref, f, p.core)
+        load_w(other_ref, f, 1 - p.core)
 
     for copy in att_loads:
         copy.wait()
@@ -954,6 +1030,16 @@
     for u in range(hpd):
         base = lay.base(u)
         row0 = u * lay.size
+
+        @pl.loop(0, lay.half_blocks)
+        def _(b):
+            cols = pl.ds(al(b * BLK, BLK), BLK)
+            here = pl.ds(al(row0 + b * BLK, BLK), BLK)
+            qn[cols, :] = qst[:, here].astype(F32).T.astype(BF16)
+            vn[cols, :] = pad_rows(vt[:, here].astype(F32)).T.astype(BF16)
+            dk[cols, :] = jnp.zeros((BLK, BLK), F32)
+            dv[cols, :] = jnp.zeros((BLK, BLK), F32)
+
         do_swaps[u].wait()
 
         @pl.loop(0, lay.half_blocks)
@@ -965,10 +1051,6 @@
             block = pad_rows(block)
             dost[:, cols] = block.astype(BF16)
             don[cols, :] = block.T.astype(BF16)
-            qn[cols, :] = qst[:, here].astype(F32).T.astype(BF16)
-            vn[cols, :] = pad_rows(vt[:, here].astype(F32)).T.astype(BF16)
-            dk[cols, :] = jnp.zeros((BLK, BLK), F32)
-            dv[cols, :] = jnp.zeros((BLK, BLK), F32)
 
         @pl.loop(0, lay.size // tile)
         def _(qi):
@@ -995,10 +1077,9 @@
             if u == hpd - 1:
                 @pl.when(qi == lay.size // tile // 2 - 1)
                 def _():
-                    if hpd == 1:
-                        reduce.xy(0)
-                    reduce.after_y(0)
-                    reduce.chain(0, 0)
+                    if hpd == 2:
+                        reduce.xy(1)
+                        reduce.after_y(0)
 
         @pl.loop(0, lay.half_blocks)
         def _(b):
@@ -1017,15 +1098,23 @@
 
         @pl.loop(0, n)
         def _(d):
-            left[u, :, pl.ds(al(d * BLK, BLK), BLK)] = natural[rel_ref[2 * d + lay.half(u)]]
-
+            left[u, :, pl.ds(al(d * BLK, BLK), BLK)] = natural[lay.within(deal_ref, d, u)]
+
+        if u == 0:
+            own_weight_grads()
+        if u < hpd - 1:
+            reduce.xy(0)
+            reduce.start_x(2)
         gradient_swap(u).start()
         if u < hpd - 1:
-            reduce.xy(0)
             for k, (unit, _) in enumerate(steps):
                 if unit == u:
                     weights_of_head(k)
-    reduce.xy(1)
+    if hpd == 1:
+        reduce.xy(0)
+        reduce.xy(1)
+        reduce.start_x(2)
+        reduce.after_y(0)
 
     for k, (unit, _) in enumerate(steps):
         if unit == hpd - 1:
@@ -1042,12 +1131,17 @@
 
     for s, peer in enumerate(p.fpeers):
         x_copy(s, peer).start()
-    reduce.start_x(zlen - 1)
+    for t in range(3, zlen):
+        reduce.start_x(t)
     for s, peer in enumerate(p.fpeers):
         xw_copy(s, peer).start()
 
-    spread = Spread(p, dw_out, ag_send, ag_recv, 3)
-    spread2 = Spread(p, fw_out, fg_send, fg_recv, fw_out.shape[1])
+    pieces = fw_out.shape[1]
+    result = reduce_scratch[0]
+    cut = height // zlen // pieces
+    spread = Spread(p, dw_out, ag_send, ag_recv, 3, lambda i: dwown.at[i], own_sem.at[0])
+    spread2 = Spread(
+        p, fw_out, fg_send, fg_recv, pieces, lambda i: result.at[pl.ds(i * cut, cut)], own_sem.at[1])
 
     def start_spread():
         total = dwsend[f].astype(F32)
@@ -1056,78 +1150,69 @@
             total = total + dwrecv[s].astype(F32)
         for i in range(3):
             dwown[i] = total[i * HD : (i + 1) * HD].astype(BF16)
-        own = pltpu.make_async_copy(dwown, dw_out.at[c], own_sem)
-        own.start()
-        own.wait()
-        for i in range(3):
             spread.start(i)
 
-    for t in range(2, 2 * zlen - 1):
-        if t < zlen:
-            reduce.xy(t)
-        if t <= zlen:
-            reduce.after_y(t - 1)
-            reduce.chain(t - 1, 0)
-        for hop in range(1, zlen - 1):
-            if 0 <= t - 1 - hop < zlen:
-                reduce.chain(t - 1 - hop, hop)
-        if t == 2:
-            start_spread()
-        if 1 <= t - 2 < zlen:
-            for i in range(3):
-                spread.chain(t - 2, i)
-                spread.pair(t - 3, i)
-    reduce.last()
-    result = reduce_scratch[0]
-    pieces = fw_out.shape[1]
-    own = [
-        pltpu.make_async_copy(result.at[pl.ds(i * (height // zlen // pieces), height // zlen // pieces)],
-                              fw_out.at[c, i], own_sem)
-        for i in range(pieces)
-    ]
-    for i in range(pieces):
-        own[i].start()
-        own[i].wait()
-        spread2.start(i)
-    done = max(2 * zlen - 4, 0)
-    for k in range(1, zlen):
-        if k > min(done, zlen - 1):
+    def spread_events(k):
+        if 1 <= k < zlen:
             for i in range(3):
                 spread.chain(k, i)
                 spread.pair(k - 1, i)
+
+    def gather_rows():
+        for u in range(hpd):
+            gradient_swap(u).wait()
+        for m in range(3):
+            for i in range(2):
+                for h in range(H):
+                    block = back[i, h] if hpd == 2 else back[0, 2 * h + i]
+                    wide[m, pl.ds(h * HD, HD), pl.ds(i * BLK, BLK)] = block[m * HD : (m + 1) * HD]
+        for copy in w_loads[:2]:
+            copy.wait()
+
+    def row_grads(mats, more):
+        @pl.loop(0, D // WIDE)
+        def _(j):
+            at = pl.ds(al(j * WIDE, WIDE), WIDE)
+            total = None
+            for m in mats:
+                term = dot(big[pl.ds(al(m * D + j * WIDE, WIDE), WIDE), :], wide[m])
+                total = term if total is None else total + term
+            total = total.T
+            gx_out[:, at] = gx_out[:, at] + total if more else total
+
+    for t in range(2, zlen):
+        reduce.after_y(t - 1)
+        reduce.xy(t)
+        if t == 2:
+            start_spread()
+        else:
+            spread_events(t - 2)
+    gather_rows()
+    row_grads((0, 1), False)
+    reduce.after_y(zlen - 1)
+    for k in range(zlen - 2, zlen):
+        spread_events(k)
+    reduce.last()
+    for i in range(pieces):
+        spread2.start(i)
+    for i in range(3):
+        spread.pair(zlen - 1, i)
 
     for s, (peer, source) in enumerate(zip(p.fpeers, p.fsources)):
         xw_copy(s, peer).wait_recv()
         tg_copy(s).start()
         load_w(xw_out.at[s], source, p.core)
-
-    for u in range(hpd):
-        gradient_swap(u).wait()
-    for m in range(3):
-        for i in range(2):
-            for h in range(H):
-                block = back[i, h] if hpd == 2 else back[0, 2 * h + i]
-                wide[m, pl.ds(h * HD, HD), pl.ds(i * BLK, BLK)] = block[m * HD : (m + 1) * HD]
+    for copy in row_loads:
+        copy.wait()
     for s, source in enumerate(p.fsources):
         tg_copy(s).wait_recv()
         load_w(tw_out.at[s], source, 1 - p.core)
-    for copy in w_loads:
+    for copy in w_loads[2:]:
         copy.wait()
-
-    @pl.loop(0, D // WIDE)
-    def _(j):
-        def rows_of(m):
-            return big[pl.ds(al(m * D + j * WIDE, WIDE), WIDE), :]
-        total = dot(rows_of(0), wide[0]) + dot(rows_of(1), wide[1]) + dot(rows_of(2), wide[2])
-        gx_out[:, pl.ds(al(j * WIDE, WIDE), WIDE)] = total.T
-
-    for i in range(3):
-        spread.pair(zlen - 1, i)
+    row_grads((2,), True)
     for i in range(pieces):
         spread2.chain(1, i)
         spread2.pair(0, i)
-    for copy in row_loads:
-        copy.wait()
     x = x_ref[...].astype(F32)
     r1 = lax.rsqrt(jnp.mean(x * x, axis=-1, keepdims=True) + EPS)
     na = x * r1
@@ -1149,7 +1234,7 @@
 
     for s, peer in enumerate(p.fpeers):
         v_copy(s, peer, f).start()
-    scaled = da * g1_ref[...]
+    scaled = da * g1_ref[0:1, :]
     mean = jnp.mean(scaled * na, axis=-1, keepdims=True)
     gx_out[...] = dh_ref[...] + r1 * (scaled - na * mean)
     for s, (peer, source) in enumerate(zip(p.fpeers, p.fsources)):
@@ -1161,7 +1246,7 @@
         return pltpu.make_async_remote_copy(
             src_ref=vsum, dst_ref=vall.at[block],
             send_sem=u_send.at[s], recv_sem=u_recv.at[s],
-            device_id=((c + s) % n, f), device_id_type=MESH,
+            device_id=(c ^ s, f), device_id_type=MESH,
         )
 
     for s in range(1, n):
@@ -1177,7 +1262,7 @@
             when(guard, lambda zz=zz: spread.from_twin(zz))
             when(guard, lambda zz=zz: spread2.from_twin(zz))
     for s in range(1, n):
-        u_copy(s, (c + n - s) % n).wait_recv()
+        u_copy(s, c ^ s).wait_recv()
     vec_out[...] = vall[...]
 
     for u in range(hpd):
@@ -1195,7 +1280,7 @@
         u_copy(s, c).wait_send()
 
 
-def backward(lay, nf, within, inverse, lengths, gt, factor, g1, dg2, ffn_parts, cot, kept, tokens, mats, mine, other, x, dh):
+def backward(lay, nf, deal, inverse, lengths, gt, factor, g1, dg2, ffn_parts, cot, kept, tokens, mats, mine, other, x, dh):
     n, hpd, rows, size = lay.n, lay.hpd, lay.rows, lay.size
     dma = pltpu.SemaphoreType.DMA
     shard = D // nf
@@ -1216,7 +1301,7 @@
             jax.ShapeDtypeStruct((peers, part, D), BF16),
             jax.ShapeDtypeStruct((peers, part, D), BF16),
         ),
-        in_specs=[in_smem()] * 3 + [in_vmem()] * 4 + [in_any()] * 19,
+        in_specs=[in_smem()] * 3 + [in_vmem()] * 4 + [in_any()] * 18,
         out_specs=(in_vmem(), in_any(), in_any(), in_vmem(), in_any(), in_any()),
         scratch_shapes=[
             VMEM((3 * D, D), BF16), VMEM((nf, height, D), BF16), VMEM((3, D, tok), BF16),
@@ -1230,9 +1315,9 @@
             VMEM((hpd, n, 3 * HD, BLK), BF16), VMEM((3 * HD, D), F32), VMEM((nf, 3 * HD, shard), BF16),
             VMEM((peers, 3 * HD, shard), BF16), VMEM((3, HD, shard), BF16),
             VMEM((nf, VEC_ROWS, BLK), F32), VMEM((VEC_ROWS, BLK), F32), VMEM((n, VEC_ROWS, BLK), F32),
-            dma((15 + 6 * nf,)), dma((hpd, n)), dma((hpd, n)), dma((hpd,)), dma((hpd, n)), dma((hpd, n)), dma((hpd,)),
-            dma((nf,)), dma((nf,)), dma((peers,)), dma((peers,)), dma((peers,)), dma((peers,)), dma((2,)),
-            dma((peers,)), dma((peers,)), dma, dma((4, n, 3)), dma((n, 3)), dma((4, n, pieces)), dma((n, pieces)),
+            dma((25 + 2 * nf,)), dma((hpd, n)), dma((hpd, n)), dma((hpd,)), dma((hpd, n)), dma((hpd, n)), dma((hpd,)),
+            dma((peers,)), dma((peers,)), dma((peers,)), dma((peers,)), dma((2,)),
+            dma((peers,)), dma((peers,)), dma((2, 3)), dma((4, n, 3)), dma((n, 3)), dma((4, n, pieces)), dma((n, pieces)),
             dma((peers,)), dma((peers,)), dma((n,)), dma((n,)),
         ] + [VMEM((n, HD, BLK), BF16)] * hpd + Reduce.scratch(nf, zlen, height),
         compiler_params=pltpu.CompilerParams(
@@ -1240,139 +1325,126 @@
         ),
         cost_estimate=cost(130),
         name="backward",
-    )(within, inverse, lengths, gt, factor, g1, dg2, *ffn_parts, cot, *kept, tokens, mats, mine, other, x, dh)
-
-
-def turn_kernel(hpd, dw_ref, q_ref, k_ref, v_ref, wide):
-    j = pl.program_id(0)
-
-    @pl.when(j == 0)
-    def _():
-        for m in range(3):
-            for h in range(H):
-                if hpd == 2:
-                    block = dw_ref[h, m].astype(F32)
-                else:
-                    block = dw_ref[2 * h, m].astype(F32) + dw_ref[2 * h + 1, m].astype(F32)
-                wide[m, pl.ds(h * HD, HD), :] = block
-
-    for m, out in enumerate((q_ref, k_ref, v_ref)):
-        out[...] = wide[m, pl.ds(al(j * WIDE, WIDE), WIDE), :].T
-
-
-def turn(hpd, dw):
-    n, _, _, rows = dw.shape
-    spec = pl.BlockSpec((rows, WIDE), lambda j: (0, j))
+    )(deal, inverse, lengths, gt, factor, g1, dg2, *ffn_parts, cot, *kept, tokens, mats, mine, other, x, dh)
+
+
+def results_kernel(
+    n, nf, hpd,
+    dw_in, pieces_in, vec_ref, scale_ref,
+    q_out, k_out, v_out, o_out, u_out, d_out, ga_out, bq_out, bv_out, gf_out, sc_out,
+    dw, pieces, wide, full, tail, ld_sem, st_sem,
+):
+    f = lax.axis_index("fsdp")
+    rows = dw.shape[3]
+    part = rows // 2
+    zlen, height = pieces.shape[0], pieces.shape[3]
+    loads = Loads(ld_sem)
+    piece_load = loads.start(pieces_in, pieces)
+    dw_load = loads.start(dw_in, dw)
+    stores = Loads(st_sem)
+
+    piece_load.wait()
+    for m, out in enumerate((o_out, u_out, d_out)):
+        for core in range(2):
+            for y in range(2):
+                for z in range(zlen):
+                    first, last = max(m * part, z * height), min((m + 1) * part, (z + 1) * height)
+                    if first < last:
+                        at = core * part + first - m * part
+                        full[m, at : at + last - first, y * (D // 2) : (y + 1) * (D // 2)] = pieces[
+                            z, y, core, first - z * height : last - z * height, :
+                        ].astype(F32)
+        stores.start(full.at[m], out)
+
+    dw_load.wait()
+    for m, out in enumerate((q_out, k_out, v_out)):
+        for h in range(H):
+            if hpd == 2:
+                block = dw[h, m].astype(F32)
+            else:
+                block = dw[2 * h, m].astype(F32) + dw[2 * h + 1, m].astype(F32)
+            wide[pl.ds(h * HD, HD), :] = block
+        for j in range(D // WIDE):
+            full[3 + m, :, j * WIDE : (j + 1) * WIDE] = wide[j * WIDE : (j + 1) * WIDE, :].T
+        stores.start(full.at[3 + m], out)
+
+    tail[...] = jnp.zeros_like(tail)
+    total = jnp.sum(vec_ref[...], axis=0)
+    for r in range(D // BLK):
+        tail[0:1, r * BLK : (r + 1) * BLK] = total[r : r + 1]
+        tail[1:2, r * BLK : (r + 1) * BLK] = total[D // BLK + r : D // BLK + r + 1]
+    for r in (21, 22):
+        for h in range(H):
+            if hpd == 2:
+                row = vec_ref[h, r : r + 1, 0:HD]
+            else:
+                row = vec_ref[2 * h, r : r + 1, 0:HD] + vec_ref[2 * h + 1, r : r + 1, 0:HD]
+            tail[r - 19 : r - 18, h * HD : (h + 1) * HD] = row
+    scale = scale_ref[4:5, 0:BLK]
+    tail[4:5, 0:BLK] = total[20:21] * (1.0 / (1.0 + jnp.exp(-scale))) * (LOG2E / math.sqrt(HD))
+    share = HD // nf
+    for source in range(nf):
+        @pl.when(f == source)
+        def _():
+            for r, out in enumerate((ga_out, gf_out, bq_out, bv_out)):
+                for k in range(out.shape[0]):
+                    at = source * rows + k * BLK
+                    out[k : k + 1, :] = tail[r : r + 1, at : at + BLK]
+            sc_out[...] = tail[4:5, source * share : source * share + BLK]
+    stores.wait()
+
+
+def results(n, nf, hpd, dw, pieces, vectors, scale):
+    rows = dw.shape[3]
+    zlen = n // 4
+    height = pieces.shape[1] * pieces.shape[2]
+    pieces = pieces.reshape(zlen, 2, 2, height, D // 2)
+    dma = pltpu.SemaphoreType.DMA
+    mat, row = jax.ShapeDtypeStruct((rows, D), F32), jax.ShapeDtypeStruct((-(-rows // BLK), BLK), F32)
     return pl.pallas_call(
-        functools.partial(turn_kernel, hpd),
-        grid=(D // WIDE,),
-        out_shape=tuple([jax.ShapeDtypeStruct((rows, D), F32)] * 3),
-        in_specs=[pl.BlockSpec((n, 3, HD, rows), lambda j: (0, 0, 0, 0))],
-        out_specs=(spec, spec, spec),
-        scratch_shapes=[VMEM((3, D, rows), F32)],
+        functools.partial(results_kernel, n, nf, hpd),
+        out_shape=(mat,) * 6 + (row,) * 4 + (jax.ShapeDtypeStruct((1, BLK), F32),),
+        in_specs=[in_any(), in_any(), in_vmem(), in_vmem()],
+        out_specs=(in_any(),) * 6 + (in_vmem(),) * 5,
+        scratch_shapes=[
+            VMEM(dw.shape, BF16), VMEM(pieces.shape, BF16), VMEM((D, rows), F32), VMEM((6, rows, D), F32),
+            VMEM((8, D + 2 * BLK), F32), dma((2,)), dma((6,)),
+        ],
         compiler_params=pltpu.CompilerParams(vmem_limit_bytes=60 * MIB),
-        cost_estimate=cost(6),
-        name="turn",
-    )(dw)
-
-
-def widen_kernel(zlen, part, in_ref, o_ref, u_ref, d_ref):
-    j, y = pl.program_id(0), pl.program_id(1)
-    height = in_ref.shape[3]
-    for m, out in enumerate((o_ref, u_ref, d_ref)):
-        for z in range(zlen):
-            first, last = max(m * part, z * height), min((m + 1) * part, (z + 1) * height)
-            if first < last:
-                out[first - m * part : last - m * part, :] = in_ref[
-                    z, y, j, first - z * height : last - z * height, :
-                ].astype(F32)
-
-
-def widen(zlen, part, pieces):
-    half = pieces.shape[-1]
-    height = pieces.shape[1] * pieces.shape[2]
-    spec = pl.BlockSpec((part, half), lambda j, y: (j, y))
-    return pl.pallas_call(
-        functools.partial(widen_kernel, zlen, part),
-        grid=(2, 2),
-        out_shape=tuple([jax.ShapeDtypeStruct((2 * part, D), F32)] * 3),
-        in_specs=[pl.BlockSpec((zlen, 2, 2, height, half), lambda j, y: (0, 0, 0, 0, 0))],
-        out_specs=(spec, spec, spec),
-        compiler_params=pltpu.CompilerParams(vmem_limit_bytes=60 * MIB),
-        cost_estimate=cost(5),
-        name="widen",
-    )(pieces.reshape(zlen, 2, 2, height, half))
+        cost_estimate=cost(11),
+        name="results",
+    )(dw, pieces, vectors, scale)
 
 
 def local(
     n, nf, tokens, cotangent, lengths, deal, gain_attn, query_weight, query_bias, key_weight,
     value_weight, value_bias, query_scale, proj_weight, gain_ffn, up_weight, down_weight,
 ):
-    c = lax.axis_index("ctx")
-    f = lax.axis_index("fsdp")
     lay = Layout(n, deal.shape[0])
-    head = c * lay.hpd // 2
     rows = query_weight.shape[0]
     x, cot = tokens[0], cotangent[0]
 
-    def low(v):
-        return lax.reduce_precision(v, exponent_bits=8, mantissa_bits=7)
-
-    g1_own = low(gain_attn)
-    slices = [
-        lax.dynamic_slice(w, (0, head * HD), (rows, HD)) for w in (query_weight, key_weight, value_weight)
-    ]
-    wh = jnp.pad(jnp.concatenate(slices, axis=1), ((0, 0), (0, 256 - 3 * HD))).astype(BF16)
-    scale = low(query_scale)
-    factor = jnp.log(1.0 + jnp.exp(scale)) * (LOG2E / math.sqrt(HD))
-    shares = lax.dynamic_update_slice(
-        jnp.zeros((2, rows), F32), jnp.stack([factor, scale]), (0, f * query_scale.shape[0]))
-    vec = jnp.concatenate(
-        [jnp.stack([g1_own, low(query_bias), low(value_bias), low(gain_ffn)]), shares])
-    vec = jnp.pad(vec, ((0, 2), (0, -rows % 128)))
+    def in_rows(v):
+        return jnp.pad(v, (0, -v.shape[0] % BLK)).reshape(-1, BLK)
+
+    vectors = tuple(in_rows(v) for v in (gain_attn, query_bias, value_bias, gain_ffn, query_scale))
     blocks = jnp.arange(deal.shape[0], dtype=jnp.int32)
     inverse = jnp.sum(jnp.where(deal[None, :] == blocks[:, None], blocks[None, :] // 2, 0), axis=1, dtype=jnp.int32)
-    within = deal % lay.half_blocks
-
-    a_all, mats, mine, other, whole, factor_col, dg2, *stored = forward(
-        lay, nf, within, inverse, lengths, x, cot, wh, vec,
+
+    a_all, mats, mine, other, twin_t, twin_r, whole, factor_col, dg2, *stored = forward(
+        lay, nf, deal, inverse, lengths, x, cot, vectors,
         (proj_weight, up_weight, down_weight, query_weight, key_weight, value_weight),
     )
-    kept, (layer_out, dh, gt, ott, bt, zt, gb, du) = stored[:7], stored[7:]
-    g1 = whole[0:1]
-    q_param = whole[5, :HD]
-
-    grad_x, dw, pieces, vectors, *_ = backward(
-        lay, nf, within, inverse, lengths, gt.reshape(n, lay.hpd, HD, BLK), factor_col, g1, dg2,
-        (ott, bt, zt, gb, du), cot, kept, a_all, mats, mine, other, x, dh,
+    kept, (layer_out, dh, gt, own_t, own_r) = stored[:7], stored[7:]
+    grad_x, dw, pieces, sums, *_ = backward(
+        lay, nf, deal, inverse, lengths, gt.reshape(n, lay.hpd, HD, BLK), factor_col, whole, dg2,
+        (own_t, own_r, twin_t, twin_r), cot, kept, a_all, mats, mine, other, x, dh,
     )
-    dwq, dwk, dwv = turn(lay.hpd, dw)
-    grads = widen(n // 4, rows // 2, pieces)
-
-    def own(v):
-        size = v.shape[0] // nf
-        return lax.dynamic_slice(v, (f * size,), (size,))
-
-    def of_heads(r):
-        return vectors[:, r, :HD].reshape(H, 2 // lay.hpd, HD).sum(axis=1).reshape(D)
-
-    gains = jnp.sum(vectors[:, : 2 * D // BLK], axis=0).reshape(2, D)
-    grad_scale = jnp.sum(vectors[:, 20, :HD], axis=0) * jax.nn.sigmoid(q_param) * (LOG2E / math.sqrt(HD))
-    return (
-        layer_out[None],
-        grad_x[None],
-        own(gains[0]),
-        dwq,
-        own(of_heads(21)),
-        dwk,
-        dwv,
-        own(of_heads(22)),
-        own(grad_scale),
-        grads[0],
-        own(gains[1]),
-        grads[1],
-        grads[2],
-    )
+    dwq, dwk, dwv, dwo, dw1, dw2, ga, bq, bv, gf, scale = results(
+        n, nf, lay.hpd, dw, pieces, sums, whole)
+    ga, bq, bv, gf = (v.reshape(-1)[:rows] for v in (ga, bq, bv, gf))
+    scale = scale.reshape(-1)[: query_scale.shape[0]]
+    return layer_out[None], grad_x[None], ga, dwq, bq, dwk, dwv, bv, scale, dwo, gf, dw1, dw2
 
 
 def solution(mesh):

time: 315 us -> 292 us (0.927)
  Pallas kernels: 294 us -> 283 us
  other arithmetic: 9.49 us -> 1.28 us
  local copies, waits for them, and re-layouts: 10.1 us -> 4.24 us
    pallas_call x1, Pallas kernels: 162 us -> 157 us  [backward(): pl.pallas_call(functools.partial(backward_kernel, lay, n, nf), out_shape=...]
    dynamic_slice x5 -> x0, local copies, waits for them, and re-layouts: 3.26 us -> none  [own(): return lax.dynamic_slice(v, (f * size,), (size,))]
    pallas_call x2 -> x1, Pallas kernels: 14.4 us -> 11.2 us  [results(): pl.pallas_call(functools.partial(results_kernel, n, nf, hpd), out_shape=(...]
where the time goes in v5:
time: 292 us; the launch traced here: 290 us
  Pallas kernels  283 us (97%)
  local copies, waits for them, and re-layouts  4.24 us (1%)
    pallas_call x1, Pallas kernels, backward(): pl.pallas_call(functools.partial(backward_kernel, lay, n, nf), out_shape=...  157 us
    pallas_call x1, Pallas kernels, forward(): pl.pallas_call(functools.partial(forward_kernel, lay, n, nf), out_shape=t...  116 us
    pallas_call x1, Pallas kernels, results(): pl.pallas_call(functools.partial(results_kernel, n, nf, hpd), out_shape=(...  11.2 us

profile of v5, /device:TPU:0, one launch (start us, length us, event | category | flops | bytes accessed | tf_op | source)
XLA Modules:
  0.0 289.5 jit_solution(5165302777486937392)
XLA Ops:
  0.6 1.2 pad_bitcast_fusion.rest_4_
  1.8 1.3 select_reduce_fusion.inv_ref
  3.1 115.6 %forward.1 = (bf16[16,2,128,1280]{3,2,1,0:T(8,128)(2,1)}, bf16[5,1280,1280]{2,1,0:T(8,128)(2,1)}, bf16[320,1280]{1,0:T(8,128)(2,1)}, bf16[320,1280]{1,0:T(8,128)...) custom-call(s32[32]{0:T(128)} %deal_ref.3, ...), custom_call_target="tpu_custom_call" | custom-call | bytes 300000000 | tf_op jit(solution)/shard_map/forward/pallas_call | solution.py:859
  118.7 156.5 %backward.1 = (f32[256,1280]{1,0:T(8,128)}, bf16[16,3,80,640]{3,2,1,0:T(8,128)(2,1)}, bf16[16,3,80,640]{3,2,1,0:T(8,128)(2,1)}, f32[16,24,128]{2,1,0:T(8,128)}, ...) custom-call(s32[32]{0:T(128)} %deal_ref.3, s32[32]{0:T(128)} %select_reduce_fusion.inv_ref, s32[1,8]{1,0:T(1,128)} %len_ref.3, ...), custom_call_target="tpu_custom_call" | custom-call | bytes 390000000 | tf_op jit(solution)/shard_map/backward/pallas_call | solution.py:1294
  275.3 0.0 copy-start.1
  275.3 0.0 copy-start
  275.3 11.2 %results.1 = (f32[640,1280]{1,0:T(8,128)}, f32[640,1280]{1,0:T(8,128)}, f32[640,1280]{1,0:T(8,128)}, f32[640,1280]{1,0:T(8,128)}, f32[640,1280]{1,0:T(8,128)}, /...) custom-call(bf16[16,3,80,640]{3,2,1,0:T(8,128)(2,1)} %get-tuple-elem, ...), custom_call_target="tpu_custom_call" | custom-call | bytes 33000000 | tf_op jit(solution)/shard_map/results/pallas_call | solution.py:1404
  286.5 1.2 slice_bitcast_fusion
  287.6 0.0 copy-done.1
  287.6 0.8 copy.30
  288.5 0.0 copy-done
  288.5 1.1 copy.31
  (1 shorter events, 0.0 us)
Async XLA Ops:
  275.3 12.4 %copy-start.1 = (bf16[256,1280]{1,0:T(8,128)(2,1)S(1)}, bf16[256,1280]{1,0:T(8,128)(2,1)}, u32[]{:S(2)}) copy-start(bf16[256,1280]{1,0:T(8,128)(2,1)} %get-tuple-element.49) | copy-start | bytes 1966084
  275.3 13.2 %copy-start = (f32[256,1280]{1,0:T(8,128)S(1)}, f32[256,1280]{1,0:T(8,128)}, u32[]{:S(2)}) copy-start(f32[256,1280]{1,0:T(8,128)} %get-tuple-element.70) | copy-start | bytes 3932164

commit v6 on v5

--- a/solution.py
+++ b/solution.py
@@ -107,7 +107,8 @@
 
 
 class Spread:
-    def __init__(self, place, buf, send_sem, recv_sem, pieces, own=None, own_sem=None):
+    def __init__(self, place, buf, send_sem, recv_sem, pieces, wide=(), own=None, own_sem=None):
+        self.wide = wide
         self.p, self.buf, self.send_sem, self.recv_sem, self.pieces = place, buf, send_sem, recv_sem, pieces
         self.own, self.own_sem = own, own_sem
 
@@ -142,16 +143,27 @@
                 origin = p.idx(zz, p.y, p.core)
                 self.arrive(origin, i)
                 self.send(1 if sign == 1 else 0, origin, i)
-                self.send(2, origin, i)
+                when(self.crosses(zz, i), lambda: self.send(2, origin, i))
                 self.send(3, origin, i)
             when(guard, body)
 
+    def crosses(self, zz, i):
+        return (zz > 0) & (zz < self.p.zlen - 1) if i in self.wide else None
+
+    def both_chains(self, zz, sign, i, act):
+        if i in self.wide:
+            p, origin = self.p, self.p.idx(zz, 1 - self.p.y, self.p.core)
+            for way, end, signs in ((0, 0, (0, -1)), (1, p.zlen - 1, (0, 1))):
+                if sign in signs:
+                    pl.when((zz == end) & p.guards[way])(lambda way=way: act(way, origin, i))
+
     def pair(self, k, i):
         p = self.p
-        for zz, guard, _ in p.level(k):
-            def body(zz=zz):
+        for zz, guard, sign in p.level(k):
+            def body(zz=zz, sign=sign):
                 origin = p.idx(zz, 1 - p.y, p.core)
                 self.arrive(origin, i)
+                self.both_chains(zz, sign, i, lambda way, o, i: self.copy(way, o, i).start())
                 self.send(3, origin, i)
             when(guard, body)
 
@@ -175,8 +187,9 @@
                             origin = p.idx(zz, p.y, p.core)
                             on = 1 if sign == 1 else 0
                             when(p.guards[on], lambda: self.copy(on, origin, i).wait_send())
-                            self.copy(2, origin, i).wait_send()
+                            when(self.crosses(zz, i), lambda: self.copy(2, origin, i).wait_send())
                             self.copy(3, origin, i).wait_send()
+                        self.both_chains(zz, sign, i, lambda way, o, i: self.copy(way, o, i).wait_send())
                         self.copy(3, p.idx(zz, 1 - p.y, p.core), i).wait_send()
                     when(guard, body)
 
@@ -485,7 +498,8 @@
     for copy in window_loads:
         copy.start()
     vec_ref[...] = jnp.zeros_like(vec_ref)
-    for r, ref in enumerate(row_refs):
+    vec_ref[4:5, 0 : row_refs[4].shape[0]] = row_refs[4][...].reshape(1, -1)
+    for r, ref in enumerate(row_refs[:4]):
         for k in range(ref.shape[0]):
             vec_ref[r : r + 1, k * BLK : (k + 1) * BLK] = ref[k : k + 1, :]
     p.greet_all(True)
@@ -691,7 +705,7 @@
             qst[:, cols] = pad_rows(qr * factor).astype(BF16)
             kt[:, cols] = kr.astype(BF16)
             vt[:, cols] = vr.astype(BF16)
-            kn[cols, :] = pad_rows(kr).T.astype(BF16)
+            kn[cols, :] = pad_rows(kr.astype(BF16)).T
 
         @pl.loop(0, lay.size // tile)
         def _(qi):
@@ -702,19 +716,29 @@
             l_ref[...] = jnp.zeros_like(l_ref)
             acc_ref[...] = jnp.zeros_like(acc_ref)
 
-            @pl.loop(0, qi + 1)
-            def _(j):
-                keys = pl.ds(al(row0 + j * tile, tile), tile)
-                s = dot(kn[keys, :], qst[:, cols])
-                token = j * tile + lax.broadcasted_iota(jnp.int32, (tile, 1), 0)
-                s = jnp.where((token >= start) & (token <= t_row), s, NEG)
-                m_old = m_ref[...]
+            def visit(key0, count, ahead, causal):
+                keys = pl.ds(al(row0 + key0, count), count)
+                side = slice(ahead, tile)
+                s = dot(kn[keys, :], qst[:, pl.ds(al(row0 + qi * tile + ahead, BLK), tile - ahead)])
+                token = key0 + lax.broadcasted_iota(jnp.int32, (count, 1), 0)
+                seen = token >= start[:, side]
+                if causal:
+                    seen = seen & (token <= t_row[:, side])
+                s = jnp.where(seen, s, NEG)
+                m_old = m_ref[:, side]
                 m_new = jnp.maximum(m_old, jnp.max(s, axis=0, keepdims=True))
                 prob = jnp.exp(s - m_new)
                 shrink = jnp.exp(m_old - m_new)
-                m_ref[...] = m_new
-                l_ref[...] = l_ref[...] * shrink + jnp.sum(prob, axis=0, keepdims=True)
-                acc_ref[...] = acc_ref[...] * shrink + dot(vt[:, keys], prob.astype(BF16))
+                m_ref[:, side] = m_new
+                l_ref[:, side] = l_ref[:, side] * shrink + jnp.sum(prob, axis=0, keepdims=True)
+                acc_ref[:, side] = acc_ref[:, side] * shrink + dot(vt[:, keys], prob.astype(BF16))
+
+            @pl.loop(0, qi)
+            def _(j):
+                visit(j * tile, tile, 0, False)
+
+            visit(qi * tile, tile // 2, 0, True)
+            visit(qi * tile + tile // 2, tile // 2, tile // 2, True)
 
             out = acc_ref[...] / l_ref[...]
             ot[:, cols] = out
@@ -1035,8 +1059,8 @@
         def _(b):
             cols = pl.ds(al(b * BLK, BLK), BLK)
             here = pl.ds(al(row0 + b * BLK, BLK), BLK)
-            qn[cols, :] = qst[:, here].astype(F32).T.astype(BF16)
-            vn[cols, :] = pad_rows(vt[:, here].astype(F32)).T.astype(BF16)
+            qn[cols, :] = qst[:, here].T
+            vn[cols, :] = pad_rows(vt[:, here]).T
             dk[cols, :] = jnp.zeros((BLK, BLK), F32)
             dv[cols, :] = jnp.zeros((BLK, BLK), F32)
 
@@ -1048,25 +1072,27 @@
             here = pl.ds(al(row0 + b * BLK, BLK), BLK)
             block = dob[u][inv_ref[b + lay.half(u) * lay.half_blocks]].astype(F32)
             delta[:, cols] = jnp.sum(block * ot[:, here], axis=0, keepdims=True)
-            block = pad_rows(block)
-            dost[:, cols] = block.astype(BF16)
-            don[cols, :] = block.T.astype(BF16)
+            block = pad_rows(block.astype(BF16))
+            dost[:, cols] = block
+            don[cols, :] = block.T
 
         @pl.loop(0, lay.size // tile)
         def _(qi):
-            cols = pl.ds(al(qi * tile, tile), tile)
-            here = pl.ds(al(row0 + qi * tile, tile), tile)
             t_row = qi * tile + lax.broadcasted_iota(jnp.int32, (1, tile), 1)
             start = seq_start(ends, base, t_row)
-            dqt[:, cols] = jnp.zeros((HD, tile), F32)
-
-            @pl.loop(0, qi + 1)
-            def _(j):
-                keys = pl.ds(al(j * tile, tile), tile)
-                keys_here = pl.ds(al(row0 + j * tile, tile), tile)
+            dqt[:, pl.ds(al(qi * tile, tile), tile)] = jnp.zeros((HD, tile), F32)
+
+            def visit(key0, count, ahead, causal):
+                side = slice(ahead, tile)
+                cols = pl.ds(al(qi * tile + ahead, BLK), tile - ahead)
+                here = pl.ds(al(row0 + qi * tile + ahead, BLK), tile - ahead)
+                keys = pl.ds(al(key0, count), count)
+                keys_here = pl.ds(al(row0 + key0, count), count)
                 s = dot(kn[keys_here, :], qst[:, here])
-                token = j * tile + lax.broadcasted_iota(jnp.int32, (tile, 1), 0)
-                seen = (token >= start) & (token <= t_row)
+                token = key0 + lax.broadcasted_iota(jnp.int32, (count, 1), 0)
+                seen = token >= start[:, side]
+                if causal:
+                    seen = seen & (token <= t_row[:, side])
                 prob = jnp.exp(jnp.where(seen, s - lse[:, here], NEG))
                 dp = dot(vn[keys, :], dost[:, cols])
                 ds = (prob * (dp - delta[:, cols])).astype(BF16)
@@ -1074,6 +1100,13 @@
                 dk[keys, :] += dot(ds, qn[cols, :])
                 dqt[:, cols] += dot(kt[:, keys_here], ds)
 
+            @pl.loop(0, qi)
+            def _(j):
+                visit(j * tile, tile, 0, False)
+
+            visit(qi * tile, tile // 2, 0, True)
+            visit(qi * tile + tile // 2, tile // 2, tile // 2, True)
+
             if u == hpd - 1:
                 @pl.when(qi == lay.size // tile // 2 - 1)
                 def _():
@@ -1087,8 +1120,8 @@
             here = pl.ds(al(row0 + b * BLK, BLK), BLK)
             dqs = dqt[:, cols]
             dq = (dqs * c_ref[...]).astype(BF16)
-            dkt = dk[cols, :].T[:HD].astype(BF16)
-            dvt = dv[cols, :].T[:HD].astype(BF16)
+            dkt = dk[cols, :].astype(BF16).T[:HD]
+            dvt = dv[cols, :].astype(BF16).T[:HD]
             natural[b, 0:HD] = dq
             natural[b, HD : 2 * HD] = dkt
             natural[b, 2 * HD : 3 * HD] = dvt
@@ -1106,19 +1139,14 @@
             reduce.xy(0)
             reduce.start_x(2)
         gradient_swap(u).start()
-        if u < hpd - 1:
-            for k, (unit, _) in enumerate(steps):
-                if unit == u:
-                    weights_of_head(k)
     if hpd == 1:
         reduce.xy(0)
         reduce.xy(1)
         reduce.start_x(2)
         reduce.after_y(0)
 
-    for k, (unit, _) in enumerate(steps):
-        if unit == hpd - 1:
-            weights_of_head(k)
+    for k in range(len(steps)):
+        weights_of_head(k)
     for source in range(nf):
         dwsend[source] = dw[:, source * rows : (source + 1) * rows].astype(BF16)
 
@@ -1139,9 +1167,9 @@
     pieces = fw_out.shape[1]
     result = reduce_scratch[0]
     cut = height // zlen // pieces
-    spread = Spread(p, dw_out, ag_send, ag_recv, 3, lambda i: dwown.at[i], own_sem.at[0])
+    spread = Spread(p, dw_out, ag_send, ag_recv, 3, (), lambda i: dwown.at[i], own_sem.at[0])
     spread2 = Spread(
-        p, fw_out, fg_send, fg_recv, pieces, lambda i: result.at[pl.ds(i * cut, cut)], own_sem.at[1])
+        p, fw_out, fg_send, fg_recv, pieces, (0, 2), lambda i: result.at[pl.ds(i * cut, cut)], own_sem.at[1])
 
     def start_spread():
         total = dwsend[f].astype(F32)
@@ -1390,7 +1418,7 @@
                 for k in range(out.shape[0]):
                     at = source * rows + k * BLK
                     out[k : k + 1, :] = tail[r : r + 1, at : at + BLK]
-            sc_out[...] = tail[4:5, source * share : source * share + BLK]
+            sc_out[...] = tail[4:5, source * share : (source + 1) * share].reshape(share)
     stores.wait()
 
 
@@ -1403,7 +1431,7 @@
     mat, row = jax.ShapeDtypeStruct((rows, D), F32), jax.ShapeDtypeStruct((-(-rows // BLK), BLK), F32)
     return pl.pallas_call(
         functools.partial(results_kernel, n, nf, hpd),
-        out_shape=(mat,) * 6 + (row,) * 4 + (jax.ShapeDtypeStruct((1, BLK), F32),),
+        out_shape=(mat,) * 6 + (row,) * 4 + (jax.ShapeDtypeStruct((HD // nf,), F32),),
         in_specs=[in_any(), in_any(), in_vmem(), in_vmem()],
         out_specs=(in_any(),) * 6 + (in_vmem(),) * 5,
         scratch_shapes=[
@@ -1427,7 +1455,7 @@
     def in_rows(v):
         return jnp.pad(v, (0, -v.shape[0] % BLK)).reshape(-1, BLK)
 
-    vectors = tuple(in_rows(v) for v in (gain_attn, query_bias, value_bias, gain_ffn, query_scale))
+    vectors = tuple(in_rows(v) for v in (gain_attn, query_bias, value_bias, gain_ffn)) + (query_scale,)
     blocks = jnp.arange(deal.shape[0], dtype=jnp.int32)
     inverse = jnp.sum(jnp.where(deal[None, :] == blocks[:, None], blocks[None, :] // 2, 0), axis=1, dtype=jnp.int32)
 
@@ -1443,7 +1471,6 @@
     dwq, dwk, dwv, dwo, dw1, dw2, ga, bq, bv, gf, scale = results(
         n, nf, lay.hpd, dw, pieces, sums, whole)
     ga, bq, bv, gf = (v.reshape(-1)[:rows] for v in (ga, bq, bv, gf))
-    scale = scale.reshape(-1)[: query_scale.shape[0]]
     return layer_out[None], grad_x[None], ga, dwq, bq, dwk, dwv, bv, scale, dwo, gf, dw1, dw2
 
 

time: 292 us -> 285 us (0.976)
  no operation moved by 1% of the time
where the time goes in v6:
time: 285 us
  Pallas kernels  281 us (99%)
    pallas_call x1, Pallas kernels, backward(): pl.pallas_call(functools.partial(backward_kernel, lay, n, nf), out_shape=...  155 us
    pallas_call x1, Pallas kernels, forward(): pl.pallas_call(functools.partial(forward_kernel, lay, n, nf), out_shape=t...  115 us
    pallas_call x1, Pallas kernels, results(): pl.pallas_call(functools.partial(results_kernel, n, nf, hpd), out_shape=(...  11.2 us

profile of v6, /device:TPU:0, one launch (start us, length us, event | category | flops | bytes accessed | tf_op | source)
XLA Modules:
  0.0 284.8 jit_solution(6010611476987051337)
XLA Ops:
  0.7 1.3 select_reduce_fusion.inv_ref
  1.9 115.0 %forward.1 = (bf16[16,2,128,1280]{3,2,1,0:T(8,128)(2,1)}, bf16[5,1280,1280]{2,1,0:T(8,128)(2,1)}, bf16[320,1280]{1,0:T(8,128)(2,1)}, bf16[320,1280]{1,0:T(8,128)...) custom-call(s32[32]{0:T(128)} %deal_ref.3, ...), custom_call_target="tpu_custom_call" | custom-call | bytes 300000000 | tf_op jit(solution)/shard_map/forward/pallas_call | solution.py:883
  116.9 154.8 %backward.1 = (f32[256,1280]{1,0:T(8,128)}, bf16[16,3,80,640]{3,2,1,0:T(8,128)(2,1)}, bf16[16,3,80,640]{3,2,1,0:T(8,128)(2,1)}, f32[16,24,128]{2,1,0:T(8,128)}, ...) custom-call(s32[32]{0:T(128)} %deal_ref.3, s32[32]{0:T(128)} %select_reduce_fusion.inv_ref, s32[1,8]{1,0:T(1,128)} %len_ref.3, ...), custom_call_target="tpu_custom_call" | custom-call | bytes 390000000 | tf_op jit(solution)/shard_map/backward/pallas_call | solution.py:1322
  271.7 0.0 copy-start.1
  271.7 0.0 copy-start
  271.8 11.2 %results.1 = (f32[640,1280]{1,0:T(8,128)}, f32[640,1280]{1,0:T(8,128)}, f32[640,1280]{1,0:T(8,128)}, f32[640,1280]{1,0:T(8,128)}, f32[640,1280]{1,0:T(8,128)}, /...) custom-call(bf16[16,3,80,640]{3,2,1,0:T(8,128)(2,1)} %get-tuple-elem, ...), custom_call_target="tpu_custom_call" | custom-call | bytes 33000000 | tf_op jit(solution)/shard_map/results/pallas_call | solution.py:1432
  282.9 0.0 copy-done.1
  282.9 0.8 copy.30
  283.8 0.0 copy-done
  283.8 1.1 copy.31
  (1 shorter events, 0.0 us)
Async XLA Ops:
  271.7 11.2 %copy-start.1 = (bf16[256,1280]{1,0:T(8,128)(2,1)S(1)}, bf16[256,1280]{1,0:T(8,128)(2,1)}, u32[]{:S(2)}) copy-start(bf16[256,1280]{1,0:T(8,128)(2,1)} %get-tuple-element.49) | copy-start | bytes 1966084
  271.7 12.0 %copy-start = (f32[256,1280]{1,0:T(8,128)S(1)}, f32[256,1280]{1,0:T(8,128)}, u32[]{:S(2)}) copy-start(f32[256,1280]{1,0:T(8,128)} %get-tuple-element.70) | copy-start | bytes 3932164

commit v7 on v6

--- a/solution.py
+++ b/solution.py
@@ -1169,7 +1169,7 @@
     cut = height // zlen // pieces
     spread = Spread(p, dw_out, ag_send, ag_recv, 3, (), lambda i: dwown.at[i], own_sem.at[0])
     spread2 = Spread(
-        p, fw_out, fg_send, fg_recv, pieces, (0, 2), lambda i: result.at[pl.ds(i * cut, cut)], own_sem.at[1])
+        p, fw_out, fg_send, fg_recv, pieces, (0, 2, 4), lambda i: result.at[pl.ds(i * cut, cut)], own_sem.at[1])
 
     def start_spread():
         total = dwsend[f].astype(F32)
@@ -1316,7 +1316,7 @@
     zlen = n // 4
     height = -(-3 * part // (16 * zlen)) * 16 * zlen
     piece = height // zlen
-    pieces = 3 if piece % 48 == 0 else 1
+    pieces = 5 if piece % 80 == 0 else 1
     peers = max(nf - 1, 1)
     tok = x.shape[0]
     return pl.pallas_call(
@@ -1345,7 +1345,7 @@
             VMEM((nf, VEC_ROWS, BLK), F32), VMEM((VEC_ROWS, BLK), F32), VMEM((n, VEC_ROWS, BLK), F32),
             dma((25 + 2 * nf,)), dma((hpd, n)), dma((hpd, n)), dma((hpd,)), dma((hpd, n)), dma((hpd, n)), dma((hpd,)),
             dma((peers,)), dma((peers,)), dma((peers,)), dma((peers,)), dma((2,)),
-            dma((peers,)), dma((peers,)), dma((2, 3)), dma((4, n, 3)), dma((n, 3)), dma((4, n, pieces)), dma((n, pieces)),
+            dma((peers,)), dma((peers,)), dma((2, 5)), dma((4, n, 3)), dma((n, 3)), dma((4, n, pieces)), dma((n, pieces)),
             dma((peers,)), dma((peers,)), dma((n,)), dma((n,)),
         ] + [VMEM((n, HD, BLK), BF16)] * hpd + Reduce.scratch(nf, zlen, height),
         compiler_params=pltpu.CompilerParams(

time: 285 us -> 286 us (level)
  no operation moved by 1% of the time
where the time goes in v7:
time: 286 us; the launch traced here: 285 us
  Pallas kernels  282 us (99%)
    pallas_call x1, Pallas kernels, backward(): pl.pallas_call(functools.partial(backward_kernel, lay, n, nf), out_shape=...  155 us
    pallas_call x1, Pallas kernels, forward(): pl.pallas_call(functools.partial(forward_kernel, lay, n, nf), out_shape=t...  115 us
    pallas_call x1, Pallas kernels, results(): pl.pallas_call(functools.partial(results_kernel, n, nf, hpd), out_shape=(...  11.2 us

profile of v7, /device:TPU:0, one launch (start us, length us, event | category | flops | bytes accessed | tf_op | source)
XLA Modules:
  0.0 285.4 jit_solution(1157080597967796230)
XLA Ops:
  0.7 1.3 select_reduce_fusion.inv_ref
  1.9 115.0 %forward.1 = (bf16[16,2,128,1280]{3,2,1,0:T(8,128)(2,1)}, bf16[5,1280,1280]{2,1,0:T(8,128)(2,1)}, bf16[320,1280]{1,0:T(8,128)(2,1)}, bf16[320,1280]{1,0:T(8,128)...) custom-call(s32[32]{0:T(128)} %deal_ref.3, ...), custom_call_target="tpu_custom_call" | custom-call | bytes 300000000 | tf_op jit(solution)/shard_map/forward/pallas_call | solution.py:883
  116.9 155.4 %backward.1 = (f32[256,1280]{1,0:T(8,128)}, bf16[16,3,80,640]{3,2,1,0:T(8,128)(2,1)}, bf16[16,5,48,640]{3,2,1,0:T(8,128)(2,1)}, f32[16,24,128]{2,1,0:T(8,128)}, ...) custom-call(s32[32]{0:T(128)} %deal_ref.3, s32[32]{0:T(128)} %select_reduce_fusion.inv_ref, s32[1,8]{1,0:T(1,128)} %len_ref.3, ...), custom_call_target="tpu_custom_call" | custom-call | bytes 390000000 | tf_op jit(solution)/shard_map/backward/pallas_call | solution.py:1322
  272.3 0.0 copy-start.1
  272.3 0.0 copy-start
  272.3 11.2 %results.1 = (f32[640,1280]{1,0:T(8,128)}, f32[640,1280]{1,0:T(8,128)}, f32[640,1280]{1,0:T(8,128)}, f32[640,1280]{1,0:T(8,128)}, f32[640,1280]{1,0:T(8,128)}, /...) custom-call(bf16[16,3,80,640]{3,2,1,0:T(8,128)(2,1)} %get-tuple-elem, ...), custom_call_target="tpu_custom_call" | custom-call | bytes 33000000 | tf_op jit(solution)/shard_map/results/pallas_call | solution.py:1432
  283.5 0.0 copy-done.1
  283.5 0.8 copy.30
  284.4 0.0 copy-done
  284.4 1.1 copy.31
  (1 shorter events, 0.0 us)
Async XLA Ops:
  272.3 11.2 %copy-start.1 = (bf16[256,1280]{1,0:T(8,128)(2,1)S(1)}, bf16[256,1280]{1,0:T(8,128)(2,1)}, u32[]{:S(2)}) copy-start(bf16[256,1280]{1,0:T(8,128)(2,1)} %get-tuple-element.49) | copy-start | bytes 1966084
  272.3 12.0 %copy-start = (f32[256,1280]{1,0:T(8,128)S(1)}, f32[256,1280]{1,0:T(8,128)}, u32[]{:S(2)}) copy-start(f32[256,1280]{1,0:T(8,128)} %get-tuple-element.70) | copy-start | bytes 3932164
